TPU v7x, 256 devices: a whole 4x4x8 slice. The times are simulated.
256 devices in a mesh: leaf: 64 (over y, z, core), col: 4 (over x).
Axes of the slice: x: 4, y: 4, z: 8, core: 2. Of those that a mesh axis runs over, the one named last changes fastest.
Arguments:
- ratings: float32 [65536, 2048], P('leaf', 'col'), may hold values from -6 to 6
- dense_blocks: float32 [64, 1024, 1024], P('leaf'), may hold values from -0.1875 to 0.1875
- row_basis: float32 [64, 1024, 256], P('leaf'), may hold values from -0.375 to 0.375
- col_basis: float32 [64, 1024, 256], P('leaf'), may hold values from -0.1875 to 0.1875
- transfers: float32 [2, 4, 256, 256], replicated, may hold values from -0.1875 to 0.1875
- couplings: float32 [3, 3, 256, 256], replicated, may hold values from -0.21875 to 0.21875
Outputs:
- predicted: float32 [65536, 2048], P('leaf', 'col')
All inputs are finite; a program needn't handle non-finite values.
Results may differ from a plain program's by a relative error of at most 0.0001.
Values sent between devices are 32-bit elements; how exact they have to be, the bound alone decides.
No kernel may reach another device: no remote copies, remote signals or barrier semaphores. Data moves between devices by JAX's collectives and lax.ppermute only.
A program may use at most 128 MiB of HBM per device.

v0:
```python
import jax
import jax.numpy as jnp
from jax import lax
from jax.sharding import PartitionSpec as P


def from_partner(block, axis, bit):
    count = lax.axis_size(axis)
    route = []
    for low in range(count):
        high = low | 1 << bit
        if high != low and high < count:
            route += [(low, high), (high, low)]
    return lax.ppermute(block, axis, route)


def tree_depth(leaves):
    return 1 + min(1, leaves // 8) + min(1, leaves // 32) + min(1, leaves // 128)


def collect(current, low_bit, fanout, leaf_id):
    siblings = current[None]
    for rounds in range(fanout.bit_length() - 1):
        bit_pos = low_bit + rounds
        partner = from_partner(siblings, "leaf", bit_pos)
        is_lower = leaf_id >> bit_pos & 1 == 0
        siblings = jnp.where(
            is_lower,
            jnp.concatenate([siblings, partner], 0),
            jnp.concatenate([partner, siblings], 0),
        )
    return siblings


def couple(siblings, position, height, fanout, coupling_all):
    highest = lax.Precision.HIGHEST
    field = jnp.zeros(siblings.shape[1:], jnp.float32)
    for offset in range(1, fanout):
        chosen = lax.dynamic_index_in_dim(siblings, (position + offset) % fanout, 0, keepdims=False)
        field = field + jnp.dot(
            coupling_all[height, offset - 1],
            chosen,
            precision=highest,
            preferred_element_type=jnp.float32,
        )
    return field


def assemble(pieces, leaves, rank, columns):
    quarter_cols = pieces.shape[2]
    return (
        pieces.reshape(leaves // 4, 4, rank, quarter_cols)
        .transpose(0, 2, 1, 3)
        .reshape(leaves // 4, rank, columns)
    )


def local(ratings, dense_blocks, row_basis, col_basis, transfers, couplings):
    highest = lax.Precision.HIGHEST
    leaves = lax.axis_size("leaf")
    depth = tree_depth(leaves)
    tops = leaves // 4 ** (depth - 1)
    leaf_id = lax.axis_index("leaf")
    near_part = jnp.dot(
        dense_blocks[0], ratings, precision=highest, preferred_element_type=jnp.float32
    )
    coef = jnp.einsum("ia,ic->ac", col_basis[0], ratings, precision=highest)
    rank = coef.shape[0]
    columns = coef.shape[1]
    siblings = collect(coef, 0, 4, leaf_id)
    leaf_pos = leaf_id % 4
    leaf_field = couple(siblings, leaf_pos, 0, 4, couplings)
    current = jnp.einsum("kab,kac->bc", transfers[0], siblings, precision=highest)
    upper_fields = []
    upper_places = []
    quarter_cols = columns // 4
    part_id = leaf_id % 4
    portion = lax.dynamic_slice_in_dim(current, part_id * quarter_cols, quarter_cols, 1)
    own_pos = (leaf_id >> 2) % 4
    own_transfer = lax.dynamic_index_in_dim(transfers[1], own_pos, 0, keepdims=False)
    lifted = jnp.dot(own_transfer.T, portion, precision=highest, preferred_element_type=jnp.float32)
    outgoing = jnp.stack([portion, lifted], 0)
    received = lax.all_gather(outgoing[:, None], "leaf", axis=1, tiled=True)
    level_coef = assemble(received[0], leaves, rank, columns)
    for height in range(1, depth):
        fanout = 4 if height < depth - 1 else tops
        node_id = leaf_id >> 2 * height
        start = node_id // fanout * fanout
        siblings = lax.dynamic_slice_in_dim(level_coef, start, fanout, 0)
        position = node_id % fanout
        upper_fields.append(couple(siblings, position, height, fanout, couplings))
        upper_places.append(position)
        if height < depth - 1:
            level_coef = (
                assemble(received[1], leaves, rank, columns).reshape(-1, 4, rank, columns).sum(1)
            )
    downward = upper_fields[-1]
    height = 1
    lifted_op = lax.dynamic_index_in_dim(
        transfers[height], upper_places[height - 1], 0, keepdims=False
    )
    downward = upper_fields[height - 1] + jnp.dot(
        lifted_op, downward, precision=highest, preferred_element_type=jnp.float32
    )
    lowest = lax.dynamic_index_in_dim(transfers[0], leaf_pos, 0, keepdims=False)
    downward = leaf_field + jnp.dot(
        lowest, downward, precision=highest, preferred_element_type=jnp.float32
    )
    far_part = jnp.dot(
        row_basis[0], downward, precision=highest, preferred_element_type=jnp.float32
    )
    return near_part + far_part


def solution(mesh):
    placed = (
        P("leaf", "col"),
        P("leaf", None, None),
        P("leaf", None, None),
        P("leaf", None, None),
        P(),
        P(),
    )
    return jax.shard_map(
        local, mesh=mesh, in_specs=placed, out_specs=P("leaf", "col"), check_vma=False
    )
```

profile of v0, /device:TPU:1, one launch (start us, length us, event | category | flops | bytes accessed | tf_op | source)
XLA Modules:
  0.0 242.3 jit_solution(1094805285573532567)
XLA Ops:
  6.5 1.6 copy-done
  8.1 3.2 %convolution_bitcast_fusion.1 = f32[1,256,512]{2,1,0:T(8,128)S(1)} fusion(f32[1024,512]{1,0:T(8,128)S(1)} %copy-done, f32[1,1024,256]{2,1,0:T(8,128)} %param.9), kind=kOutput, calls=%fused_computation.5 | convolution fusion | flops 1610612736 | bytes 3670016 | tf_op jit(solution)/shard_map/ia,ic->ac/dot_general | solution.py:67
  11.3 3.3 %collective-permute-start = (f32[1,256,512]{2,1,0:T(8,128)S(1)}, f32[1,256,512]{2,1,0:T(8,128)}, u32[]{:S(2)}, u32[]{:S(2)}) collective-permute-start(f32[1,256,512]{2,1,0:T(8,128)S(1)} %convolution_bitcast_fusion.1), channel_id=1, source_target_pairs={{0,4},{4,0},{8,12},{12,8},{16,20},{20,16},{24,28},{28,24},{32,36},... | collective-permute-start | bytes 1572872 | tf_op jit(solution)/shard_map/ppermute | solution.py:14
  14.6 1.7 collective-permute-done
  16.3 1.7 maximum_select_fusion.1
  18.0 0.3 collective-permute-start.1
  18.4 2.7 %fusion.69 = (f32[1,4,256,256]{3,2,1,0:T(8,128)}, f32[1,4,256,256]{3,2,1,0:T(8,128)S(1)}) fusion(f32[2,4,256,256]{3,2,1,0:T(8,128)} %param.10), kind=kLoop, calls=%fused_computation.84 | loop fusion | bytes 4194304 | tf_op jit(solution)/shard_map/slice | solution.py:105
  21.1 21.7 %collective-permute-done.1 = f32[2,256,512]{2,1,0:T(8,128)} collective-permute-done((f32[2,256,512]{2,1,0:T(8,128)S(1)}, f32[2,256,512]{2,1,0:T(8,128)}, u32[]{:S(2)}, u32[]{:S(2)}) %collective-permute-start.1) | collective-permute-done | bytes 1048608 | tf_op jit(solution)/shard_map/ppermute | solution.py:14
  42.8 1.9 maximum_select_fusion
  44.7 3.4 %convolution_bitcast_fusion = f32[512,256]{1,0:T(8,128)S(1)} fusion(f32[4,256,512]{2,1,0:T(8,128)S(1)} %maximum_select_fusion, f32[2,4,256,256]{3,2,1,0:T(8,128)S(1)} %copy-done.5), kind=kOutput, calls=%fused_computation.4 | convolution fusion | flops 1610612736 | bytes 3670016 | tf_op jit(solution)/shard_map/kab,kac->bc/dot_general | solution.py:73
  48.2 0.3 convolution_bitcast_fusion.2
  48.5 0.7 pad_maximum_fusion
  49.5 9.7 %fusion = f32[1024,512]{1,0:T(8,128)} fusion(f32[1024,512]{1,0:T(8,128)S(1)} %copy-done, f32[1,1024,1024]{2,1,0:T(8,128)} %param.7), kind=kOutput, calls=%fused_computation | convolution fusion | flops 6442450944 | bytes 8388608 | tf_op jit(solution)/shard_map/dot_general | solution.py:64
  59.2 2.0 fusion.18
  61.2 2.0 fusion.16
  63.2 2.0 fusion.4
  65.2 93.5 %all-gather.3.cloned.1.call-done = f32[2,16384,128]{1,2,0:T(8,128)} async-done(((f32[2,256,128]{1,2,0:T(8,128)}), f32[2,16384,128]{1,2,0:T(8,128)}) %all-gather.3.cloned.1.call-update) | async-done | bytes 16777232 | tf_op jit(solution)/shard_map/all_gather | solution.py:83
  158.7 11.3 %fusion.68 = (f32[1,16384,128]{1,2,0:T(8,128)}, f32[1,16384,128]{1,2,0:T(8,128)}) fusion(f32[2,16384,128]{1,2,0:T(8,128)} %all-gather.3.cloned.1.call-done), kind=kLoop, calls=%fused_computation.83 | loop fusion | bytes 33554432 | tf_op jit(solution)/shard_map/slice | solution.py:95
  170.0 10.8 %reshape_squeeze.7 = f32[16,4,256,128]{2,1,0,3:T(4,128)} reshape(f32[1,16384,128]{1,2,0:T(8,128)} %get-tuple-element.5) | data formatting | bytes 16777216 | tf_op jit(solution)/shard_map/reshape;squeeze | solution.py:52
  180.8 11.5 %copy.18 = f32[16,4,256,128]{2,3,1,0:T(8,128)} copy(f32[16,4,256,128]{2,1,0,3:T(4,128)} %reshape_squeeze.7) | data formatting | bytes 16777216 | tf_op jit(solution)/shard_map/reshape;squeeze | solution.py:52
  192.2 10.8 %reshape_squeeze.6 = f32[16,4,256,128]{2,1,0,3:T(4,128)} reshape(f32[1,16384,128]{1,2,0:T(8,128)} %get-tuple-element.6) | data formatting | bytes 16777216 | tf_op jit(solution)/shard_map/reshape;squeeze | solution.py:52
  203.0 11.5 %copy.17 = f32[16,4,256,128]{2,3,1,0:T(8,128)} copy(f32[16,4,256,128]{2,1,0,3:T(4,128)} %reshape_squeeze.6) | data formatting | bytes 16777216 | tf_op jit(solution)/shard_map/reshape;squeeze | solution.py:52
  214.5 4.2 %reduce_sum.9 = f32[4,256,512]{1,2,0:T(8,128)S(1)} reduce(f32[4,4,256,512]{2,3,1,0:T(8,128)} %bitcast.106, f32[]{:T(128)} %constant.167.clone.1), dimensions={1}, to_apply=%region_0.1 | reduce | flops 1572864 | bytes 10485764 | tf_op jit(solution)/shard_map/reduce_sum | solution.py:95
  218.7 1.6 fusion.10
  220.3 1.6 convolution_add_fusion.3
  221.8 1.6 convolution_add_fusion.2
  223.4 1.7 fusion.14
  225.2 1.7 convolution_add_fusion.5
  226.9 1.7 fusion.2
  228.7 1.8 convolution_add_fusion.1
  230.4 1.7 convolution_add_fusion
  232.2 3.3 %bitcast_add_fusion = f32[1024,512]{1,0:T(8,128)} fusion(f32[1024,512]{1,0:T(8,128)S(1)} %copy-done.4, f32[256,512]{0,1:T(8,128)S(1)} %convolution_add_fusion, f32[1,1024,256]{2,1,0:T(8,128)S(1)} %copy-done.8), kind=kOutput, calls=%fused_computation.3 | convolution fusion | flops 1611137024 | bytes 5767168 | tf_op jit(solution)/shard_map/dot_general | solution.py:109
  (20 shorter events, 0.1 us)
Async XLA Ops:
  6.5 1.6 copy-start
  6.5 152.2 %all-gather.3.cloned.1.call-start = ((), (), s32[]{:S(2)}) async-start(), calls=%async_computation | async-start | bytes 17039360 | tf_op jit(solution)/shard_map/all_gather | solution.py:83
  11.3 3.3 %copy-start.7 = (f32[1,256,512]{2,1,0:T(8,128)}, f32[1,256,512]{2,1,0:T(8,128)S(1)}, u32[]{:S(2)}) copy-start(f32[1,256,512]{2,1,0:T(8,128)S(1)} %convolution_bitcast_fusion.1) | copy-start | bytes 1572868
  11.3 5.0 %collective-permute-start = (f32[1,256,512]{2,1,0:T(8,128)S(1)}, f32[1,256,512]{2,1,0:T(8,128)}, u32[]{:S(2)}, u32[]{:S(2)}) collective-permute-start(f32[1,256,512]{2,1,0:T(8,128)S(1)} %convolution_bitcast_fusion.1), channel_id=1, source_target_pairs={{0,4},{4,0},{8,12},{12,8},{16,20},{20,16},{24,28},{28,24},{32,36},... | collective-permute-start | bytes 1572872 | tf_op jit(solution)/shard_map/ppermute | solution.py:14
  18.0 24.7 %collective-permute-start.1 = (f32[2,256,512]{2,1,0:T(8,128)S(1)}, f32[2,256,512]{2,1,0:T(8,128)}, u32[]{:S(2)}, u32[]{:S(2)}) collective-permute-start(f32[2,256,512]{2,1,0:T(8,128)S(1)} %maximum_select_fusion.1), channel_id=1, source_target_pairs={{0,8},{8,0},{4,12},{12,4},{16,24},{24,16},{20,28},{28,20},{32,40},... | collective-permute-start | bytes 3145736 | tf_op jit(solution)/shard_map/ppermute | solution.py:14
  21.1 27.1 %copy-start.6 = (f32[1,4,256,256]{3,2,1,0:T(8,128)}, f32[1,4,256,256]{3,2,1,0:T(8,128)S(1)}, u32[]{:S(2)}) copy-start(f32[1,4,256,256]{3,2,1,0:T(8,128)S(1)} %get-tuple-element.8) | copy-start | bytes 3145732
  21.1 23.6 %copy-start.5 = (f32[2,4,256,256]{3,2,1,0:T(8,128)S(1)}, f32[2,4,256,256]{3,2,1,0:T(8,128)}, u32[]{:S(2)}) copy-start(f32[2,4,256,256]{3,2,1,0:T(8,128)} %param.10) | copy-start | bytes 6291460
  44.7 3.8 %copy-start.2 = (f32[4,256,512]{2,1,0:T(8,128)}, f32[4,256,512]{2,1,0:T(8,128)S(1)}, u32[]{:S(2)}) copy-start(f32[4,256,512]{2,1,0:T(8,128)S(1)} %maximum_select_fusion) | copy-start | bytes 6291460
  49.5 9.7 %copy-start.3 = (f32[4,256,512]{2,1,0:T(8,128)S(1)}, f32[4,256,512]{2,1,0:T(8,128)}, u32[]{:S(2)}) copy-start(f32[4,256,512]{2,1,0:T(8,128)} %copy-done.2) | copy-start | bytes 6291460
  228.7 3.5 %copy-start.4 = (f32[1024,512]{1,0:T(8,128)S(1)}, f32[1024,512]{1,0:T(8,128)}, u32[]{:S(2)}) copy-start(f32[1024,512]{1,0:T(8,128)} %fusion) | copy-start | bytes 6291460
  228.7 3.5 %copy-start.8 = (f32[1,1024,256]{2,1,0:T(8,128)S(1)}, f32[1,1024,256]{2,1,0:T(8,128)}, u32[]{:S(2)}) copy-start(f32[1,1024,256]{2,1,0:T(8,128)} %param.8) | copy-start | bytes 3145732
  230.4 5.0 %copy-start.1 = (f32[1024,512]{1,0:T(8,128)S(1)}, f32[1024,512]{1,0:T(8,128)}, u32[]{:S(2)}) copy-start(f32[1024,512]{1,0:T(8,128)} %param.6) | copy-start | bytes 6291460
Sparse Core Ops, SparseCore 0:
  49.4 109.2 all-gather.2
where the time goes:
time: 243 us; the launch traced here: 242 us
  waiting for transfers between devices  117 us (48%)
  local copies, waits for them, and re-layouts  60.1 us (25%)
  matrix products  39.2 us (16%)
  between operations  13.9 us (6%)
  other arithmetic  8.57 us (4%)
  starting transfers between devices  3.61 us (1%)
    all_gather x1, waiting for transfers between devices, local(): received = lax.all_gather(outgoing[:, None], 'leaf', axis=1, tiled=True)  93.5 us
    another operation x4, local copies, waits for them, and re-layouts, assemble(): pieces.reshape(leaves // 4, 4, rank, quarter_cols).transpose(0, 2, 1, 3)  44.5 us
    ppermute x2, waiting for transfers between devices, from_partner(): return lax.ppermute(block, axis, route)  23.3 us
    dot_general x9, matrix products, couple(): jnp.dot(coupling_all[height, offset - 1], chosen, precision=highest, pref...  15.9 us
    slice x1, local copies, waits for them, and re-layouts, local(): received[1]  11.3 us
    dot_general x1, matrix products, local(): jnp.dot(dense_blocks[0], ratings, precision=highest, preferred_element_ty...  9.73 us
  transfers between devices with their start and end apart: 3, of which 3 were waited for; matrix products, arithmetic and copies ran while one was open for 8% of the time, Pallas kernels for 0%

commit v1 on v0

v1 whole, which is shorter than its diff:
```python
import functools

import jax
import jax.numpy as jnp
from jax import lax
from jax.experimental import pallas as pl
from jax.experimental.pallas import tpu as pltpu
from jax.sharding import PartitionSpec as P

F32 = jnp.float32
HIGH = lax.Precision.HIGH
MIB = 1 << 20


def dot(a, b, ca, cb):
    return lax.dot_general(
        a, b, (((ca,), (cb,)), ((), ())), precision=HIGH, preferred_element_type=F32
    )


def run(body, ins, outs, name, flops, scratch=(), vmem=24):
    ins = [pltpu.with_memory_space_constraint(x, pltpu.VMEM) for x in ins]
    whole = pl.BlockSpec(memory_space=pltpu.VMEM)
    return pl.pallas_call(
        body,
        out_shape=[pltpu.VMEM(shape, F32) for shape in outs],
        in_specs=[whole] * len(ins),
        out_specs=[whole] * len(outs),
        scratch_shapes=list(scratch),
        compiler_params=pltpu.CompilerParams(vmem_limit_bytes=vmem * MIB),
        cost_estimate=pl.CostEstimate(
            flops=flops,
            bytes_accessed=4 * sum(x.size for x in ins),
            transcendentals=0,
        ),
        name=name,
    )(*ins)


def place():
    leaf = lax.axis_index("leaf")
    return leaf % 4, (leaf // 4) % 4, leaf // 16


def other(index, j):
    low, high = index % 2, index // 2
    low = 1 - low if j & 1 else low
    high = 1 - high if j & 2 else high
    return 2 * high + low


def rows(index, count):
    return pl.ds(pl.multiple_of(index * count, count), count)


def leaf_coefficients(x, basis, o0, o1, o2, o3, whole):
    p, _, _ = place()
    whole[...] = dot(x[...], basis[...], 0, 0)
    step = o0.shape[0]
    for j, out in enumerate((o0, o1, o2, o3)):
        out[...] = whole[rows(other(p, j), step), :]


def near_field(dense, x, out):
    @pl.loop(0, 4)
    def _(i):
        at = rows(i, 256)
        out[at, :] = dot(dense[at, :], x[...], 1, 0)


def up(digit, level, c0, c1, c2, c3, transfers, o0, o1, o2, o3, whole):
    own = place()[digit]
    total = None
    for j, c in enumerate((c0, c1, c2, c3)):
        term = dot(c[...], transfers[level, other(own, j)], 1, 0)
        total = term if total is None else total + term
    if o1 is None:
        o0[...] = total
        return
    whole[...] = total
    step = o0.shape[0]
    for j, out in enumerate((o0, o1, o2, o3)):
        out[...] = whole[rows(other(place()[digit + 1], j), step), :]


def up_split(digit, level, c0, c1, c2, c3, transfers, o0, o1, o2, o3, whole):
    up(digit, level, c0, c1, c2, c3, transfers, o0, o1, o2, o3, whole)


def up_last(digit, level, c0, c1, c2, c3, transfers, o0):
    up(digit, level, c0, c1, c2, c3, transfers, o0, None, None, None, None)


def field_of(target, own, parts, level, couplings):
    at = other(own, target)
    total = None
    for j, c in enumerate(parts):
        if j == target:
            continue
        offset = (other(own, j) - at + 4) % 4
        term = dot(c[...], couplings[level, offset - 1], 1, 1)
        total = term if total is None else total + term
    return total


def couple_all(digit, level, c0, c1, c2, c3, couplings, f0, f1, f2, f3):
    own = place()[digit]
    for target, out in enumerate((f0, f1, f2, f3)):
        out[...] = field_of(target, own, (c0, c1, c2, c3), level, couplings)


def top(c0, c1, c2, c3, couplings, transfers, f0, f1, f2, f3, o0, o1, o2, o3):
    _, q, r = place()
    g = field_of(0, r, (c0, c1, c2, c3), 2, couplings)
    for j, (field, out) in enumerate(zip((f0, f1, f2, f3), (o0, o1, o2, o3))):
        out[...] = field[...] + dot(g, transfers[1, other(q, j)], 1, 1)


def down(g0, g1, g2, g3, transfers, f0, f1, f2, f3, o0, o1, o2, o3, whole):
    p, q, _ = place()
    step = g0.shape[0]
    for j, g in enumerate((g0, g1, g2, g3)):
        whole[rows(other(q, j), step), :] = g[...]
    g = whole[...]
    for j, (field, out) in enumerate(zip((f0, f1, f2, f3), (o0, o1, o2, o3))):
        out[...] = field[...] + dot(g, transfers[0, other(p, j)], 1, 1)


def finish(near, row_basis, g0, g1, g2, g3, out, whole):
    @pl.when(pl.program_id(0) == 0)
    def _():
        p, _, _ = place()
        step = g0.shape[0]
        for j, g in enumerate((g0, g1, g2, g3)):
            whole[rows(other(p, j), step), :] = g[...]

    at = rows(pl.program_id(0), out.shape[0])
    out[...] = near[at, :] + dot(row_basis[at, :], whole[...], 1, 1)


def swap(block, bits):
    count = lax.axis_size("leaf")
    return lax.ppermute(block, "leaf", [(i, i ^ bits) for i in range(count)])


def exchange(blocks, digit):
    got = {j: swap(blocks[j], j << 2 * digit) for j in (2, 3, 1)}
    return [blocks[0]] + [got[j] for j in (1, 2, 3)]


def local(ratings, dense_blocks, row_basis, col_basis, transfers, couplings):
    users, columns = ratings.shape
    rank = col_basis.shape[2]
    quarter, slim = columns // 4, columns // 16
    unit = 2 * 3 * rank * rank
    dense, rbasis, cbasis = dense_blocks[0], row_basis[0], col_basis[0]

    coef = run(
        leaf_coefficients,
        [ratings, cbasis],
        [(quarter, rank)] * 4,
        "leaf_coefficients",
        6 * users * columns * rank,
        [pltpu.VMEM((columns, rank), F32)],
    )
    coef = exchange(coef, 0)
    (near,) = run(
        near_field, [dense, ratings], [(users, columns)], "near_field", 6 * users * users * columns
    )
    lifted = run(
        functools.partial(up_split, 0, 0),
        [*coef, transfers],
        [(slim, rank)] * 4,
        "lift_leaves",
        unit * columns,
        [pltpu.VMEM((quarter, rank), F32)],
    )
    lifted = exchange(lifted, 1)
    leaf_fields = run(
        functools.partial(couple_all, 0, 0),
        [*coef, couplings],
        [(quarter, rank)] * 4,
        "couple_leaves",
        unit * 3 * columns,
    )
    (crown,) = run(
        functools.partial(up_last, 1, 1),
        [*lifted, transfers],
        [(slim, rank)],
        "lift_nodes",
        unit * quarter,
    )
    crown = exchange([crown] * 4, 2)
    node_fields = run(
        functools.partial(couple_all, 1, 1),
        [*lifted, couplings],
        [(slim, rank)] * 4,
        "couple_nodes",
        unit * 3 * quarter,
    )
    node_g = run(
        top,
        [*crown, couplings, transfers, *node_fields],
        [(slim, rank)] * 4,
        "top",
        unit * 7 * slim,
    )
    node_g = exchange(node_g, 1)
    leaf_g = run(
        down,
        [*node_g, transfers, *leaf_fields],
        [(quarter, rank)] * 4,
        "down",
        unit * columns,
        [pltpu.VMEM((quarter, rank), F32)],
    )
    leaf_g = exchange(leaf_g, 0)
    ins = [
        pltpu.with_memory_space_constraint(x, pltpu.VMEM) for x in (near, rbasis, *leaf_g)
    ]
    steps = 4
    return pl.pallas_call(
        finish,
        out_shape=jax.ShapeDtypeStruct((users, columns), F32),
        grid=(steps,),
        in_specs=[pl.BlockSpec(memory_space=pltpu.VMEM)] * 6,
        out_specs=pl.BlockSpec((users // steps, columns), lambda i: (i, 0)),
        scratch_shapes=[pltpu.VMEM((columns, rank), F32)],
        compiler_params=pltpu.CompilerParams(vmem_limit_bytes=16 * MIB),
        cost_estimate=pl.CostEstimate(
            flops=6 * users * rank * columns, bytes_accessed=4 * users * columns, transcendentals=0
        ),
        name="finish",
    )(*ins)


def solution(mesh):
    placed = (
        P("leaf", "col"),
        P("leaf", None, None),
        P("leaf", None, None),
        P("leaf", None, None),
        P(),
        P(),
    )
    return jax.shard_map(
        local, mesh=mesh, in_specs=placed, out_specs=P("leaf", "col"), check_vma=False
    )
```

time: 243 us -> 61.5 us (0.25)
  waiting for transfers between devices: 117 us -> 16.1 us
  local copies, waits for them, and re-layouts: 60.1 us -> 2.99 us
  matrix products: 39.2 us -> 0 us
  starting transfers between devices: 3.61 us -> 27.6 us
  Pallas kernels: 0 us -> 14.6 us
  between operations: 13.9 us -> 0.12 us
  other arithmetic: 8.57 us -> 0 us
    all_gather x1 -> x0, waiting for transfers between devices: 93.5 us -> none  [local(): received = lax.all_gather(outgoing[:, None], 'leaf', axis=1, tiled=True)]
    another operation x5 -> x0, local copies, waits for them, and re-layouts: 44.5 us -> none  [the longest x4 44.5 us: assemble(): pieces.reshape(leaves // 4, 4, rank, quarter_cols).transpose(0, 2, 1, 3)]
    dot_general x16 -> x0, matrix products: 39.2 us -> none  [the longest x9 15.9 us: couple(): jnp.dot(coupling_all[height, offset - 1], chosen, precision=highest, pref...]
    ppermute x2 -> x15, starting transfers between devices: 3.6 us -> 27.6 us  [swap(): return lax.ppermute(block, 'leaf', [(i, i ^ bits) for i in range(count)])]
    pallas_call x0 -> x9, Pallas kernels: none -> 14.6 us  [the longest x8 11.7 us: run(): pl.pallas_call(body, out_shape=[pltpu.VMEM(shape, F32) for shape in outs]...]
    slice x2 -> x0, local copies, waits for them, and re-layouts: 14 us -> none  [the longest x1 11.3 us: local(): received[1]]
    ppermute x2 -> x15, waiting for transfers between devices: 23.3 us -> 16.1 us  [swap(): return lax.ppermute(block, 'leaf', [(i, i ^ bits) for i in range(count)])]
    reduce_sum x1 -> x0, other arithmetic: 4.22 us -> none  [local(): assemble(received[1], leaves, rank, columns).reshape(-1, 4, rank, columns)]
  transfers between devices with their start and end apart: 3 -> 15, of which waited for: 3 -> 8; matrix products, arithmetic and copies ran while one was open for 8% -> 0% of each run, Pallas kernels for 0% -> 12%
where the time goes in v1:
time: 61.5 us; the launch traced here: 61.4 us
  starting transfers between devices  27.6 us (45%)
  waiting for transfers between devices  16.1 us (26%)
  Pallas kernels  14.6 us (24%)
  local copies, waits for them, and re-layouts  2.99 us (5%)
    ppermute x15, starting transfers between devices, swap(): return lax.ppermute(block, 'leaf', [(i, i ^ bits) for i in range(count)])  27.6 us
    ppermute x15, waiting for transfers between devices, swap(): return lax.ppermute(block, 'leaf', [(i, i ^ bits) for i in range(count)])  16.1 us
    pallas_call x8, Pallas kernels, run(): pl.pallas_call(body, out_shape=[pltpu.VMEM(shape, F32) for shape in outs]...  11.7 us
    unnamed x14, local copies, waits for them, and re-layouts  2.99 us
    pallas_call x1, Pallas kernels, local(): pl.pallas_call(finish, out_shape=jax.ShapeDtypeStruct((users, columns), F...  2.91 us
  transfers between devices with their start and end apart: 15, of which 8 were waited for; matrix products, arithmetic and copies ran while one was open for 0% of the time, Pallas kernels for 12%

profile of v1, /device:TPU:1, one launch (start us, length us, event | category | flops | bytes accessed | tf_op | source)
XLA Modules:
  0.0 61.4 jit_solution(15183470420943511230)
XLA Ops:
  0.0 1.7 %copy-done.2 = f32[1024,512]{1,0:T(8,128)S(1)} copy-done((f32[1024,512]{1,0:T(8,128)S(1)}, f32[1024,512]{1,0:T(8,128)}, u32[]{:S(2)}) %copy-start.2) | copy-done | bytes 2097176
  1.7 1.2 %copy-done.4 = f32[1,1024,256]{2,1,0:T(8,128)S(1)} copy-done((f32[1,1024,256]{2,1,0:T(8,128)S(1)}, f32[1,1024,256]{2,1,0:T(8,128)}, u32[]{:S(2)}) %copy-start.4) | copy-done | bytes 1048600
  3.0 1.3 %leaf_coefficients.1 = (f32[128,256]{1,0:T(8,128)S(1)}, f32[128,256]{1,0:T(8,128)S(1)}, f32[128,256]{1,0:T(8,128)S(1)}, f32[128,256]{1,0:T(8,128)S(1)}) custom-call(f32[1024,512]{1,0:T(8,128)S(1)} %copy-done.2, f32[1024,256]{1,0:T(8,128)S(1)} %bitcast.3), custom_call_target="tpu_custom_call" | custom-call | flops 805306368 | bytes 3145728 | tf_op jit(solution)/shard_map/leaf_coefficients/pallas_call | solution.py:24
  4.3 3.3 %collective-permute-start = (f32[128,256]{1,0:T(8,128)S(1)}, f32[128,256]{1,0:T(8,128)S(1)}, u32[]{:S(2)}, u32[]{:S(2)}) collective-permute-start(f32[128,256]{1,0:T(8,128)S(1)} %get-tuple-element.30), channel_id=1, source_target_pairs={{0,4},{4,0},{8,12},{12,8},{16,20},{20,16},{24,28},{28,24},{32,36},... | collective-permute-start | bytes 393224 | tf_op jit(solution)/shard_map/ppermute | solution.py:143
  7.6 1.7 %collective-permute-start.2 = (f32[128,256]{1,0:T(8,128)S(1)}, f32[128,256]{1,0:T(8,128)S(1)}, u32[]{:S(2)}, u32[]{:S(2)}) collective-permute-start(f32[128,256]{1,0:T(8,128)S(1)} %get-tuple-element.32), channel_id=1, source_target_pairs={{0,12},{4,8},{8,4},{12,0},{16,28},{20,24},{24,20},{28,16},{32,44},... | collective-permute-start | bytes 393224 | tf_op jit(solution)/shard_map/ppermute | solution.py:143
  9.3 3.3 %collective-permute-done.1.c2 = f32[128,256]{1,0:T(8,128)S(1)} collective-permute-done((f32[128,256]{1,0:T(8,128)S(1)}, f32[128,256]{1,0:T(8,128)S(1)}, u32[]{:S(2)}, u32[]{:S(2)}) %collective-permute-start.1) | collective-permute-done | bytes 131104 | tf_op jit(solution)/shard_map/ppermute | solution.py:143
  12.6 3.0 %collective-permute-done.2.c3 = f32[128,256]{1,0:T(8,128)S(1)} collective-permute-done((f32[128,256]{1,0:T(8,128)S(1)}, f32[128,256]{1,0:T(8,128)S(1)}, u32[]{:S(2)}, u32[]{:S(2)}) %collective-permute-start.2) | collective-permute-done | bytes 131104 | tf_op jit(solution)/shard_map/ppermute | solution.py:143
  15.6 0.4 lift_leaves.1
  16.1 1.5 %collective-permute-start.3 = (f32[32,256]{1,0:T(8,128)S(1)}, f32[32,256]{1,0:T(8,128)S(1)}, u32[]{:S(2)}, u32[]{:S(2)}) collective-permute-start(f32[32,256]{1,0:T(8,128)S(1)} %get-tuple-element.34), channel_id=1, source_target_pairs={{0,16},{4,20},{8,24},{12,28},{16,0},{20,4},{24,8},{28,12},{32,48},... | collective-permute-start | bytes 98312 | tf_op jit(solution)/shard_map/ppermute | solution.py:143
  17.6 5.0 %collective-permute-start.4 = (f32[32,256]{1,0:T(8,128)S(1)}, f32[32,256]{1,0:T(8,128)S(1)}, u32[]{:S(2)}, u32[]{:S(2)}) collective-permute-start(f32[32,256]{1,0:T(8,128)S(1)} %get-tuple-element.35), channel_id=1, source_target_pairs={{0,32},{4,36},{8,40},{12,44},{16,48},{20,52},{24,56},{28,60},{32,0... | collective-permute-start | bytes 98312 | tf_op jit(solution)/shard_map/ppermute | solution.py:143
  22.5 1.8 %collective-permute-done.4.c2 = f32[32,256]{1,0:T(8,128)S(1)} collective-permute-done((f32[32,256]{1,0:T(8,128)S(1)}, f32[32,256]{1,0:T(8,128)S(1)}, u32[]{:S(2)}, u32[]{:S(2)}) %collective-permute-start.4) | collective-permute-done | bytes 32800 | tf_op jit(solution)/shard_map/ppermute | solution.py:143
  24.4 3.0 %collective-permute-done.5.c3 = f32[32,256]{1,0:T(8,128)S(1)} collective-permute-done((f32[32,256]{1,0:T(8,128)S(1)}, f32[32,256]{1,0:T(8,128)S(1)}, u32[]{:S(2)}, u32[]{:S(2)}) %collective-permute-start.5) | collective-permute-done | bytes 32800 | tf_op jit(solution)/shard_map/ppermute | solution.py:143
  27.4 0.4 lift_nodes.1.c0
  27.8 2.8 %collective-permute-start.8 = (f32[32,256]{1,0:T(8,128)S(1)}, f32[32,256]{1,0:T(8,128)S(1)}, u32[]{:S(2)}, u32[]{:S(2)}) collective-permute-start(f32[32,256]{1,0:T(8,128)S(1)} %lift_nodes.1.c0), channel_id=1, source_target_pairs={{0,192},{4,196},{8,200},{12,204},{16,208},{20,212},{24,216},{28,22... | collective-permute-start | bytes 98312 | tf_op jit(solution)/shard_map/ppermute | solution.py:143
  30.6 0.4 collective-permute-start.7
  31.0 0.3 collective-permute-start.6
  31.3 1.4 %couple_nodes.1 = (f32[32,256]{1,0:T(8,128)S(1)}, f32[32,256]{1,0:T(8,128)S(1)}, f32[32,256]{1,0:T(8,128)S(1)}, f32[32,256]{1,0:T(8,128)S(1)}) custom-call(f32[32,256]{1,0:T(8,128)S(1)} %get-tuple-element.33.c0, f32[32,256]{1,0:T(8,128)S(1)} %collective-permute-done.3.c1, f32[32,256]{1,0:T(8,128)S(1)} %collective-permute-done.4.c2, ...), custom_call_target="tpu_custom_call" | custom-call | flops 150994944 | bytes 2490368 | tf_op jit(solution)/shard_map/couple_nodes/pallas_call | solution.py:24
  32.8 2.1 %collective-permute-done.7.c2 = f32[32,256]{1,0:T(8,128)S(1)} collective-permute-done((f32[32,256]{1,0:T(8,128)S(1)}, f32[32,256]{1,0:T(8,128)S(1)}, u32[]{:S(2)}, u32[]{:S(2)}) %collective-permute-start.7) | collective-permute-done | bytes 32800 | tf_op jit(solution)/shard_map/ppermute | solution.py:143
  34.9 1.4 %top.1 = (f32[32,256]{1,0:T(8,128)S(1)}, f32[32,256]{1,0:T(8,128)S(1)}, f32[32,256]{1,0:T(8,128)S(1)}, f32[32,256]{1,0:T(8,128)S(1)}) custom-call(f32[32,256]{1,0:T(8,128)S(1)} %lift_nodes.1.c0, f32[32,256]{1,0:T(8,128)S(1)} %collective-permute-done.6.c1, f32[32,256]{1,0:T(8,128)S(1)} %collective-permute-done.7.c2, f32[32,256]{1,0:T(8,128)S(1)} %collective-permute-done.8.c3, ...), custom_call_target="tpu_custom_call" | custom-call | flops 88080384 | bytes 4718592 | tf_op jit(solution)/shard_map/top/pallas_call | solution.py:24
  36.3 1.2 %collective-permute-start.9 = (f32[32,256]{1,0:T(8,128)S(1)}, f32[32,256]{1,0:T(8,128)S(1)}, u32[]{:S(2)}, u32[]{:S(2)}) collective-permute-start(f32[32,256]{1,0:T(8,128)S(1)} %get-tuple-element.42), channel_id=1, source_target_pairs={{0,16},{4,20},{8,24},{12,28},{16,0},{20,4},{24,8},{28,12},{32,48},... | collective-permute-start | bytes 98312 | tf_op jit(solution)/shard_map/ppermute | solution.py:143
  37.5 1.9 %collective-permute-start.10 = (f32[32,256]{1,0:T(8,128)S(1)}, f32[32,256]{1,0:T(8,128)S(1)}, u32[]{:S(2)}, u32[]{:S(2)}) collective-permute-start(f32[32,256]{1,0:T(8,128)S(1)} %get-tuple-element.43), channel_id=1, source_target_pairs={{0,32},{4,36},{8,40},{12,44},{16,48},{20,52},{24,56},{28,60},{32,0... | collective-permute-start | bytes 98312 | tf_op jit(solution)/shard_map/ppermute | solution.py:143
  39.5 2.5 %collective-permute-start.11 = (f32[32,256]{1,0:T(8,128)S(1)}, f32[32,256]{1,0:T(8,128)S(1)}, u32[]{:S(2)}, u32[]{:S(2)}) collective-permute-start(f32[32,256]{1,0:T(8,128)S(1)} %get-tuple-element.44), channel_id=1, source_target_pairs={{0,48},{4,52},{8,56},{12,60},{16,32},{20,36},{24,40},{28,44},{32,1... | collective-permute-start | bytes 98312 | tf_op jit(solution)/shard_map/ppermute | solution.py:143
  42.0 1.7 %couple_leaves.1 = (f32[128,256]{1,0:T(8,128)S(1)}, f32[128,256]{1,0:T(8,128)S(1)}, f32[128,256]{1,0:T(8,128)S(1)}, f32[128,256]{1,0:T(8,128)S(1)}) custom-call(f32[128,256]{1,0:T(8,128)S(1)} %get-tuple-element.29.c0, f32[128,256]{1,0:T(8,128)S(1)} %collective-permute-done.c1, f32[128,256]{1,0:T(8,128)S(1)} %collective-permute-done.1.c2, ...), custom_call_target="tpu_custom_call" | custom-call | flops 603979776 | bytes 2883584 | tf_op jit(solution)/shard_map/couple_leaves/pallas_call | solution.py:24
  43.7 0.6 %collective-permute-done.10.g2 = f32[32,256]{1,0:T(8,128)S(1)} collective-permute-done((f32[32,256]{1,0:T(8,128)S(1)}, f32[32,256]{1,0:T(8,128)S(1)}, u32[]{:S(2)}, u32[]{:S(2)}) %collective-permute-start.10) | collective-permute-done | bytes 32800 | tf_op jit(solution)/shard_map/ppermute | solution.py:143
  44.3 0.3 collective-permute-done.11.g3
  44.6 0.7 %down.1 = (f32[128,256]{1,0:T(8,128)S(1)}, f32[128,256]{1,0:T(8,128)S(1)}, f32[128,256]{1,0:T(8,128)S(1)}, f32[128,256]{1,0:T(8,128)S(1)}) custom-call(f32[32,256]{1,0:T(8,128)S(1)} %get-tuple-element.41.g0, f32[32,256]{1,0:T(8,128)S(1)} %collective-permute-done.9.g1, f32[32,256]{1,0:T(8,128)S(1)} %collective-permute-done.10.g2, ...), custom_call_target="tpu_custom_call" | custom-call | flops 201326592 | bytes 2752512 | tf_op jit(solution)/shard_map/down/pallas_call | solution.py:24
  45.3 5.1 %collective-permute-start.12 = (f32[128,256]{1,0:T(8,128)S(1)}, f32[128,256]{1,0:T(8,128)S(1)}, u32[]{:S(2)}, u32[]{:S(2)}) collective-permute-start(f32[128,256]{1,0:T(8,128)S(1)} %get-tuple-element.50), channel_id=1, source_target_pairs={{0,4},{4,0},{8,12},{12,8},{16,20},{20,16},{24,28},{28,24},{32,36},... | collective-permute-start | bytes 393224 | tf_op jit(solution)/shard_map/ppermute | solution.py:143
  50.5 0.2 collective-permute-start.13
  50.7 1.5 %collective-permute-start.14 = (f32[128,256]{1,0:T(8,128)S(1)}, f32[128,256]{1,0:T(8,128)S(1)}, u32[]{:S(2)}, u32[]{:S(2)}) collective-permute-start(f32[128,256]{1,0:T(8,128)S(1)} %get-tuple-element.52), channel_id=1, source_target_pairs={{0,12},{4,8},{8,4},{12,0},{16,28},{20,24},{24,20},{28,16},{32,44},... | collective-permute-start | bytes 393224 | tf_op jit(solution)/shard_map/ppermute | solution.py:143
  52.2 4.5 %near_field.1.near = f32[1024,512]{1,0:T(8,128)S(1)} custom-call(f32[1024,1024]{1,0:T(8,128)S(1)} %bitcast.5, f32[1024,512]{1,0:T(8,128)S(1)} %copy-done.3), custom_call_target="tpu_custom_call" | custom-call | flops 3221225472 | bytes 6291456 | tf_op jit(solution)/shard_map/near_field/pallas_call | solution.py:24
  56.7 1.8 %collective-permute-done.14.g3 = f32[128,256]{1,0:T(8,128)S(1)} collective-permute-done((f32[128,256]{1,0:T(8,128)S(1)}, f32[128,256]{1,0:T(8,128)S(1)}, u32[]{:S(2)}, u32[]{:S(2)}) %collective-permute-start.14) | collective-permute-done | bytes 131104 | tf_op jit(solution)/shard_map/ppermute | solution.py:143
  58.5 2.9 %finish.1 = f32[1024,512]{1,0:T(8,128)} custom-call(f32[1024,512]{1,0:T(8,128)S(1)} %near_field.1.near, f32[1024,256]{1,0:T(8,128)S(1)} %bitcast.4, f32[128,256]{1,0:T(8,128)S(1)} %get-tuple-element.49.g0, f32[128,256]{1,0:T(8,128)S(1)} %collective-permute-done.12.g1, f32[128,256]{1,0:T(8,128)S(1)} %collective-permute-done.13.g2, ...), custom_call_target="tpu_custom_call" | custom-call | flops 805306368 | bytes 2097152 | tf_op jit(solution)/shard_map/finish/pallas_call | solution.py:222
  (21 shorter events, 0.0 us)
Async XLA Ops:
  0.0 15.6 %copy-start = (f32[2,4,256,256]{3,2,1,0:T(8,128)S(1)}, f32[2,4,256,256]{3,2,1,0:T(8,128)}, u32[]{:S(2)}) copy-start(f32[2,4,256,256]{3,2,1,0:T(8,128)} %transfers.7) | copy-start | bytes 6291460
  0.0 1.7 %copy-start.2 = (f32[1024,512]{1,0:T(8,128)S(1)}, f32[1024,512]{1,0:T(8,128)}, u32[]{:S(2)}) copy-start(f32[1024,512]{1,0:T(8,128)} %x.3) | copy-start | bytes 6291460
  1.7 1.2 %copy-start.4 = (f32[1,1024,256]{2,1,0:T(8,128)S(1)}, f32[1,1024,256]{2,1,0:T(8,128)}, u32[]{:S(2)}) copy-start(f32[1,1024,256]{2,1,0:T(8,128)} %param.9) | copy-start | bytes 3145732
  4.3 5.1 %collective-permute-start = (f32[128,256]{1,0:T(8,128)S(1)}, f32[128,256]{1,0:T(8,128)S(1)}, u32[]{:S(2)}, u32[]{:S(2)}) collective-permute-start(f32[128,256]{1,0:T(8,128)S(1)} %get-tuple-element.30), channel_id=1, source_target_pairs={{0,4},{4,0},{8,12},{12,8},{16,20},{20,16},{24,28},{28,24},{32,36},... | collective-permute-start | bytes 393224 | tf_op jit(solution)/shard_map/ppermute | solution.py:143
  7.6 5.1 %collective-permute-start.1 = (f32[128,256]{1,0:T(8,128)S(1)}, f32[128,256]{1,0:T(8,128)S(1)}, u32[]{:S(2)}, u32[]{:S(2)}) collective-permute-start(f32[128,256]{1,0:T(8,128)S(1)} %get-tuple-element.31), channel_id=1, source_target_pairs={{0,8},{4,12},{8,0},{12,4},{16,24},{20,28},{24,16},{28,20},{32,40},... | collective-permute-start | bytes 393224 | tf_op jit(solution)/shard_map/ppermute | solution.py:143
  7.6 8.0 %collective-permute-start.2 = (f32[128,256]{1,0:T(8,128)S(1)}, f32[128,256]{1,0:T(8,128)S(1)}, u32[]{:S(2)}, u32[]{:S(2)}) collective-permute-start(f32[128,256]{1,0:T(8,128)S(1)} %get-tuple-element.32), channel_id=1, source_target_pairs={{0,12},{4,8},{8,4},{12,0},{16,28},{20,24},{24,20},{28,16},{32,44},... | collective-permute-start | bytes 393224 | tf_op jit(solution)/shard_map/ppermute | solution.py:143
  15.6 15.7 %copy-start.1 = (f32[3,3,256,256]{3,2,1,0:T(8,128)S(1)}, f32[3,3,256,256]{3,2,1,0:T(8,128)}, u32[]{:S(2)}) copy-start(f32[3,3,256,256]{3,2,1,0:T(8,128)} %couplings.5) | copy-start | bytes 7077892
  16.1 6.5 %collective-permute-start.3 = (f32[32,256]{1,0:T(8,128)S(1)}, f32[32,256]{1,0:T(8,128)S(1)}, u32[]{:S(2)}, u32[]{:S(2)}) collective-permute-start(f32[32,256]{1,0:T(8,128)S(1)} %get-tuple-element.34), channel_id=1, source_target_pairs={{0,16},{4,20},{8,24},{12,28},{16,0},{20,4},{24,8},{28,12},{32,48},... | collective-permute-start | bytes 98312 | tf_op jit(solution)/shard_map/ppermute | solution.py:143
  17.6 6.8 %collective-permute-start.4 = (f32[32,256]{1,0:T(8,128)S(1)}, f32[32,256]{1,0:T(8,128)S(1)}, u32[]{:S(2)}, u32[]{:S(2)}) collective-permute-start(f32[32,256]{1,0:T(8,128)S(1)} %get-tuple-element.35), channel_id=1, source_target_pairs={{0,32},{4,36},{8,40},{12,44},{16,48},{20,52},{24,56},{28,60},{32,0... | collective-permute-start | bytes 98312 | tf_op jit(solution)/shard_map/ppermute | solution.py:143
  22.5 4.9 %collective-permute-start.5 = (f32[32,256]{1,0:T(8,128)S(1)}, f32[32,256]{1,0:T(8,128)S(1)}, u32[]{:S(2)}, u32[]{:S(2)}) collective-permute-start(f32[32,256]{1,0:T(8,128)S(1)} %get-tuple-element.36), channel_id=1, source_target_pairs={{0,48},{4,52},{8,56},{12,60},{16,32},{20,36},{24,40},{28,44},{32,1... | collective-permute-start | bytes 98312 | tf_op jit(solution)/shard_map/ppermute | solution.py:143
  27.8 4.9 %collective-permute-start.8 = (f32[32,256]{1,0:T(8,128)S(1)}, f32[32,256]{1,0:T(8,128)S(1)}, u32[]{:S(2)}, u32[]{:S(2)}) collective-permute-start(f32[32,256]{1,0:T(8,128)S(1)} %lift_nodes.1.c0), channel_id=1, source_target_pairs={{0,192},{4,196},{8,200},{12,204},{16,208},{20,212},{24,216},{28,22... | collective-permute-start | bytes 98312 | tf_op jit(solution)/shard_map/ppermute | solution.py:143
  30.6 4.3 %collective-permute-start.7 = (f32[32,256]{1,0:T(8,128)S(1)}, f32[32,256]{1,0:T(8,128)S(1)}, u32[]{:S(2)}, u32[]{:S(2)}) collective-permute-start(f32[32,256]{1,0:T(8,128)S(1)} %lift_nodes.1.c0), channel_id=1, source_target_pairs={{0,128},{4,132},{8,136},{12,140},{16,144},{20,148},{24,152},{28,15... | collective-permute-start | bytes 98312 | tf_op jit(solution)/shard_map/ppermute | solution.py:143
  31.0 3.9 %collective-permute-start.6 = (f32[32,256]{1,0:T(8,128)S(1)}, f32[32,256]{1,0:T(8,128)S(1)}, u32[]{:S(2)}, u32[]{:S(2)}) collective-permute-start(f32[32,256]{1,0:T(8,128)S(1)} %lift_nodes.1.c0), channel_id=1, source_target_pairs={{0,64},{4,68},{8,72},{12,76},{16,80},{20,84},{24,88},{28,92},{32,9... | collective-permute-start | bytes 98312 | tf_op jit(solution)/shard_map/ppermute | solution.py:143
  34.9 17.3 %copy-start.6 = (f32[1,1024,1024]{2,1,0:T(8,128)S(1)}, f32[1,1024,1024]{2,1,0:T(8,128)}, u32[]{:S(2)}) copy-start(f32[1,1024,1024]{2,1,0:T(8,128)} %param.7) | copy-start | bytes 12582916
  36.3 7.4 %collective-permute-start.9 = (f32[32,256]{1,0:T(8,128)S(1)}, f32[32,256]{1,0:T(8,128)S(1)}, u32[]{:S(2)}, u32[]{:S(2)}) collective-permute-start(f32[32,256]{1,0:T(8,128)S(1)} %get-tuple-element.42), channel_id=1, source_target_pairs={{0,16},{4,20},{8,24},{12,28},{16,0},{20,4},{24,8},{28,12},{32,48},... | collective-permute-start | bytes 98312 | tf_op jit(solution)/shard_map/ppermute | solution.py:143
  37.5 6.8 %collective-permute-start.10 = (f32[32,256]{1,0:T(8,128)S(1)}, f32[32,256]{1,0:T(8,128)S(1)}, u32[]{:S(2)}, u32[]{:S(2)}) collective-permute-start(f32[32,256]{1,0:T(8,128)S(1)} %get-tuple-element.43), channel_id=1, source_target_pairs={{0,32},{4,36},{8,40},{12,44},{16,48},{20,52},{24,56},{28,60},{32,0... | collective-permute-start | bytes 98312 | tf_op jit(solution)/shard_map/ppermute | solution.py:143
  39.5 5.2 %collective-permute-start.11 = (f32[32,256]{1,0:T(8,128)S(1)}, f32[32,256]{1,0:T(8,128)S(1)}, u32[]{:S(2)}, u32[]{:S(2)}) collective-permute-start(f32[32,256]{1,0:T(8,128)S(1)} %get-tuple-element.44), channel_id=1, source_target_pairs={{0,48},{4,52},{8,56},{12,60},{16,32},{20,36},{24,40},{28,44},{32,1... | collective-permute-start | bytes 98312 | tf_op jit(solution)/shard_map/ppermute | solution.py:143
  43.7 8.5 %copy-start.3 = (f32[1024,512]{1,0:T(8,128)S(1)}, f32[1024,512]{1,0:T(8,128)}, u32[]{:S(2)}) copy-start(f32[1024,512]{1,0:T(8,128)} %x.3) | copy-start | bytes 6291460
  45.3 11.4 %collective-permute-start.12 = (f32[128,256]{1,0:T(8,128)S(1)}, f32[128,256]{1,0:T(8,128)S(1)}, u32[]{:S(2)}, u32[]{:S(2)}) collective-permute-start(f32[128,256]{1,0:T(8,128)S(1)} %get-tuple-element.50), channel_id=1, source_target_pairs={{0,4},{4,0},{8,12},{12,8},{16,20},{20,16},{24,28},{28,24},{32,36},... | collective-permute-start | bytes 393224 | tf_op jit(solution)/shard_map/ppermute | solution.py:143
  50.5 6.2 %collective-permute-start.13 = (f32[128,256]{1,0:T(8,128)S(1)}, f32[128,256]{1,0:T(8,128)S(1)}, u32[]{:S(2)}, u32[]{:S(2)}) collective-permute-start(f32[128,256]{1,0:T(8,128)S(1)} %get-tuple-element.51), channel_id=1, source_target_pairs={{0,8},{4,12},{8,0},{12,4},{16,24},{20,28},{24,16},{28,20},{32,40},... | collective-permute-start | bytes 393224 | tf_op jit(solution)/shard_map/ppermute | solution.py:143
  50.7 7.8 %collective-permute-start.14 = (f32[128,256]{1,0:T(8,128)S(1)}, f32[128,256]{1,0:T(8,128)S(1)}, u32[]{:S(2)}, u32[]{:S(2)}) collective-permute-start(f32[128,256]{1,0:T(8,128)S(1)} %get-tuple-element.52), channel_id=1, source_target_pairs={{0,12},{4,8},{8,4},{12,0},{16,28},{20,24},{24,20},{28,16},{32,44},... | collective-permute-start | bytes 393224 | tf_op jit(solution)/shard_map/ppermute | solution.py:143
  52.2 6.3 %copy-start.5 = (f32[1,1024,256]{2,1,0:T(8,128)S(1)}, f32[1,1024,256]{2,1,0:T(8,128)}, u32[]{:S(2)}) copy-start(f32[1,1024,256]{2,1,0:T(8,128)} %param.8) | copy-start | bytes 3145732

commit v2 on v1

v2 whole, which is shorter than its diff:
```python
import functools

import jax
import jax.numpy as jnp
from jax import lax
from jax.experimental import pallas as pl
from jax.experimental.pallas import tpu as pltpu
from jax.sharding import PartitionSpec as P

F32 = jnp.float32
HIGH = lax.Precision.HIGH
MIB = 1 << 20
VMEM = pl.BlockSpec(memory_space=pltpu.VMEM)
ANY = pl.BlockSpec(memory_space=pl.ANY)


def dot(a, b, ca, cb):
    return lax.dot_general(
        a, b, (((ca,), (cb,)), ((), ())), precision=HIGH, preferred_element_type=F32
    )


def cost(flops, size):
    return pl.CostEstimate(flops=flops, bytes_accessed=4 * size, transcendentals=0)


def run(body, ins, outs, name, flops, after=(), scratch=(), vmem=24):
    ins = [pltpu.with_memory_space_constraint(x, pltpu.VMEM) for x in ins]

    def kernel(*refs):
        body(*refs[: len(ins)], *refs[len(ins) + len(after) :])

    return pl.pallas_call(
        kernel,
        out_shape=[pltpu.VMEM(shape, F32) for shape in outs],
        in_specs=[VMEM] * len(ins) + [ANY] * len(after),
        out_specs=[VMEM] * len(outs),
        scratch_shapes=list(scratch),
        compiler_params=pltpu.CompilerParams(vmem_limit_bytes=vmem * MIB),
        cost_estimate=cost(flops, sum(x.size for x in ins)),
        name=name,
    )(*ins, *after)


def place():
    leaf = lax.axis_index("leaf")
    return leaf % 4, (leaf // 4) % 4, leaf // 16


def other(index, j):
    low, high = index % 2, index // 2
    low = 1 - low if j & 1 else low
    high = 1 - high if j & 2 else high
    return 2 * high + low


def rows(index, count):
    return pl.ds(pl.multiple_of(index * count, count), count)


CHUNKS = 4


def leaf_coefficients(x, basis, o0, o1, o2, o3, held, basis_held, whole, sems):
    p, _, _ = place()
    chunk = x.shape[0] // CHUNKS
    copies = []
    for i in range(CHUNKS):
        at = pl.ds(i * chunk, chunk)
        pair = (
            pltpu.make_async_copy(x.at[at], held.at[at], sems.at[0, i]),
            pltpu.make_async_copy(basis.at[at], basis_held.at[at], sems.at[1, i]),
        )
        for copy in pair:
            copy.start()
        copies.append(pair)
    for i, pair in enumerate(copies):
        at = pl.ds(i * chunk, chunk)
        for copy in pair:
            copy.wait()
        term = dot(held[at, :], basis_held[at, :], 0, 0)
        whole[...] = term if i == 0 else whole[...] + term
    step = o0.shape[0]
    for j, out in enumerate((o0, o1, o2, o3)):
        out[...] = whole[rows(other(p, j), step), :]


def near_field(dense, x, out):
    @pl.loop(0, 4)
    def _(i):
        at = rows(i, 256)
        out[at, :] = dot(dense[at, :], x[...], 1, 0)


def lift(digit, level, c0, c1, c2, c3, transfers, out):
    own = place()[digit]
    total = None
    for j, c in enumerate((c0, c1, c2, c3)):
        term = dot(c[...], transfers[level, other(own, j)], 1, 0)
        total = term if total is None else total + term
    out[...] = total


def field_of(target, own, parts, level, couplings):
    at = other(own, target)
    total = None
    for j, c in enumerate(parts):
        if j == target:
            continue
        offset = (other(own, j) - at + 4) % 4
        term = dot(c[...], couplings[level, offset - 1], 1, 1)
        total = term if total is None else total + term
    return total


def couple(digit, level, c0, c1, c2, c3, couplings, *fields):
    own = place()[digit]
    for target, out in enumerate(fields):
        out[...] = field_of(target, own, (c0, c1, c2, c3), level, couplings)


def descend(c0, c1, c2, c3, couplings, transfers, field, f0, f1, f2, f3, o0, o1, o2, o3):
    p, q, r = place()
    g = field_of(0, r, (c0, c1, c2, c3), 2, couplings)
    g = field[...] + dot(g, transfers[1, q], 1, 1)
    for j, (f, out) in enumerate(zip((f0, f1, f2, f3), (o0, o1, o2, o3))):
        out[...] = f[...] + dot(g, transfers[0, other(p, j)], 1, 1)


def finish(half, near, row_basis, g0, g1, *rest):
    out, block, whole, sems = rest[-4:]
    p, _, _ = place()
    step = g0.shape[0]
    for j, g in enumerate((g0, g1)):
        whole[rows(other(p, j) % 2, step), :] = g[...]
    side = p // 2 if half == 0 else 1 - p // 2
    columns = rows(side, 2 * step)
    chunk = out.shape[0] // CHUNKS
    copies = []
    for i in range(CHUNKS):
        at = pl.ds(i * chunk, chunk)
        block[at, :] = near[at, columns] + dot(row_basis[at, :], whole[...], 1, 1)
        copy = pltpu.make_async_copy(block.at[at], out.at[at, columns], sems.at[i])
        copy.start()
        copies.append(copy)
    for copy in copies:
        copy.wait()


def swap(block, bits):
    count = lax.axis_size("leaf")
    return lax.ppermute(block, "leaf", [(i, i ^ bits) for i in range(count)])


def exchange(blocks, digit, order=(2, 3, 1)):
    got = {j: swap(blocks[j], j << 2 * digit) for j in order}
    return [blocks[0]] + [got[j] for j in (1, 2, 3)]


def local(ratings, dense_blocks, row_basis, col_basis, transfers, couplings):
    users, columns = ratings.shape
    rank = col_basis.shape[2]
    quarter = columns // 4
    unit = 2 * 3 * rank * rank
    dense, rbasis, cbasis = dense_blocks[0], row_basis[0], col_basis[0]

    *coef, held = pl.pallas_call(
        leaf_coefficients,
        out_shape=[pltpu.VMEM((quarter, rank), F32)] * 4 + [pltpu.VMEM((users, columns), F32)],
        in_specs=[ANY] * 2,
        out_specs=[VMEM] * 5,
        scratch_shapes=[
            pltpu.VMEM((users, rank), F32),
            pltpu.VMEM((columns, rank), F32),
            pltpu.SemaphoreType.DMA((2, CHUNKS)),
        ],
        compiler_params=pltpu.CompilerParams(vmem_limit_bytes=24 * MIB),
        cost_estimate=cost(6 * users * columns * rank, users * columns),
        name="leaf_coefficients",
    )(*[pltpu.with_memory_space_constraint(x, pltpu.HBM) for x in (ratings, cbasis)])
    coef = exchange(coef, 0)
    (near,) = run(
        near_field, [dense, held], [(users, columns)], "near_field", 6 * users * users * columns
    )
    (lifted,) = run(
        functools.partial(lift, 0, 0),
        [*coef, transfers],
        [(quarter, rank)],
        "lift_leaves",
        unit * columns,
        after=[near],
    )
    lifted = exchange([lifted] * 4, 1, (1, 3, 2))
    leaf_fields = run(
        functools.partial(couple, 0, 0),
        [*coef, couplings],
        [(quarter, rank)] * 4,
        "couple_leaves",
        unit * 3 * columns,
    )
    (crown,) = run(
        functools.partial(lift, 1, 1),
        [*lifted, transfers],
        [(quarter, rank)],
        "lift_nodes",
        unit * columns,
        after=leaf_fields,
    )
    crown = exchange([crown] * 4, 2, (1, 3, 2))
    (node_field,) = run(
        functools.partial(couple, 1, 1),
        [*lifted, couplings],
        [(quarter, rank)],
        "couple_nodes",
        unit * 3 * quarter,
    )
    leaf_g = run(
        descend,
        [*crown, couplings, transfers, node_field, *leaf_fields],
        [(quarter, rank)] * 4,
        "descend",
        unit * 8 * quarter,
    )
    leaf_g = exchange(leaf_g, 0)

    def half(which, pieces, out):
        ins = [
            pltpu.with_memory_space_constraint(x, pltpu.VMEM) for x in (near, rbasis, *pieces)
        ]
        return pl.pallas_call(
            functools.partial(finish, which),
            out_shape=pltpu.HBM((users, columns), F32),
            in_specs=[VMEM] * 4 + [ANY] * len(out),
            out_specs=ANY,
            scratch_shapes=[
                pltpu.VMEM((users, columns // 2), F32),
                pltpu.VMEM((columns // 2, rank), F32),
                pltpu.SemaphoreType.DMA((CHUNKS,)),
            ],
            input_output_aliases={4: 0} if out else {},
            compiler_params=pltpu.CompilerParams(vmem_limit_bytes=24 * MIB),
            cost_estimate=cost(3 * users * rank * columns, users * columns),
            name=("finish_own", "finish_other")[which],
        )(*ins, *out)

    out = half(0, leaf_g[:2], [])
    return half(1, leaf_g[2:], [out])


def solution(mesh):
    placed = (
        P("leaf", "col"),
        P("leaf", None, None),
        P("leaf", None, None),
        P("leaf", None, None),
        P(),
        P(),
    )
    return jax.shard_map(
        local, mesh=mesh, in_specs=placed, out_specs=P("leaf", "col"), check_vma=False
    )
```

time: 61.5 us -> 58.5 us (0.951)
  starting transfers between devices: 27.6 us -> 19 us
  waiting for transfers between devices: 16.1 us -> 21.3 us
  Pallas kernels: 14.6 us -> 15.7 us
  local copies, waits for them, and re-layouts: 2.99 us -> 2.2 us
    ppermute x15 -> x12, starting transfers between devices: 27.6 us -> 19 us  [swap(): return lax.ppermute(block, 'leaf', [(i, i ^ bits) for i in range(count)])]
    ppermute x15 -> x12, waiting for transfers between devices: 16.1 us -> 21.3 us  [swap(): return lax.ppermute(block, 'leaf', [(i, i ^ bits) for i in range(count)])]
    pallas_call x9, Pallas kernels: 14.6 us -> 15.7 us  [the longest x6 9.31 us: run(): pl.pallas_call(kernel, out_shape=[pltpu.VMEM(shape, F32) for shape in out...]
    unnamed x14 -> x8, local copies, waits for them, and re-layouts: 2.99 us -> 2.2 us
  transfers between devices with their start and end apart: 15 -> 12, of which waited for: 8 -> 8; matrix products, arithmetic and copies ran while one was open for 0% -> 0% of each run, Pallas kernels for 12% -> 14%
where the time goes in v2:
time: 58.5 us; the launch traced here: 58.4 us
  waiting for transfers between devices  21.3 us (36%)
  starting transfers between devices  19 us (32%)
  Pallas kernels  15.7 us (27%)
  local copies, waits for them, and re-layouts  2.2 us (4%)
    ppermute x12, waiting for transfers between devices, swap(): return lax.ppermute(block, 'leaf', [(i, i ^ bits) for i in range(count)])  21.3 us
    ppermute x12, starting transfers between devices, swap(): return lax.ppermute(block, 'leaf', [(i, i ^ bits) for i in range(count)])  19 us
    pallas_call x6, Pallas kernels, run(): pl.pallas_call(kernel, out_shape=[pltpu.VMEM(shape, F32) for shape in out...  9.31 us
    pallas_call x1, Pallas kernels, local(): pl.pallas_call(leaf_coefficients, out_shape=[pltpu.VMEM((quarter, rank),...  3.35 us
    pallas_call x2, Pallas kernels, half(): pl.pallas_call(functools.partial(finish, which), out_shape=pltpu.HBM((use...  3.04 us
    unnamed x8, local copies, waits for them, and re-layouts  2.2 us
  transfers between devices with their start and end apart: 12, of which 8 were waited for; matrix products, arithmetic and copies ran while one was open for 0% of the time, Pallas kernels for 14%

profile of v2, /device:TPU:1, one launch (start us, length us, event | category | flops | bytes accessed | tf_op | source)
XLA Modules:
  0.0 58.4 jit_solution(13857621745477416183)
XLA Ops:
  0.0 3.3 %leaf_coefficients.1 = (f32[128,256]{1,0:T(8,128)S(1)}, f32[128,256]{1,0:T(8,128)S(1)}, f32[128,256]{1,0:T(8,128)S(1)}, f32[128,256]{1,0:T(8,128)S(1)}, f32[1024,512]{1,0:T(8,128)S(1)}) custom-call(f32[1024,512]{1,0:T(8,128)} %x.1, f32[1024,256]{1,0:T(8,128)} %bitcast.6), custom_call_target="tpu_custom_call" | custom-call | flops 805306368 | bytes 2097152 | tf_op jit(solution)/shard_map/leaf_coefficients/pallas_call | solution.py:167
  3.4 3.3 %collective-permute-start = (f32[128,256]{1,0:T(8,128)S(1)}, f32[128,256]{1,0:T(8,128)S(1)}, u32[]{:S(2)}, u32[]{:S(2)}) collective-permute-start(f32[128,256]{1,0:T(8,128)S(1)} %get-tuple-element.20), channel_id=1, source_target_pairs={{0,4},{4,0},{8,12},{12,8},{16,20},{20,16},{24,28},{28,24},{32,36},... | collective-permute-start | bytes 393224 | tf_op jit(solution)/shard_map/ppermute | solution.py:152
  6.7 0.0 collective-permute-start.1
  6.7 1.7 %collective-permute-start.2 = (f32[128,256]{1,0:T(8,128)S(1)}, f32[128,256]{1,0:T(8,128)S(1)}, u32[]{:S(2)}, u32[]{:S(2)}) collective-permute-start(f32[128,256]{1,0:T(8,128)S(1)} %get-tuple-element.22), channel_id=1, source_target_pairs={{0,12},{4,8},{8,4},{12,0},{16,28},{20,24},{24,20},{28,16},{32,44},... | collective-permute-start | bytes 393224 | tf_op jit(solution)/shard_map/ppermute | solution.py:152
  8.4 2.2 %copy-done.3 = f32[1,1024,1024]{2,1,0:T(8,128)S(1)} copy-done((f32[1,1024,1024]{2,1,0:T(8,128)S(1)}, f32[1,1024,1024]{2,1,0:T(8,128)}, u32[]{:S(2)}) %copy-start.3) | copy-done | bytes 4194328
  10.6 4.5 %near_field.1.refs_5_.near = f32[1024,512]{1,0:T(8,128)S(1)} custom-call(f32[1024,1024]{1,0:T(8,128)S(1)} %bitcast.5, f32[1024,512]{1,0:T(8,128)S(1)} %get-tuple-element.18.refs_1_), custom_call_target="tpu_custom_call" | custom-call | flops 3221225472 | bytes 6291456 | tf_op jit(solution)/shard_map/near_field/pallas_call | solution.py:33
  15.1 0.0 collective-permute-done.refs_1_
  15.1 0.0 collective-permute-done.1.refs_2_
  15.1 0.0 copy-start
  15.1 0.4 lift_leaves.1.refs_0_
  15.6 4.4 %collective-permute-start.5 = (f32[128,256]{1,0:T(8,128)S(1)}, f32[128,256]{1,0:T(8,128)S(1)}, u32[]{:S(2)}, u32[]{:S(2)}) collective-permute-start(f32[128,256]{1,0:T(8,128)S(1)} %lift_leaves.1.refs_0_), channel_id=1, source_target_pairs={{0,48},{4,52},{8,56},{12,60},{16,32},{20,36},{24,40},{28,44},{32,1... | collective-permute-start | bytes 393224 | tf_op jit(solution)/shard_map/ppermute | solution.py:152
  20.0 1.0 %collective-permute-start.4 = (f32[128,256]{1,0:T(8,128)S(1)}, f32[128,256]{1,0:T(8,128)S(1)}, u32[]{:S(2)}, u32[]{:S(2)}) collective-permute-start(f32[128,256]{1,0:T(8,128)S(1)} %lift_leaves.1.refs_0_), channel_id=1, source_target_pairs={{0,32},{4,36},{8,40},{12,44},{16,48},{20,52},{24,56},{28,60},{32,0... | collective-permute-start | bytes 393224 | tf_op jit(solution)/shard_map/ppermute | solution.py:152
  20.9 1.2 %collective-permute-start.3 = (f32[128,256]{1,0:T(8,128)S(1)}, f32[128,256]{1,0:T(8,128)S(1)}, u32[]{:S(2)}, u32[]{:S(2)}) collective-permute-start(f32[128,256]{1,0:T(8,128)S(1)} %lift_leaves.1.refs_0_), channel_id=1, source_target_pairs={{0,16},{4,20},{8,24},{12,28},{16,0},{20,4},{24,8},{28,12},{32,48},... | collective-permute-start | bytes 393224 | tf_op jit(solution)/shard_map/ppermute | solution.py:152
  22.1 1.7 %couple_leaves.1 = (f32[128,256]{1,0:T(8,128)S(1)}, f32[128,256]{1,0:T(8,128)S(1)}, f32[128,256]{1,0:T(8,128)S(1)}, f32[128,256]{1,0:T(8,128)S(1)}) custom-call(f32[128,256]{1,0:T(8,128)S(1)} %get-tuple-element.19.refs_0_, f32[128,256]{1,0:T(8,128)S(1)} %collective-permute-done.refs_1_, f32[128,256]{1,0:T(8,128)S(1)} %collective-permute-done.1.refs_2_, ...), custom_call_target="tpu_custom_call" | custom-call | flops 603979776 | bytes 2883584 | tf_op jit(solution)/shard_map/couple_leaves/pallas_call | solution.py:33
  23.8 2.8 %collective-permute-done.5.refs_3_ = f32[128,256]{1,0:T(8,128)S(1)} collective-permute-done((f32[128,256]{1,0:T(8,128)S(1)}, f32[128,256]{1,0:T(8,128)S(1)}, u32[]{:S(2)}, u32[]{:S(2)}) %collective-permute-start.5) | collective-permute-done | bytes 131104 | tf_op jit(solution)/shard_map/ppermute | solution.py:152
  26.6 2.0 %collective-permute-done.4.refs_2_ = f32[128,256]{1,0:T(8,128)S(1)} collective-permute-done((f32[128,256]{1,0:T(8,128)S(1)}, f32[128,256]{1,0:T(8,128)S(1)}, u32[]{:S(2)}, u32[]{:S(2)}) %collective-permute-start.4) | collective-permute-done | bytes 131104 | tf_op jit(solution)/shard_map/ppermute | solution.py:152
  28.6 6.5 %collective-permute-done.3.refs_1_ = f32[128,256]{1,0:T(8,128)S(1)} collective-permute-done((f32[128,256]{1,0:T(8,128)S(1)}, f32[128,256]{1,0:T(8,128)S(1)}, u32[]{:S(2)}, u32[]{:S(2)}) %collective-permute-start.3) | collective-permute-done | bytes 131104 | tf_op jit(solution)/shard_map/ppermute | solution.py:152
  35.0 0.4 lift_nodes.1.refs_0_
  35.5 2.8 %collective-permute-start.8 = (f32[128,256]{1,0:T(8,128)S(1)}, f32[128,256]{1,0:T(8,128)S(1)}, u32[]{:S(2)}, u32[]{:S(2)}) collective-permute-start(f32[128,256]{1,0:T(8,128)S(1)} %lift_nodes.1.refs_0_), channel_id=1, source_target_pairs={{0,192},{4,196},{8,200},{12,204},{16,208},{20,212},{24,216},{28,22... | collective-permute-start | bytes 393224 | tf_op jit(solution)/shard_map/ppermute | solution.py:152
  38.3 0.3 collective-permute-start.7
  38.6 0.3 collective-permute-start.6
  39.0 0.6 couple_nodes.1.refs_6_
  39.5 4.3 %collective-permute-done.8.refs_3_ = f32[128,256]{1,0:T(8,128)S(1)} collective-permute-done((f32[128,256]{1,0:T(8,128)S(1)}, f32[128,256]{1,0:T(8,128)S(1)}, u32[]{:S(2)}, u32[]{:S(2)}) %collective-permute-start.8) | collective-permute-done | bytes 131104 | tf_op jit(solution)/shard_map/ppermute | solution.py:152
  43.8 0.3 collective-permute-done.7.refs_2_
  44.1 0.8 %collective-permute-done.6.refs_1_ = f32[128,256]{1,0:T(8,128)S(1)} collective-permute-done((f32[128,256]{1,0:T(8,128)S(1)}, f32[128,256]{1,0:T(8,128)S(1)}, u32[]{:S(2)}, u32[]{:S(2)}) %collective-permute-start.6) | collective-permute-done | bytes 131104 | tf_op jit(solution)/shard_map/ppermute | solution.py:152
  44.8 1.7 %descend.1 = (f32[128,256]{1,0:T(8,128)S(1)}, f32[128,256]{1,0:T(8,128)S(1)}, f32[128,256]{1,0:T(8,128)S(1)}, f32[128,256]{1,0:T(8,128)S(1)}) custom-call(f32[128,256]{1,0:T(8,128)S(1)} %lift_nodes.1.refs_0_, f32[128,256]{1,0:T(8,128)S(1)} %collective-permute-done.6.refs_1_, f32[128,256]{1,0:T(8,128)S(1)} %collective-permute-done.7.refs_2_, ...), custom_call_target="tpu_custom_call" | custom-call | flops 402653184 | bytes 5636096 | tf_op jit(solution)/shard_map/descend/pallas_call | solution.py:33
  46.6 2.2 %collective-permute-start.11 = (f32[128,256]{1,0:T(8,128)S(1)}, f32[128,256]{1,0:T(8,128)S(1)}, u32[]{:S(2)}, u32[]{:S(2)}) collective-permute-start(f32[128,256]{1,0:T(8,128)S(1)} %get-tuple-element.30), channel_id=1, source_target_pairs={{0,4},{4,0},{8,12},{12,8},{16,20},{20,16},{24,28},{28,24},{32,36},... | collective-permute-start | bytes 393224 | tf_op jit(solution)/shard_map/ppermute | solution.py:152
  48.8 1.7 %collective-permute-start.10 = (f32[128,256]{1,0:T(8,128)S(1)}, f32[128,256]{1,0:T(8,128)S(1)}, u32[]{:S(2)}, u32[]{:S(2)}) collective-permute-start(f32[128,256]{1,0:T(8,128)S(1)} %get-tuple-element.28), channel_id=1, source_target_pairs={{0,12},{4,8},{8,4},{12,0},{16,28},{20,24},{24,20},{28,16},{32,44},... | collective-permute-start | bytes 393224 | tf_op jit(solution)/shard_map/ppermute | solution.py:152
  50.5 1.5 %finish_own.1.rest_0_ = f32[1024,512]{1,0:T(8,128)} custom-call(f32[1024,512]{1,0:T(8,128)S(1)} %near_field.1.refs_5_.near, f32[1024,256]{1,0:T(8,128)S(1)} %bitcast.3, f32[128,256]{1,0:T(8,128)S(1)} %get-tuple-element.29.g0, f32[128,256]{1,0:T(8,128)S(1)} %collective-permute-done.11.g1), custom_call_target="tpu_custom_call" | custom-call | flops 402653184 | bytes 2097152 | tf_op jit(solution)/shard_map/finish_own/pallas_call | solution.py:230
  52.0 1.8 %collective-permute-done.9.g0 = f32[128,256]{1,0:T(8,128)S(1)} collective-permute-done((f32[128,256]{1,0:T(8,128)S(1)}, f32[128,256]{1,0:T(8,128)S(1)}, u32[]{:S(2)}, u32[]{:S(2)}) %collective-permute-start.9) | collective-permute-done | bytes 131104 | tf_op jit(solution)/shard_map/ppermute | solution.py:152
  53.9 3.0 %collective-permute-done.10.g1 = f32[128,256]{1,0:T(8,128)S(1)} collective-permute-done((f32[128,256]{1,0:T(8,128)S(1)}, f32[128,256]{1,0:T(8,128)S(1)}, u32[]{:S(2)}, u32[]{:S(2)}) %collective-permute-start.10) | collective-permute-done | bytes 131104 | tf_op jit(solution)/shard_map/ppermute | solution.py:152
  56.8 1.5 %finish_other.1 = f32[1024,512]{1,0:T(8,128)} custom-call(f32[1024,512]{1,0:T(8,128)S(1)} %near_field.1.refs_5_.near, f32[1024,256]{1,0:T(8,128)S(1)} %bitcast.4, f32[128,256]{1,0:T(8,128)S(1)} %collective-permute-done.9.g0, f32[128,256]{1,0:T(8,128)S(1)} %collective-permute-done.10.g1, f32[1024,512]{1,0:T(8,128)} %finish_own.1.rest_0_), custom_call_target="tpu_custom_call", output_to_operand_aliasing={{}: (4, {})} | custom-call | flops 402653184 | bytes 2097152 | tf_op jit(solution)/shard_map/finish_other/pallas_call | solution.py:230
  (9 shorter events, 0.0 us)
Async XLA Ops:
  3.4 11.7 %collective-permute-start = (f32[128,256]{1,0:T(8,128)S(1)}, f32[128,256]{1,0:T(8,128)S(1)}, u32[]{:S(2)}, u32[]{:S(2)}) collective-permute-start(f32[128,256]{1,0:T(8,128)S(1)} %get-tuple-element.20), channel_id=1, source_target_pairs={{0,4},{4,0},{8,12},{12,8},{16,20},{20,16},{24,28},{28,24},{32,36},... | collective-permute-start | bytes 393224 | tf_op jit(solution)/shard_map/ppermute | solution.py:152
  6.7 8.4 %collective-permute-start.1 = (f32[128,256]{1,0:T(8,128)S(1)}, f32[128,256]{1,0:T(8,128)S(1)}, u32[]{:S(2)}, u32[]{:S(2)}) collective-permute-start(f32[128,256]{1,0:T(8,128)S(1)} %get-tuple-element.21), channel_id=1, source_target_pairs={{0,8},{4,12},{8,0},{12,4},{16,24},{20,28},{24,16},{28,20},{32,40},... | collective-permute-start | bytes 393224 | tf_op jit(solution)/shard_map/ppermute | solution.py:152
  6.7 8.4 %collective-permute-start.2 = (f32[128,256]{1,0:T(8,128)S(1)}, f32[128,256]{1,0:T(8,128)S(1)}, u32[]{:S(2)}, u32[]{:S(2)}) collective-permute-start(f32[128,256]{1,0:T(8,128)S(1)} %get-tuple-element.22), channel_id=1, source_target_pairs={{0,12},{4,8},{8,4},{12,0},{16,28},{20,24},{24,20},{28,16},{32,44},... | collective-permute-start | bytes 393224 | tf_op jit(solution)/shard_map/ppermute | solution.py:152
  8.4 2.2 %copy-start.3 = (f32[1,1024,1024]{2,1,0:T(8,128)S(1)}, f32[1,1024,1024]{2,1,0:T(8,128)}, u32[]{:S(2)}) copy-start(f32[1,1024,1024]{2,1,0:T(8,128)} %param.7) | copy-start | bytes 12582916
  10.6 4.5 %copy-start.1 = (f32[2,4,256,256]{3,2,1,0:T(8,128)S(1)}, f32[2,4,256,256]{3,2,1,0:T(8,128)}, u32[]{:S(2)}) copy-start(f32[2,4,256,256]{3,2,1,0:T(8,128)} %refs_5_.1) | copy-start | bytes 6291460
  15.1 7.0 %copy-start = (f32[3,3,256,256]{3,2,1,0:T(8,128)S(1)}, f32[3,3,256,256]{3,2,1,0:T(8,128)}, u32[]{:S(2)}) copy-start(f32[3,3,256,256]{3,2,1,0:T(8,128)} %refs_4_.9) | copy-start | bytes 7077892
  15.6 11.0 %collective-permute-start.5 = (f32[128,256]{1,0:T(8,128)S(1)}, f32[128,256]{1,0:T(8,128)S(1)}, u32[]{:S(2)}, u32[]{:S(2)}) collective-permute-start(f32[128,256]{1,0:T(8,128)S(1)} %lift_leaves.1.refs_0_), channel_id=1, source_target_pairs={{0,48},{4,52},{8,56},{12,60},{16,32},{20,36},{24,40},{28,44},{32,1... | collective-permute-start | bytes 393224 | tf_op jit(solution)/shard_map/ppermute | solution.py:152
  20.0 8.6 %collective-permute-start.4 = (f32[128,256]{1,0:T(8,128)S(1)}, f32[128,256]{1,0:T(8,128)S(1)}, u32[]{:S(2)}, u32[]{:S(2)}) collective-permute-start(f32[128,256]{1,0:T(8,128)S(1)} %lift_leaves.1.refs_0_), channel_id=1, source_target_pairs={{0,32},{4,36},{8,40},{12,44},{16,48},{20,52},{24,56},{28,60},{32,0... | collective-permute-start | bytes 393224 | tf_op jit(solution)/shard_map/ppermute | solution.py:152
  20.9 14.1 %collective-permute-start.3 = (f32[128,256]{1,0:T(8,128)S(1)}, f32[128,256]{1,0:T(8,128)S(1)}, u32[]{:S(2)}, u32[]{:S(2)}) collective-permute-start(f32[128,256]{1,0:T(8,128)S(1)} %lift_leaves.1.refs_0_), channel_id=1, source_target_pairs={{0,16},{4,20},{8,24},{12,28},{16,0},{20,4},{24,8},{28,12},{32,48},... | collective-permute-start | bytes 393224 | tf_op jit(solution)/shard_map/ppermute | solution.py:152
  35.5 8.3 %collective-permute-start.8 = (f32[128,256]{1,0:T(8,128)S(1)}, f32[128,256]{1,0:T(8,128)S(1)}, u32[]{:S(2)}, u32[]{:S(2)}) collective-permute-start(f32[128,256]{1,0:T(8,128)S(1)} %lift_nodes.1.refs_0_), channel_id=1, source_target_pairs={{0,192},{4,196},{8,200},{12,204},{16,208},{20,212},{24,216},{28,22... | collective-permute-start | bytes 393224 | tf_op jit(solution)/shard_map/ppermute | solution.py:152
  38.3 5.8 %collective-permute-start.7 = (f32[128,256]{1,0:T(8,128)S(1)}, f32[128,256]{1,0:T(8,128)S(1)}, u32[]{:S(2)}, u32[]{:S(2)}) collective-permute-start(f32[128,256]{1,0:T(8,128)S(1)} %lift_nodes.1.refs_0_), channel_id=1, source_target_pairs={{0,128},{4,132},{8,136},{12,140},{16,144},{20,148},{24,152},{28,15... | collective-permute-start | bytes 393224 | tf_op jit(solution)/shard_map/ppermute | solution.py:152
  38.6 6.2 %collective-permute-start.6 = (f32[128,256]{1,0:T(8,128)S(1)}, f32[128,256]{1,0:T(8,128)S(1)}, u32[]{:S(2)}, u32[]{:S(2)}) collective-permute-start(f32[128,256]{1,0:T(8,128)S(1)} %lift_nodes.1.refs_0_), channel_id=1, source_target_pairs={{0,64},{4,68},{8,72},{12,76},{16,80},{20,84},{24,88},{28,92},{32,9... | collective-permute-start | bytes 393224 | tf_op jit(solution)/shard_map/ppermute | solution.py:152
  39.5 11.0 %copy-start.2 = (f32[1,1024,256]{2,1,0:T(8,128)S(1)}, f32[1,1024,256]{2,1,0:T(8,128)}, u32[]{:S(2)}) copy-start(f32[1,1024,256]{2,1,0:T(8,128)} %param.8) | copy-start | bytes 3145732
  46.6 3.9 %collective-permute-start.11 = (f32[128,256]{1,0:T(8,128)S(1)}, f32[128,256]{1,0:T(8,128)S(1)}, u32[]{:S(2)}, u32[]{:S(2)}) collective-permute-start(f32[128,256]{1,0:T(8,128)S(1)} %get-tuple-element.30), channel_id=1, source_target_pairs={{0,4},{4,0},{8,12},{12,8},{16,20},{20,16},{24,28},{28,24},{32,36},... | collective-permute-start | bytes 393224 | tf_op jit(solution)/shard_map/ppermute | solution.py:152
  48.8 5.1 %collective-permute-start.9 = (f32[128,256]{1,0:T(8,128)S(1)}, f32[128,256]{1,0:T(8,128)S(1)}, u32[]{:S(2)}, u32[]{:S(2)}) collective-permute-start(f32[128,256]{1,0:T(8,128)S(1)} %get-tuple-element.27), channel_id=1, source_target_pairs={{0,8},{4,12},{8,0},{12,4},{16,24},{20,28},{24,16},{28,20},{32,40},... | collective-permute-start | bytes 393224 | tf_op jit(solution)/shard_map/ppermute | solution.py:152
  48.8 8.0 %collective-permute-start.10 = (f32[128,256]{1,0:T(8,128)S(1)}, f32[128,256]{1,0:T(8,128)S(1)}, u32[]{:S(2)}, u32[]{:S(2)}) collective-permute-start(f32[128,256]{1,0:T(8,128)S(1)} %get-tuple-element.28), channel_id=1, source_target_pairs={{0,12},{4,8},{8,4},{12,0},{16,28},{20,24},{24,20},{28,16},{32,44},... | collective-permute-start | bytes 393224 | tf_op jit(solution)/shard_map/ppermute | solution.py:152

commit v3 on v2

v3 whole, which is shorter than its diff:
```python
import functools

import jax
import jax.numpy as jnp
from jax import lax
from jax.experimental import pallas as pl
from jax.experimental.pallas import tpu as pltpu
from jax.sharding import PartitionSpec as P


F32 = jnp.float32
HIGH = lax.Precision.HIGH
MIB = 1 << 20
VMEM = pl.BlockSpec(memory_space=pltpu.VMEM)
ANY = pl.BlockSpec(memory_space=pl.ANY)
CHUNKS = 4


def dot(a, b, ca, cb):
    return lax.dot_general(
        a, b, (((ca,), (cb,)), ((), ())), precision=HIGH, preferred_element_type=F32
    )


def in_vmem(arrays):
    return [pltpu.with_memory_space_constraint(x, pltpu.VMEM) for x in arrays]


def in_hbm(arrays):
    return [pltpu.with_memory_space_constraint(x, pltpu.HBM) for x in arrays]


def settings(flops, size, name):
    return dict(
        compiler_params=pltpu.CompilerParams(vmem_limit_bytes=24 * MIB),
        cost_estimate=pl.CostEstimate(flops=flops, bytes_accessed=4 * size, transcendentals=0),
        name=name,
    )


def run(body, ins, outs, name, flops, after=(), scratch=()):
    def kernel(*refs):
        body(*refs[: len(ins)], *refs[len(ins) + len(after) :])

    return pl.pallas_call(
        kernel,
        out_shape=[pltpu.VMEM(shape, F32) for shape in outs],
        in_specs=[VMEM] * len(ins) + [ANY] * len(after),
        out_specs=[VMEM] * len(outs),
        scratch_shapes=[pltpu.VMEM(shape, F32) for shape in scratch],
        **settings(flops, sum(x.size for x in ins), name),
    )(*in_vmem(ins), *after)


def place():
    leaf = lax.axis_index("leaf")
    return leaf // 16, leaf // 4 % 4, leaf % 4, leaf % 2


def span(index, count):
    return pl.ds(pl.multiple_of(index * count, count), count)


def pick(core, first, second):
    return jnp.where(core == 0, first[...], second[...])


def offset(source, target):
    return (source - target + 4) % 4 - 1


def far_coefficients(x, basis, o2, o3, held, basis_held, whole, sems, rest_sem):
    _, m, k, _ = place()
    users, wide = x.shape[0], x.shape[1] // 2
    chunk = users // CHUNKS
    far = 1 - (k ^ m) // 2
    columns = span(far, wide)
    copies = []
    for i in range(CHUNKS):
        at = pl.ds(i * chunk, chunk)
        pair = (
            pltpu.make_async_copy(basis.at[at], basis_held.at[at], sems.at[0, i]),
            pltpu.make_async_copy(x.at[at, columns], held.at[at, columns], sems.at[1, i]),
        )
        for copy in pair:
            copy.start()
        copies.append(pair)
    near_columns = span(1 - far, wide)
    rest = pltpu.make_async_copy(x.at[:, near_columns], held.at[:, near_columns], rest_sem)
    rest.start()
    for i, pair in enumerate(copies):
        at = pl.ds(i * chunk, chunk)
        for copy in pair:
            copy.wait()
        term = dot(held[at, columns], basis_held[at, :], 0, 0)
        whole[...] = term if i == 0 else whole[...] + term
    for j, out in ((2, o2), (3, o3)):
        out[...] = whole[span((k ^ m ^ j) % 2, wide // 2), :]
    rest.wait()


def own_coefficients(held, basis_held, o0, o1, whole):
    _, m, k, _ = place()
    wide = held.shape[1] // 2
    whole[...] = dot(held[:, span((k ^ m) // 2, wide)], basis_held[...], 0, 0)
    for j, out in ((0, o0), (1, o1)):
        out[...] = whole[span((k ^ m ^ j) % 2, wide // 2), :]


def near_field(dense, x, out, held, sems):
    chunk = dense.shape[0] // CHUNKS
    copies = []
    for i in range(CHUNKS):
        at = pl.ds(i * chunk, chunk)
        copy = pltpu.make_async_copy(dense.at[at], held.at[at], sems.at[i])
        copy.start()
        copies.append(copy)
    for i, copy in enumerate(copies):
        at = pl.ds(i * chunk, chunk)
        copy.wait()
        out[at, :] = dot(held[at, :], x[...], 1, 0)


def split_out(core, m, whole, a, rest):
    step = a.shape[0]
    a[...] = whole[span((m // 2 + 1 - core) % 2, step), :]
    rest[...] = whole[span((m // 2 + core) % 2, step), :]


def lift_leaves(c0, c1, c2, c3, transfers, a, rest, whole):
    _, m, k, core = place()
    whole[...] = (
        dot(c0[...], transfers[0, k], 1, 0)
        + dot(c1[...], transfers[0, k ^ 1], 1, 0)
        + dot(c2[...], transfers[0, k ^ 2], 1, 0)
        + dot(c3[...], transfers[0, k ^ 3], 1, 0)
    )
    split_out(core, m, whole, a, rest)


def couple_leaves(c0, c1, c2, c3, couplings, *fields):
    k = place()[2]
    parts = (c0, c1, c2, c3)
    for target, out in enumerate(fields):
        at = k ^ target
        out[...] = sum(
            dot(parts[target ^ d][...], couplings[0, offset(at ^ d, at)], 1, 1) for d in (1, 2, 3)
        )


def lift_nodes(rest, a, b, swapped_rest, swapped_a, swapped_b, transfers, out, parts):
    _, m, _, core = place()
    step = out.shape[0]
    blocks = (
        pick(core, rest, swapped_rest),
        pick(core, swapped_a, a),
        pick(core, a, swapped_a),
        pick(core, swapped_b, b),
    )
    total = None
    for j, block in enumerate(blocks):
        parts[pl.ds(j * step, step), :] = block
        term = dot(block, transfers[1, m ^ j], 1, 0)
        total = term if total is None else total + term
    out[...] = total


def couple_nodes(parts, couplings, a, rest):
    _, m, _, core = place()
    step = a.shape[0]
    for target, out in ((2 - core, a), (3 * core, rest)):
        at = m ^ target
        out[...] = sum(
            dot(parts[span(target ^ d, step), :], couplings[1, offset(at ^ d, at)], 1, 1)
            for d in (1, 2, 3)
        )


def top(a, b, swapped_a, swapped_b, couplings, transfers, field_a, field_rest, out_a, out_rest):
    r, m, _, core = place()
    blocks = (pick(core, swapped_a, a), pick(core, a, swapped_a), pick(core, swapped_b, b))
    g = sum(
        dot(block, couplings[2, offset(r ^ d, r)], 1, 1) for d, block in zip((1, 2, 3), blocks)
    )
    out_a[...] = field_a[...] + dot(g, transfers[1, m ^ (2 - core)], 1, 1)
    out_rest[...] = field_rest[...] + dot(g, transfers[1, m ^ (3 * core)], 1, 1)


def descend(rest, a, b, transfers, f0, f1, f2, f3, o0, o1, o2, o3, whole):
    _, m, k, core = place()
    step = a.shape[0]
    whole[span(m // 2, step), :] = pick(core, rest, a)
    whole[span(1 - m // 2, step), :] = pick(core, a, b)
    g = whole[...]
    for j, (field, out) in enumerate(((f0, o0), (f1, o1), (f2, o2), (f3, o3))):
        out[...] = field[...] + dot(g, transfers[0, k ^ j], 1, 1)


def finish(first, near, row_basis, *rest):
    out, block, whole, sems = rest[-4:]
    _, m, k, _ = place()
    wide, step = whole.shape[0], rest[0].shape[0]
    if wide == step:
        whole[...] = rest[0][...]
        columns = span(k ^ m ^ first, wide)
    else:
        for j in (0, 1):
            whole[span((k ^ m ^ j) % 2, step), :] = rest[j][...]
        columns = span((k ^ m ^ first) // 2, wide)
    chunk = out.shape[0] // CHUNKS
    copies = []
    for i in range(CHUNKS):
        at = pl.ds(i * chunk, chunk)
        block[at, :] = near[at, columns] + dot(row_basis[at, :], whole[...], 1, 1)
        copy = pltpu.make_async_copy(block.at[at], out.at[at, columns], sems.at[i])
        copy.start()
        copies.append(copy)
    for copy in copies:
        copy.wait()


def send(block, target):
    pairs = [(i, target(i, i % 2)) for i in range(lax.axis_size("leaf"))]
    return lax.ppermute(block, "leaf", [pair for pair in pairs if pair[1] is not None])


def swap(block, bits):
    return send(block, lambda i, core: i ^ bits)


def to_nodes(a, rest):
    got_a = send(a, lambda i, core: i ^ (4 if core else 10))
    return got_a, send(rest, lambda i, core: i ^ 14 if core else None)


def to_tops(block):
    got_a = send(block, lambda i, core: i ^ (16 if core else 32))
    return got_a, send(block, lambda i, core: i ^ 48 if core else None)


def to_core_0(block):
    return send(block, lambda i, core: i ^ 1 if core else None)


def to_core_1(block):
    return send(block, lambda i, core: None if core else i ^ 1)


def local(ratings, dense_blocks, row_basis, col_basis, transfers, couplings):
    users, columns = ratings.shape
    rank = col_basis.shape[2]
    quarter, slim = columns // 4, columns // 8
    unit = 2 * 3 * rank * rank
    dense, rbasis, cbasis = dense_blocks[0], row_basis[0], col_basis[0]

    c2, c3, held, basis_held = pl.pallas_call(
        far_coefficients,
        out_shape=[
            pltpu.VMEM(shape, F32)
            for shape in ((quarter, rank), (quarter, rank), (users, columns), (users, rank))
        ],
        in_specs=[ANY] * 2,
        out_specs=[VMEM] * 4,
        scratch_shapes=[
            pltpu.VMEM((columns // 2, rank), F32),
            pltpu.SemaphoreType.DMA((2, CHUNKS)),
            pltpu.SemaphoreType.DMA,
        ],
        **settings(3 * users * columns * rank, users * columns, "far_coefficients"),
    )(*in_hbm([ratings, cbasis]))
    c2, c3 = swap(c2, 2), swap(c3, 3)
    c0, c1 = run(
        own_coefficients,
        [held, basis_held],
        [(quarter, rank)] * 2,
        "own_coefficients",
        3 * users * columns * rank,
        scratch=[(columns // 2, rank)],
    )
    c1 = swap(c1, 1)
    near = pl.pallas_call(
        near_field,
        out_shape=pltpu.VMEM((users, columns), F32),
        in_specs=[ANY, VMEM],
        out_specs=VMEM,
        scratch_shapes=[pltpu.VMEM((users, users), F32), pltpu.SemaphoreType.DMA((CHUNKS,))],
        **settings(6 * users * users * columns, users * users, "near_field"),
    )(*in_hbm([dense]), *in_vmem([held]))
    coef = [c0, c1, c2, c3]
    a, rest = run(
        lift_leaves,
        [*coef, transfers],
        [(slim, rank)] * 2,
        "lift_leaves",
        unit * columns,
        after=[near],
        scratch=[(quarter, rank)],
    )
    got_a, got_b = to_nodes(a, rest)
    swapped_rest = to_core_1(rest)
    leaf_fields = run(
        couple_leaves, [*coef, couplings], [(quarter, rank)] * 4, "couple_leaves", unit * 3 * columns
    )
    swapped_a, swapped_b = swap(got_a, 1), to_core_0(got_b)
    crown, parts = run(
        lift_nodes,
        [rest, got_a, got_b, swapped_rest, swapped_a, swapped_b, transfers],
        [(slim, rank), (4 * slim, rank)],
        "lift_nodes",
        unit * 4 * slim,
    )
    got_a, got_b = to_tops(crown)
    node_fields = run(
        couple_nodes, [parts, couplings], [(slim, rank)] * 2, "couple_nodes", unit * 6 * slim
    )
    a, rest = run(
        top,
        [got_a, got_b, swap(got_a, 1), to_core_0(got_b), couplings, transfers, *node_fields],
        [(slim, rank)] * 2,
        "top",
        unit * 5 * slim,
    )
    got_a, got_b = to_nodes(a, rest)

    g0, g1, g2, g3 = run(
        descend,
        [rest, got_a, got_b, transfers, *leaf_fields],
        [(quarter, rank)] * 4,
        "descend",
        unit * columns,
        scratch=[(quarter, rank)],
    )
    g2, g3, g1 = swap(g2, 2), swap(g3, 3), swap(g1, 1)

    def write(first, pieces, out):
        wide = len(pieces) * quarter
        return pl.pallas_call(
            functools.partial(finish, first),
            out_shape=pltpu.HBM((users, columns), F32),
            in_specs=[VMEM] * (2 + len(pieces)) + [ANY] * len(out),
            out_specs=ANY,
            scratch_shapes=[
                pltpu.VMEM((users, wide), F32),
                pltpu.VMEM((wide, rank), F32),
                pltpu.SemaphoreType.DMA((CHUNKS,)),
            ],
            input_output_aliases={2 + len(pieces): 0} if out else {},
            **settings(6 * users * rank * wide, users * wide, "finish_%d" % first),
        )(*in_vmem([near, rbasis, *pieces]), *out)

    out = write(0, [g0, g1], [])
    out = write(2, [g2], [out])
    return write(3, [g3], [out])


def solution(mesh):
    placed = (
        P("leaf", "col"),
        P("leaf", None, None),
        P("leaf", None, None),
        P("leaf", None, None),
        P(),
        P(),
    )
    return jax.shard_map(
        local, mesh=mesh, in_specs=placed, out_specs=P("leaf", "col"), check_vma=False
    )
```

time: 58.5 us -> 58.2 us (level)
  waiting for transfers between devices: 21.3 us -> 7.87 us
  starting transfers between devices: 19 us -> 31.3 us
  Pallas kernels: 15.7 us -> 18.4 us
  local copies, waits for them, and re-layouts: 2.2 us -> 0.02 us
    ppermute x12 -> x17, waiting for transfers between devices: 21.3 us -> 7.87 us  [send(): lax.ppermute(block, 'leaf', [pair for pair in pairs if pair[1] is not None])]
    ppermute x12 -> x17, starting transfers between devices: 19 us -> 31.3 us  [send(): lax.ppermute(block, 'leaf', [pair for pair in pairs if pair[1] is not None])]
    pallas_call x3 -> x5, Pallas kernels: 6.39 us -> 12.3 us  [the longest x1 5.8 us: local(): pl.pallas_call(near_field, out_shape=pltpu.VMEM((users, columns), F32), i...]
    pallas_call x6 -> x7, Pallas kernels: 9.31 us -> 6.04 us  [run(): pl.pallas_call(kernel, out_shape=[pltpu.VMEM(shape, F32) for shape in out...]
    unnamed x8 -> x6, local copies, waits for them, and re-layouts: 2.2 us -> 0.02 us
  transfers between devices with their start and end apart: 12 -> 17, of which waited for: 8 -> 7; matrix products, arithmetic and copies ran while one was open for 0% -> 0% of each run, Pallas kernels for 14% -> 19%
where the time goes in v3:
time: 58.2 us; the launch traced here: 57.9 us
  starting transfers between devices  31.3 us (54%)
  Pallas kernels  18.4 us (32%)
  waiting for transfers between devices  7.87 us (14%)
    ppermute x17, starting transfers between devices, send(): lax.ppermute(block, 'leaf', [pair for pair in pairs if pair[1] is not None])  31.3 us
    ppermute x17, waiting for transfers between devices, send(): lax.ppermute(block, 'leaf', [pair for pair in pairs if pair[1] is not None])  7.87 us
    pallas_call x7, Pallas kernels, run(): pl.pallas_call(kernel, out_shape=[pltpu.VMEM(shape, F32) for shape in out...  6.04 us
    pallas_call x1, Pallas kernels, local(): pl.pallas_call(near_field, out_shape=pltpu.VMEM((users, columns), F32), i...  5.8 us
    pallas_call x3, Pallas kernels, write(): pl.pallas_call(functools.partial(finish, first), out_shape=pltpu.HBM((use...  4.05 us
    pallas_call x1, Pallas kernels, local(): pl.pallas_call(far_coefficients, out_shape=[pltpu.VMEM(shape, F32) for sh...  2.49 us
  transfers between devices with their start and end apart: 17, of which 7 were waited for; matrix products, arithmetic and copies ran while one was open for 0% of the time, Pallas kernels for 19%

profile of v3, /device:TPU:1, one launch (start us, length us, event | category | flops | bytes accessed | tf_op | source)
XLA Modules:
  0.0 57.9 jit_solution(4589201927834410835)
XLA Ops:
  0.0 2.5 %far_coefficients.1 = (f32[128,256]{1,0:T(8,128)S(1)}, f32[128,256]{1,0:T(8,128)S(1)}, f32[1024,512]{1,0:T(8,128)S(1)}, f32[1024,256]{1,0:T(8,128)S(1)}) custom-call(f32[1024,512]{1,0:T(8,128)} %x.1, f32[1024,256]{1,0:T(8,128)} %bitcast.6), custom_call_target="tpu_custom_call" | custom-call | flops 402653184 | bytes 2097152 | tf_op jit(solution)/shard_map/far_coefficients/pallas_call | solution.py:256
  2.5 0.8 %own_coefficients.1 = (f32[128,256]{1,0:T(8,128)S(1)}, f32[128,256]{1,0:T(8,128)S(1)}) custom-call(f32[1024,512]{1,0:T(8,128)S(1)} %get-tuple-element.27.x.refs_0_, f32[1024,256]{1,0:T(8,128)S(1)} %get-tuple-element.28.refs_1_), custom_call_target="tpu_custom_call" | custom-call | flops 402653184 | bytes 3145728 | tf_op jit(solution)/shard_map/own_coefficients/pallas_call | solution.py:45
  3.3 3.3 %collective-permute-start = (f32[128,256]{1,0:T(8,128)S(1)}, f32[128,256]{1,0:T(8,128)S(1)}, u32[]{:S(2)}, u32[]{:S(2)}) collective-permute-start(f32[128,256]{1,0:T(8,128)S(1)} %get-tuple-element.30), channel_id=1, source_target_pairs={{0,4},{4,0},{8,12},{12,8},{16,20},{20,16},{24,28},{28,24},{32,36},... | collective-permute-start | bytes 393224 | tf_op jit(solution)/shard_map/ppermute | solution.py:224
  6.7 1.7 %collective-permute-start.2 = (f32[128,256]{1,0:T(8,128)S(1)}, f32[128,256]{1,0:T(8,128)S(1)}, u32[]{:S(2)}, u32[]{:S(2)}) collective-permute-start(f32[128,256]{1,0:T(8,128)S(1)} %get-tuple-element.32), channel_id=1, source_target_pairs={{0,12},{4,8},{8,4},{12,0},{16,28},{20,24},{24,20},{28,16},{32,44},... | collective-permute-start | bytes 393224 | tf_op jit(solution)/shard_map/ppermute | solution.py:224
  8.4 5.8 %near_field.1.refs_5_.near = f32[1024,512]{1,0:T(8,128)S(1)} custom-call(f32[1024,1024]{1,0:T(8,128)} %bitcast.7, f32[1024,512]{1,0:T(8,128)S(1)} %get-tuple-element.27.x.refs_0_), custom_call_target="tpu_custom_call" | custom-call | flops 3221225472 | bytes 4194304 | tf_op jit(solution)/shard_map/near_field/pallas_call | solution.py:281
  14.2 0.5 collective-permute-done.2.refs_3_
  14.7 0.4 lift_leaves.1
  15.2 1.5 %collective-permute-start.3 = (f32[64,256]{1,0:T(8,128)S(1)}, f32[64,256]{1,0:T(8,128)S(1)}, u32[]{:S(2)}, u32[]{:S(2)}) collective-permute-start(f32[64,256]{1,0:T(8,128)S(1)} %get-tuple-element.34), channel_id=1, source_target_pairs={{0,40},{4,20},{8,32},{12,28},{16,56},{20,4},{24,48},{28,12},{32,8}... | collective-permute-start | bytes 196616 | tf_op jit(solution)/shard_map/ppermute | solution.py:224
  16.6 5.5 %collective-permute-start.4 = (f32[64,256]{1,0:T(8,128)S(1)}, f32[64,256]{1,0:T(8,128)S(1)}, u32[]{:S(2)}, u32[]{:S(2)}) collective-permute-start(f32[64,256]{1,0:T(8,128)S(1)} %get-tuple-element.33.refs_0_), channel_id=1, source_target_pairs={{4,60},{12,52},{20,44},{28,36},{36,28},{44,20},{52,12},{60,4},{68,... | collective-permute-start | bytes 196616 | tf_op jit(solution)/shard_map/ppermute | solution.py:224
  22.2 1.3 %collective-permute-start.5 = (f32[64,256]{1,0:T(8,128)S(1)}, f32[64,256]{1,0:T(8,128)S(1)}, u32[]{:S(2)}, u32[]{:S(2)}) collective-permute-start(f32[64,256]{1,0:T(8,128)S(1)} %get-tuple-element.33.refs_0_), channel_id=1, source_target_pairs={{0,4},{8,12},{16,20},{24,28},{32,36},{40,44},{48,52},{56,60},{64,6... | collective-permute-start | bytes 196616 | tf_op jit(solution)/shard_map/ppermute | solution.py:224
  23.5 1.2 %collective-permute-start.6 = (f32[64,256]{1,0:T(8,128)S(1)}, f32[64,256]{1,0:T(8,128)S(1)}, u32[]{:S(2)}, u32[]{:S(2)}) collective-permute-start(f32[64,256]{1,0:T(8,128)S(1)} %collective-permute-done.3.refs_1_), channel_id=1, source_target_pairs={{0,4},{4,0},{8,12},{12,8},{16,20},{20,16},{24,28},{28,24},{32,36},... | collective-permute-start | bytes 196616 | tf_op jit(solution)/shard_map/ppermute | solution.py:224
  24.7 1.9 %collective-permute-start.7 = (f32[64,256]{1,0:T(8,128)S(1)}, f32[64,256]{1,0:T(8,128)S(1)}, u32[]{:S(2)}, u32[]{:S(2)}) collective-permute-start(f32[64,256]{1,0:T(8,128)S(1)} %collective-permute-done.4.refs_2_), channel_id=1, source_target_pairs={{4,0},{12,8},{20,16},{28,24},{36,32},{44,40},{52,48},{60,56},{68,6... | collective-permute-start | bytes 196616 | tf_op jit(solution)/shard_map/ppermute | solution.py:224
  26.6 0.9 %collective-permute-done.7.refs_5_ = f32[64,256]{1,0:T(8,128)S(1)} collective-permute-done((f32[64,256]{1,0:T(8,128)S(1)}, f32[64,256]{1,0:T(8,128)S(1)}, u32[]{:S(2)}, u32[]{:S(2)}) %collective-permute-start.7) | collective-permute-done | bytes 65568 | tf_op jit(solution)/shard_map/ppermute | solution.py:224
  27.5 0.4 lift_nodes.1
  27.9 4.6 %collective-permute-start.9 = (f32[64,256]{1,0:T(8,128)S(1)}, f32[64,256]{1,0:T(8,128)S(1)}, u32[]{:S(2)}, u32[]{:S(2)}) collective-permute-start(f32[64,256]{1,0:T(8,128)S(1)} %get-tuple-element.35), channel_id=1, source_target_pairs={{4,196},{12,204},{20,212},{28,220},{36,228},{44,236},{52,244},{60,... | collective-permute-start | bytes 196616 | tf_op jit(solution)/shard_map/ppermute | solution.py:224
  32.7 2.1 %collective-permute-done.9.refs_1_ = f32[64,256]{1,0:T(8,128)S(1)} collective-permute-done((f32[64,256]{1,0:T(8,128)S(1)}, f32[64,256]{1,0:T(8,128)S(1)}, u32[]{:S(2)}, u32[]{:S(2)}) %collective-permute-start.9) | collective-permute-done | bytes 65568 | tf_op jit(solution)/shard_map/ppermute | solution.py:224
  34.8 1.3 %collective-permute-start.11 = (f32[64,256]{1,0:T(8,128)S(1)}, f32[64,256]{1,0:T(8,128)S(1)}, u32[]{:S(2)}, u32[]{:S(2)}) collective-permute-start(f32[64,256]{1,0:T(8,128)S(1)} %collective-permute-done.9.refs_1_), channel_id=1, source_target_pairs={{4,0},{12,8},{20,16},{28,24},{36,32},{44,40},{52,48},{60,56},{68,6... | collective-permute-start | bytes 196616 | tf_op jit(solution)/shard_map/ppermute | solution.py:224
  36.2 0.9 %couple_nodes.1 = (f32[64,256]{1,0:T(8,128)S(1)}, f32[64,256]{1,0:T(8,128)S(1)}) custom-call(f32[256,256]{1,0:T(8,128)S(1)} %get-tuple-element.36.refs_0_, f32[3,3,256,256]{3,2,1,0:T(8,128)S(1)} %copy-done.1), custom_call_target="tpu_custom_call" | custom-call | flops 150994944 | bytes 2621440 | tf_op jit(solution)/shard_map/couple_nodes/pallas_call | solution.py:45
  37.1 0.3 collective-permute-done.10.refs_2_
  37.5 1.1 %top.1 = (f32[64,256]{1,0:T(8,128)S(1)}, f32[64,256]{1,0:T(8,128)S(1)}) custom-call(f32[64,256]{1,0:T(8,128)S(1)} %collective-permute-done.8.refs_0_, f32[64,256]{1,0:T(8,128)S(1)} %collective-permute-done.9.refs_1_, f32[64,256]{1,0:T(8,128)S(1)} %collective-permute-done.10.refs_2_, f32[64,256]{1,0:T(8,128)S(1)} %collective-permute-done.11.refs_3_, ...), custom_call_target="tpu_custom_call" | custom-call | flops 125829120 | bytes 4849664 | tf_op jit(solution)/shard_map/top/pallas_call | solution.py:45
  38.6 2.4 %collective-permute-start.12 = (f32[64,256]{1,0:T(8,128)S(1)}, f32[64,256]{1,0:T(8,128)S(1)}, u32[]{:S(2)}, u32[]{:S(2)}) collective-permute-start(f32[64,256]{1,0:T(8,128)S(1)} %get-tuple-element.40), channel_id=1, source_target_pairs={{0,40},{4,20},{8,32},{12,28},{16,56},{20,4},{24,48},{28,12},{32,8}... | collective-permute-start | bytes 196616 | tf_op jit(solution)/shard_map/ppermute | solution.py:224
  41.0 3.9 %collective-permute-start.13 = (f32[64,256]{1,0:T(8,128)S(1)}, f32[64,256]{1,0:T(8,128)S(1)}, u32[]{:S(2)}, u32[]{:S(2)}) collective-permute-start(f32[64,256]{1,0:T(8,128)S(1)} %get-tuple-element.39.refs_0_), channel_id=1, source_target_pairs={{4,60},{12,52},{20,44},{28,36},{36,28},{44,20},{52,12},{60,4},{68,... | collective-permute-start | bytes 196616 | tf_op jit(solution)/shard_map/ppermute | solution.py:224
  44.9 1.7 %couple_leaves.1 = (f32[128,256]{1,0:T(8,128)S(1)}, f32[128,256]{1,0:T(8,128)S(1)}, f32[128,256]{1,0:T(8,128)S(1)}, f32[128,256]{1,0:T(8,128)S(1)}) custom-call(f32[128,256]{1,0:T(8,128)S(1)} %get-tuple-element.29.refs_0_, f32[128,256]{1,0:T(8,128)S(1)} %collective-permute-done.refs_1_, f32[128,256]{1,0:T(8,128)S(1)} %collective-permute-done.1.refs_2_, ...), custom_call_target="tpu_custom_call" | custom-call | flops 603979776 | bytes 2883584 | tf_op jit(solution)/shard_map/couple_leaves/pallas_call | solution.py:45
  46.6 0.6 collective-permute-done.13.refs_2_
  47.2 0.7 %descend.1 = (f32[128,256]{1,0:T(8,128)S(1)}, f32[128,256]{1,0:T(8,128)S(1)}, f32[128,256]{1,0:T(8,128)S(1)}, f32[128,256]{1,0:T(8,128)S(1)}) custom-call(f32[64,256]{1,0:T(8,128)S(1)} %get-tuple-element.39.refs_0_, f32[64,256]{1,0:T(8,128)S(1)} %collective-permute-done.12.refs_1_, f32[64,256]{1,0:T(8,128)S(1)} %collective-permute-done.13.refs_2_, ...), custom_call_target="tpu_custom_call" | custom-call | flops 201326592 | bytes 2818048 | tf_op jit(solution)/shard_map/descend/pallas_call | solution.py:45
  48.0 2.0 %collective-permute-start.15 = (f32[128,256]{1,0:T(8,128)S(1)}, f32[128,256]{1,0:T(8,128)S(1)}, u32[]{:S(2)}, u32[]{:S(2)}) collective-permute-start(f32[128,256]{1,0:T(8,128)S(1)} %get-tuple-element.46), channel_id=1, source_target_pairs={{0,8},{4,12},{8,0},{12,4},{16,24},{20,28},{24,16},{28,20},{32,40},... | collective-permute-start | bytes 393224 | tf_op jit(solution)/shard_map/ppermute | solution.py:224
  49.9 0.3 collective-permute-start.14
  50.3 1.5 %finish_0.1.rest_1_ = f32[1024,512]{1,0:T(8,128)} custom-call(f32[1024,512]{1,0:T(8,128)S(1)} %near_field.1.refs_5_.near, f32[1024,256]{1,0:T(8,128)S(1)} %bitcast.3, f32[128,256]{1,0:T(8,128)S(1)} %get-tuple-element.47.rest_0_, f32[128,256]{1,0:T(8,128)S(1)} %collective-permute-done.16.rest_1_), custom_call_target="tpu_custom_call" | custom-call | flops 402653184 | bytes 1048576 | tf_op jit(solution)/shard_map/finish_0/pallas_call | solution.py:337
  51.8 1.7 %collective-permute-done.15.rest_0_ = f32[128,256]{1,0:T(8,128)S(1)} collective-permute-done((f32[128,256]{1,0:T(8,128)S(1)}, f32[128,256]{1,0:T(8,128)S(1)}, u32[]{:S(2)}, u32[]{:S(2)}) %collective-permute-start.15) | collective-permute-done | bytes 131104 | tf_op jit(solution)/shard_map/ppermute | solution.py:224
  53.5 1.3 %finish_2.1.rest_1_ = f32[1024,512]{1,0:T(8,128)} custom-call(f32[1024,512]{1,0:T(8,128)S(1)} %near_field.1.refs_5_.near, f32[1024,256]{1,0:T(8,128)S(1)} %bitcast.4, f32[128,256]{1,0:T(8,128)S(1)} %collective-permute-done.15.rest_0_, f32[1024,512]{1,0:T(8,128)} %finish_0.1.rest_1_), custom_call_target="tpu_custom_call", output_to_operand_aliasing={{}: (3, {})} | custom-call | flops 201326592 | bytes 524288 | tf_op jit(solution)/shard_map/finish_2/pallas_call | solution.py:337
  54.7 1.8 %collective-permute-done.14.rest_0_ = f32[128,256]{1,0:T(8,128)S(1)} collective-permute-done((f32[128,256]{1,0:T(8,128)S(1)}, f32[128,256]{1,0:T(8,128)S(1)}, u32[]{:S(2)}, u32[]{:S(2)}) %collective-permute-start.14) | collective-permute-done | bytes 131104 | tf_op jit(solution)/shard_map/ppermute | solution.py:224
  56.5 1.3 %finish_3.1 = f32[1024,512]{1,0:T(8,128)} custom-call(f32[1024,512]{1,0:T(8,128)S(1)} %near_field.1.refs_5_.near, f32[1024,256]{1,0:T(8,128)S(1)} %bitcast.5, f32[128,256]{1,0:T(8,128)S(1)} %collective-permute-done.14.rest_0_, f32[1024,512]{1,0:T(8,128)} %finish_2.1.rest_1_), custom_call_target="tpu_custom_call", output_to_operand_aliasing={{}: (3, {})} | custom-call | flops 201326592 | bytes 524288 | tf_op jit(solution)/shard_map/finish_3/pallas_call | solution.py:337
  (20 shorter events, 0.3 us)
Async XLA Ops:
  3.3 10.9 %collective-permute-start = (f32[128,256]{1,0:T(8,128)S(1)}, f32[128,256]{1,0:T(8,128)S(1)}, u32[]{:S(2)}, u32[]{:S(2)}) collective-permute-start(f32[128,256]{1,0:T(8,128)S(1)} %get-tuple-element.30), channel_id=1, source_target_pairs={{0,4},{4,0},{8,12},{12,8},{16,20},{20,16},{24,28},{28,24},{32,36},... | collective-permute-start | bytes 393224 | tf_op jit(solution)/shard_map/ppermute | solution.py:224
  6.7 7.6 %collective-permute-start.1 = (f32[128,256]{1,0:T(8,128)S(1)}, f32[128,256]{1,0:T(8,128)S(1)}, u32[]{:S(2)}, u32[]{:S(2)}) collective-permute-start(f32[128,256]{1,0:T(8,128)S(1)} %get-tuple-element.31), channel_id=1, source_target_pairs={{0,8},{4,12},{8,0},{12,4},{16,24},{20,28},{24,16},{28,20},{32,40},... | collective-permute-start | bytes 393224 | tf_op jit(solution)/shard_map/ppermute | solution.py:224
  6.7 8.0 %collective-permute-start.2 = (f32[128,256]{1,0:T(8,128)S(1)}, f32[128,256]{1,0:T(8,128)S(1)}, u32[]{:S(2)}, u32[]{:S(2)}) collective-permute-start(f32[128,256]{1,0:T(8,128)S(1)} %get-tuple-element.32), channel_id=1, source_target_pairs={{0,12},{4,8},{8,4},{12,0},{16,28},{20,24},{24,20},{28,16},{32,44},... | collective-permute-start | bytes 393224 | tf_op jit(solution)/shard_map/ppermute | solution.py:224
  8.4 6.3 %copy-start = (f32[2,4,256,256]{3,2,1,0:T(8,128)S(1)}, f32[2,4,256,256]{3,2,1,0:T(8,128)}, u32[]{:S(2)}) copy-start(f32[2,4,256,256]{3,2,1,0:T(8,128)} %refs_3_.1) | copy-start | bytes 6291460
  15.1 21.1 %copy-start.1 = (f32[3,3,256,256]{3,2,1,0:T(8,128)S(1)}, f32[3,3,256,256]{3,2,1,0:T(8,128)}, u32[]{:S(2)}) copy-start(f32[3,3,256,256]{3,2,1,0:T(8,128)} %refs_4_.5) | copy-start | bytes 7077892
  15.2 8.3 %collective-permute-start.3 = (f32[64,256]{1,0:T(8,128)S(1)}, f32[64,256]{1,0:T(8,128)S(1)}, u32[]{:S(2)}, u32[]{:S(2)}) collective-permute-start(f32[64,256]{1,0:T(8,128)S(1)} %get-tuple-element.34), channel_id=1, source_target_pairs={{0,40},{4,20},{8,32},{12,28},{16,56},{20,4},{24,48},{28,12},{32,8}... | collective-permute-start | bytes 196616 | tf_op jit(solution)/shard_map/ppermute | solution.py:224
  16.6 8.0 %collective-permute-start.4 = (f32[64,256]{1,0:T(8,128)S(1)}, f32[64,256]{1,0:T(8,128)S(1)}, u32[]{:S(2)}, u32[]{:S(2)}) collective-permute-start(f32[64,256]{1,0:T(8,128)S(1)} %get-tuple-element.33.refs_0_), channel_id=1, source_target_pairs={{4,60},{12,52},{20,44},{28,36},{36,28},{44,20},{52,12},{60,4},{68,... | collective-permute-start | bytes 196616 | tf_op jit(solution)/shard_map/ppermute | solution.py:224
  22.2 4.5 %collective-permute-start.5 = (f32[64,256]{1,0:T(8,128)S(1)}, f32[64,256]{1,0:T(8,128)S(1)}, u32[]{:S(2)}, u32[]{:S(2)}) collective-permute-start(f32[64,256]{1,0:T(8,128)S(1)} %get-tuple-element.33.refs_0_), channel_id=1, source_target_pairs={{0,4},{8,12},{16,20},{24,28},{32,36},{40,44},{48,52},{56,60},{64,6... | collective-permute-start | bytes 196616 | tf_op jit(solution)/shard_map/ppermute | solution.py:224
  23.5 3.2 %collective-permute-start.6 = (f32[64,256]{1,0:T(8,128)S(1)}, f32[64,256]{1,0:T(8,128)S(1)}, u32[]{:S(2)}, u32[]{:S(2)}) collective-permute-start(f32[64,256]{1,0:T(8,128)S(1)} %collective-permute-done.3.refs_1_), channel_id=1, source_target_pairs={{0,4},{4,0},{8,12},{12,8},{16,20},{20,16},{24,28},{28,24},{32,36},... | collective-permute-start | bytes 196616 | tf_op jit(solution)/shard_map/ppermute | solution.py:224
  24.7 2.8 %collective-permute-start.7 = (f32[64,256]{1,0:T(8,128)S(1)}, f32[64,256]{1,0:T(8,128)S(1)}, u32[]{:S(2)}, u32[]{:S(2)}) collective-permute-start(f32[64,256]{1,0:T(8,128)S(1)} %collective-permute-done.4.refs_2_), channel_id=1, source_target_pairs={{4,0},{12,8},{20,16},{28,24},{36,32},{44,40},{52,48},{60,56},{68,6... | collective-permute-start | bytes 196616 | tf_op jit(solution)/shard_map/ppermute | solution.py:224
  27.9 6.9 %collective-permute-start.9 = (f32[64,256]{1,0:T(8,128)S(1)}, f32[64,256]{1,0:T(8,128)S(1)}, u32[]{:S(2)}, u32[]{:S(2)}) collective-permute-start(f32[64,256]{1,0:T(8,128)S(1)} %get-tuple-element.35), channel_id=1, source_target_pairs={{4,196},{12,204},{20,212},{28,220},{36,228},{44,236},{52,244},{60,... | collective-permute-start | bytes 196616 | tf_op jit(solution)/shard_map/ppermute | solution.py:224
  32.6 3.5 %collective-permute-start.8 = (f32[64,256]{1,0:T(8,128)S(1)}, f32[64,256]{1,0:T(8,128)S(1)}, u32[]{:S(2)}, u32[]{:S(2)}) collective-permute-start(f32[64,256]{1,0:T(8,128)S(1)} %get-tuple-element.35), channel_id=1, source_target_pairs={{0,128},{4,68},{8,136},{12,76},{16,144},{20,84},{24,152},{28,92},{... | collective-permute-start | bytes 196616 | tf_op jit(solution)/shard_map/ppermute | solution.py:224
  34.8 2.3 %collective-permute-start.11 = (f32[64,256]{1,0:T(8,128)S(1)}, f32[64,256]{1,0:T(8,128)S(1)}, u32[]{:S(2)}, u32[]{:S(2)}) collective-permute-start(f32[64,256]{1,0:T(8,128)S(1)} %collective-permute-done.9.refs_1_), channel_id=1, source_target_pairs={{4,0},{12,8},{20,16},{28,24},{36,32},{44,40},{52,48},{60,56},{68,6... | collective-permute-start | bytes 196616 | tf_op jit(solution)/shard_map/ppermute | solution.py:224
  36.1 1.3 %collective-permute-start.10 = (f32[64,256]{1,0:T(8,128)S(1)}, f32[64,256]{1,0:T(8,128)S(1)}, u32[]{:S(2)}, u32[]{:S(2)}) collective-permute-start(f32[64,256]{1,0:T(8,128)S(1)} %collective-permute-done.8.refs_0_), channel_id=1, source_target_pairs={{0,4},{4,0},{8,12},{12,8},{16,20},{20,16},{24,28},{28,24},{32,36},... | collective-permute-start | bytes 196616 | tf_op jit(solution)/shard_map/ppermute | solution.py:224
  38.6 8.0 %collective-permute-start.12 = (f32[64,256]{1,0:T(8,128)S(1)}, f32[64,256]{1,0:T(8,128)S(1)}, u32[]{:S(2)}, u32[]{:S(2)}) collective-permute-start(f32[64,256]{1,0:T(8,128)S(1)} %get-tuple-element.40), channel_id=1, source_target_pairs={{0,40},{4,20},{8,32},{12,28},{16,56},{20,4},{24,48},{28,12},{32,8}... | collective-permute-start | bytes 196616 | tf_op jit(solution)/shard_map/ppermute | solution.py:224
  41.0 6.2 %collective-permute-start.13 = (f32[64,256]{1,0:T(8,128)S(1)}, f32[64,256]{1,0:T(8,128)S(1)}, u32[]{:S(2)}, u32[]{:S(2)}) collective-permute-start(f32[64,256]{1,0:T(8,128)S(1)} %get-tuple-element.39.refs_0_), channel_id=1, source_target_pairs={{4,60},{12,52},{20,44},{28,36},{36,28},{44,20},{52,12},{60,4},{68,... | collective-permute-start | bytes 196616 | tf_op jit(solution)/shard_map/ppermute | solution.py:224
  46.6 3.7 %copy-start.2 = (f32[1,1024,256]{2,1,0:T(8,128)S(1)}, f32[1,1024,256]{2,1,0:T(8,128)}, u32[]{:S(2)}) copy-start(f32[1,1024,256]{2,1,0:T(8,128)} %param.8) | copy-start | bytes 3145732
  47.9 2.4 %collective-permute-start.16 = (f32[128,256]{1,0:T(8,128)S(1)}, f32[128,256]{1,0:T(8,128)S(1)}, u32[]{:S(2)}, u32[]{:S(2)}) collective-permute-start(f32[128,256]{1,0:T(8,128)S(1)} %get-tuple-element.48), channel_id=1, source_target_pairs={{0,4},{4,0},{8,12},{12,8},{16,20},{20,16},{24,28},{28,24},{32,36},... | collective-permute-start | bytes 393224 | tf_op jit(solution)/shard_map/ppermute | solution.py:224
  48.0 5.5 %collective-permute-start.15 = (f32[128,256]{1,0:T(8,128)S(1)}, f32[128,256]{1,0:T(8,128)S(1)}, u32[]{:S(2)}, u32[]{:S(2)}) collective-permute-start(f32[128,256]{1,0:T(8,128)S(1)} %get-tuple-element.46), channel_id=1, source_target_pairs={{0,8},{4,12},{8,0},{12,4},{16,24},{20,28},{24,16},{28,20},{32,40},... | collective-permute-start | bytes 393224 | tf_op jit(solution)/shard_map/ppermute | solution.py:224
  49.9 6.6 %collective-permute-start.14 = (f32[128,256]{1,0:T(8,128)S(1)}, f32[128,256]{1,0:T(8,128)S(1)}, u32[]{:S(2)}, u32[]{:S(2)}) collective-permute-start(f32[128,256]{1,0:T(8,128)S(1)} %get-tuple-element.45), channel_id=1, source_target_pairs={{0,12},{4,8},{8,4},{12,0},{16,28},{20,24},{24,20},{28,16},{32,44},... | collective-permute-start | bytes 393224 | tf_op jit(solution)/shard_map/ppermute | solution.py:224

commit v4 on v3

--- a/solution.py
+++ b/solution.py
@@ -99,26 +99,34 @@
     rest.wait()
 
 
-def own_coefficients(held, basis_held, o0, o1, whole):
+def own_and_near(held, basis_held, dense, o0, o1, out, dense_rest, whole, dense_held, sems):
     _, m, k, _ = place()
     wide = held.shape[1] // 2
-    whole[...] = dot(held[:, span((k ^ m) // 2, wide)], basis_held[...], 0, 0)
-    for j, out in ((0, o0), (1, o1)):
-        out[...] = whole[span((k ^ m ^ j) % 2, wide // 2), :]
-
-
-def near_field(dense, x, out, held, sems):
-    chunk = dense.shape[0] // CHUNKS
+    users = dense.shape[0]
+    chunk = users // (2 * CHUNKS)
     copies = []
     for i in range(CHUNKS):
         at = pl.ds(i * chunk, chunk)
-        copy = pltpu.make_async_copy(dense.at[at], held.at[at], sems.at[i])
+        copies.append(pltpu.make_async_copy(dense.at[at], dense_held.at[at], sems.at[i]))
+    below = pl.ds(users // 2, users // 2)
+    copies.append(pltpu.make_async_copy(dense.at[below], dense_rest, sems.at[CHUNKS]))
+    for copy in copies:
         copy.start()
-        copies.append(copy)
-    for i, copy in enumerate(copies):
-        at = pl.ds(i * chunk, chunk)
-        copy.wait()
-        out[at, :] = dot(held[at, :], x[...], 1, 0)
+    whole[...] = dot(held[:, span((k ^ m) // 2, wide)], basis_held[...], 0, 0)
+    for j, piece in ((0, o0), (1, o1)):
+        piece[...] = whole[span((k ^ m ^ j) % 2, wide // 2), :]
+    for i in range(CHUNKS):
+        at = pl.ds(i * chunk, chunk)
+        copies[i].wait()
+        out[at, :] = dot(dense_held[at, :], held[...], 1, 0)
+    copies[CHUNKS].wait()
+
+
+def near_field(dense, x, out):
+    half = dense.shape[0] // 2
+    for i in range(2):
+        at = pl.ds(i * half, half)
+        out[at, :] = dot(dense[at, :], x[...], 1, 0)
 
 
 def split_out(core, m, whole, a, rest):
@@ -148,11 +156,11 @@
         )
 
 
-def lift_nodes(rest, a, b, swapped_rest, swapped_a, swapped_b, transfers, out, parts):
+def lift_nodes(a, b, swapped_a, swapped_b, transfers, out, parts):
     _, m, _, core = place()
     step = out.shape[0]
     blocks = (
-        pick(core, rest, swapped_rest),
+        pick(core, b, swapped_b),
         pick(core, swapped_a, a),
         pick(core, a, swapped_a),
         pick(core, swapped_b, b),
@@ -186,17 +194,17 @@
     out_rest[...] = field_rest[...] + dot(g, transfers[1, m ^ (3 * core)], 1, 1)
 
 
-def descend(rest, a, b, transfers, f0, f1, f2, f3, o0, o1, o2, o3, whole):
+def descend(a, b, transfers, f0, f1, f2, f3, o0, o1, o2, o3, whole):
     _, m, k, core = place()
     step = a.shape[0]
-    whole[span(m // 2, step), :] = pick(core, rest, a)
+    whole[span(m // 2, step), :] = pick(core, b, a)
     whole[span(1 - m // 2, step), :] = pick(core, a, b)
     g = whole[...]
     for j, (field, out) in enumerate(((f0, o0), (f1, o1), (f2, o2), (f3, o3))):
         out[...] = field[...] + dot(g, transfers[0, k ^ j], 1, 1)
 
 
-def finish(first, near, row_basis, *rest):
+def finish(first, near_above, near_below, row_basis, *rest):
     out, block, whole, sems = rest[-4:]
     _, m, k, _ = place()
     wide, step = whole.shape[0], rest[0].shape[0]
@@ -211,7 +219,9 @@
     copies = []
     for i in range(CHUNKS):
         at = pl.ds(i * chunk, chunk)
-        block[at, :] = near[at, columns] + dot(row_basis[at, :], whole[...], 1, 1)
+        near = near_above if 2 * i < CHUNKS else near_below
+        part = near[pl.ds(i * chunk % near.shape[0], chunk), columns]
+        block[at, :] = part + dot(row_basis[at, :], whole[...], 1, 1)
         copy = pltpu.make_async_copy(block.at[at], out.at[at, columns], sems.at[i])
         copy.start()
         copies.append(copy)
@@ -220,8 +230,9 @@
 
 
 def send(block, target):
-    pairs = [(i, target(i, i % 2)) for i in range(lax.axis_size("leaf"))]
-    return lax.ppermute(block, "leaf", [pair for pair in pairs if pair[1] is not None])
+    return lax.ppermute(
+        block, "leaf", [(i, target(i, i % 2)) for i in range(lax.axis_size("leaf"))]
+    )
 
 
 def swap(block, bits):
@@ -229,21 +240,15 @@
 
 
 def to_nodes(a, rest):
-    got_a = send(a, lambda i, core: i ^ (4 if core else 10))
-    return got_a, send(rest, lambda i, core: i ^ 14 if core else None)
+    return send(a, lambda i, core: i ^ (4 if core else 10)), send(
+        rest, lambda i, core: i ^ (14 if core else 0)
+    )
 
 
 def to_tops(block):
-    got_a = send(block, lambda i, core: i ^ (16 if core else 32))
-    return got_a, send(block, lambda i, core: i ^ 48 if core else None)
-
-
-def to_core_0(block):
-    return send(block, lambda i, core: i ^ 1 if core else None)
-
-
-def to_core_1(block):
-    return send(block, lambda i, core: None if core else i ^ 1)
+    return send(block, lambda i, core: i ^ (16 if core else 32)), send(
+        block, lambda i, core: i ^ (48 if core else 0)
+    )
 
 
 def local(ratings, dense_blocks, row_basis, col_basis, transfers, couplings):
@@ -269,23 +274,34 @@
         **settings(3 * users * columns * rank, users * columns, "far_coefficients"),
     )(*in_hbm([ratings, cbasis]))
     c2, c3 = swap(c2, 2), swap(c3, 3)
-    c0, c1 = run(
-        own_coefficients,
-        [held, basis_held],
-        [(quarter, rank)] * 2,
-        "own_coefficients",
-        3 * users * columns * rank,
-        scratch=[(columns // 2, rank)],
-    )
+    c0, c1, near_above, dense_rest = pl.pallas_call(
+        own_and_near,
+        out_shape=[
+            pltpu.VMEM(shape, F32)
+            for shape in (
+                (quarter, rank),
+                (quarter, rank),
+                (users // 2, columns),
+                (users // 2, users),
+            )
+        ],
+        in_specs=[VMEM, VMEM, ANY],
+        out_specs=[VMEM] * 4,
+        scratch_shapes=[
+            pltpu.VMEM((columns // 2, rank), F32),
+            pltpu.VMEM((users // 2, users), F32),
+            pltpu.SemaphoreType.DMA((CHUNKS + 1,)),
+        ],
+        **settings(3 * users * users * columns, users * users, "own_and_near"),
+    )(*in_vmem([held, basis_held]), *in_hbm([dense]))
     c1 = swap(c1, 1)
-    near = pl.pallas_call(
+    (near_below,) = run(
         near_field,
-        out_shape=pltpu.VMEM((users, columns), F32),
-        in_specs=[ANY, VMEM],
-        out_specs=VMEM,
-        scratch_shapes=[pltpu.VMEM((users, users), F32), pltpu.SemaphoreType.DMA((CHUNKS,))],
-        **settings(6 * users * users * columns, users * users, "near_field"),
-    )(*in_hbm([dense]), *in_vmem([held]))
+        [dense_rest, held],
+        [(users // 2, columns)],
+        "near_field",
+        3 * users * users * columns,
+    )
     coef = [c0, c1, c2, c3]
     a, rest = run(
         lift_leaves,
@@ -293,18 +309,16 @@
         [(slim, rank)] * 2,
         "lift_leaves",
         unit * columns,
-        after=[near],
         scratch=[(quarter, rank)],
     )
     got_a, got_b = to_nodes(a, rest)
-    swapped_rest = to_core_1(rest)
     leaf_fields = run(
         couple_leaves, [*coef, couplings], [(quarter, rank)] * 4, "couple_leaves", unit * 3 * columns
     )
-    swapped_a, swapped_b = swap(got_a, 1), to_core_0(got_b)
+    swapped_a, swapped_b = swap(got_a, 1), swap(got_b, 1)
     crown, parts = run(
         lift_nodes,
-        [rest, got_a, got_b, swapped_rest, swapped_a, swapped_b, transfers],
+        [got_a, got_b, swapped_a, swapped_b, transfers],
         [(slim, rank), (4 * slim, rank)],
         "lift_nodes",
         unit * 4 * slim,
@@ -315,7 +329,7 @@
     )
     a, rest = run(
         top,
-        [got_a, got_b, swap(got_a, 1), to_core_0(got_b), couplings, transfers, *node_fields],
+        [got_a, got_b, swap(got_a, 1), swap(got_b, 1), couplings, transfers, *node_fields],
         [(slim, rank)] * 2,
         "top",
         unit * 5 * slim,
@@ -324,7 +338,7 @@
 
     g0, g1, g2, g3 = run(
         descend,
-        [rest, got_a, got_b, transfers, *leaf_fields],
+        [got_a, got_b, transfers, *leaf_fields],
         [(quarter, rank)] * 4,
         "descend",
         unit * columns,
@@ -337,16 +351,16 @@
         return pl.pallas_call(
             functools.partial(finish, first),
             out_shape=pltpu.HBM((users, columns), F32),
-            in_specs=[VMEM] * (2 + len(pieces)) + [ANY] * len(out),
+            in_specs=[VMEM] * (3 + len(pieces)) + [ANY] * len(out),
             out_specs=ANY,
             scratch_shapes=[
                 pltpu.VMEM((users, wide), F32),
                 pltpu.VMEM((wide, rank), F32),
                 pltpu.SemaphoreType.DMA((CHUNKS,)),
             ],
-            input_output_aliases={2 + len(pieces): 0} if out else {},
+            input_output_aliases={3 + len(pieces): 0} if out else {},
             **settings(6 * users * rank * wide, users * wide, "finish_%d" % first),
-        )(*in_vmem([near, rbasis, *pieces]), *out)
+        )(*in_vmem([near_above, near_below, rbasis, *pieces]), *out)
 
     out = write(0, [g0, g1], [])
     out = write(2, [g2], [out])

time: 58.2 us -> 56.2 us (0.966)
  starting transfers between devices: 31.3 us -> 27.3 us
  waiting for transfers between devices: 7.87 us -> 9.9 us
    ppermute x17 -> x16, starting transfers between devices: 31.3 us -> 27.3 us  [send(): lax.ppermute(block, 'leaf', [(i, target(i, i % 2)) for i in range(lax.axi...]
    ppermute x17 -> x16, waiting for transfers between devices: 7.87 us -> 9.9 us  [send(): lax.ppermute(block, 'leaf', [(i, target(i, i % 2)) for i in range(lax.axi...]
    pallas_call x7, Pallas kernels: 6.04 us -> 7.24 us  [run(): pl.pallas_call(kernel, out_shape=[pltpu.VMEM(shape, F32) for shape in out...]
    pallas_call x1, Pallas kernels: 5.8 us -> 4.67 us  [local(): pl.pallas_call(own_and_near, out_shape=[pltpu.VMEM(shape, F32) for shape...]
  transfers between devices with their start and end apart: 17 -> 16, of which waited for: 7 -> 9; matrix products, arithmetic and copies ran while one was open for 0% -> 0% of each run, Pallas kernels for 19% -> 21%
where the time goes in v4:
time: 56.2 us; the launch traced here: 56 us
  starting transfers between devices  27.3 us (49%)
  Pallas kernels  18.5 us (33%)
  waiting for transfers between devices  9.9 us (18%)
    ppermute x16, starting transfers between devices, send(): lax.ppermute(block, 'leaf', [(i, target(i, i % 2)) for i in range(lax.axi...  27.3 us
    ppermute x16, waiting for transfers between devices, send(): lax.ppermute(block, 'leaf', [(i, target(i, i % 2)) for i in range(lax.axi...  9.9 us
    pallas_call x7, Pallas kernels, run(): pl.pallas_call(kernel, out_shape=[pltpu.VMEM(shape, F32) for shape in out...  7.24 us
    pallas_call x1, Pallas kernels, local(): pl.pallas_call(own_and_near, out_shape=[pltpu.VMEM(shape, F32) for shape...  4.67 us
    pallas_call x3, Pallas kernels, write(): pl.pallas_call(functools.partial(finish, first), out_shape=pltpu.HBM((use...  4.06 us
    pallas_call x1, Pallas kernels, local(): pl.pallas_call(far_coefficients, out_shape=[pltpu.VMEM(shape, F32) for sh...  2.49 us
  transfers between devices with their start and end apart: 16, of which 9 were waited for; matrix products, arithmetic and copies ran while one was open for 0% of the time, Pallas kernels for 21%

profile of v4, /device:TPU:1, one launch (start us, length us, event | category | flops | bytes accessed | tf_op | source)
XLA Modules:
  0.0 56.0 jit_solution(14509213095636323750)
XLA Ops:
  0.0 2.5 %far_coefficients.1 = (f32[128,256]{1,0:T(8,128)S(1)}, f32[128,256]{1,0:T(8,128)S(1)}, f32[1024,512]{1,0:T(8,128)S(1)}, f32[1024,256]{1,0:T(8,128)S(1)}) custom-call(f32[1024,512]{1,0:T(8,128)} %x.1, f32[1024,256]{1,0:T(8,128)} %bitcast.7), custom_call_target="tpu_custom_call" | custom-call | flops 402653184 | bytes 2097152 | tf_op jit(solution)/shard_map/far_coefficients/pallas_call | solution.py:261
  2.5 2.5 %collective-permute-start.1 = (f32[128,256]{1,0:T(8,128)S(1)}, f32[128,256]{1,0:T(8,128)S(1)}, u32[]{:S(2)}, u32[]{:S(2)}) collective-permute-start(f32[128,256]{1,0:T(8,128)S(1)} %get-tuple-element.35), channel_id=1, source_target_pairs={{0,8},{4,12},{8,0},{12,4},{16,24},{20,28},{24,16},{28,20},{32,40},... | collective-permute-start | bytes 393224 | tf_op jit(solution)/shard_map/ppermute | solution.py:233
  5.0 2.4 %collective-permute-start.2 = (f32[128,256]{1,0:T(8,128)S(1)}, f32[128,256]{1,0:T(8,128)S(1)}, u32[]{:S(2)}, u32[]{:S(2)}) collective-permute-start(f32[128,256]{1,0:T(8,128)S(1)} %get-tuple-element.36), channel_id=1, source_target_pairs={{0,12},{4,8},{8,4},{12,0},{16,28},{20,24},{24,20},{28,16},{32,44},... | collective-permute-start | bytes 393224 | tf_op jit(solution)/shard_map/ppermute | solution.py:233
  7.5 4.7 %own_and_near.1 = (f32[128,256]{1,0:T(8,128)S(1)}, f32[128,256]{1,0:T(8,128)S(1)}, f32[512,512]{1,0:T(8,128)S(1)}, f32[512,1024]{1,0:T(8,128)S(1)}) custom-call(f32[1024,512]{1,0:T(8,128)S(1)} %get-tuple-element.29.held.refs_1_, f32[1024,256]{1,0:T(8,128)S(1)} %get-tuple-element.30.basis_held, f32[1024,1024]{1,0:T(8,128)} %bitcast.6), custom_call_target="tpu_custom_call" | custom-call | flops 1610612736 | bytes 4194304 | tf_op jit(solution)/shard_map/own_and_near/pallas_call | solution.py:277
  12.3 0.2 collective-permute-done.2.refs_3_
  12.5 1.1 %collective-permute-done.refs_1_ = f32[128,256]{1,0:T(8,128)S(1)} collective-permute-done((f32[128,256]{1,0:T(8,128)S(1)}, f32[128,256]{1,0:T(8,128)S(1)}, u32[]{:S(2)}, u32[]{:S(2)}) %collective-permute-start) | collective-permute-done | bytes 131104 | tf_op jit(solution)/shard_map/ppermute | solution.py:233
  13.6 0.4 lift_leaves.1
  14.0 1.3 %collective-permute-start.3 = (f32[64,256]{1,0:T(8,128)S(1)}, f32[64,256]{1,0:T(8,128)S(1)}, u32[]{:S(2)}, u32[]{:S(2)}) collective-permute-start(f32[64,256]{1,0:T(8,128)S(1)} %get-tuple-element.37), channel_id=1, source_target_pairs={{0,40},{4,20},{8,32},{12,28},{16,56},{20,4},{24,48},{28,12},{32,8}... | collective-permute-start | bytes 196616 | tf_op jit(solution)/shard_map/ppermute | solution.py:233
  15.4 5.7 %collective-permute-start.4 = (f32[64,256]{1,0:T(8,128)S(1)}, f32[64,256]{1,0:T(8,128)S(1)}, u32[]{:S(2)}, u32[]{:S(2)}) collective-permute-start(f32[64,256]{1,0:T(8,128)S(1)} %get-tuple-element.38), channel_id=1, source_target_pairs={{0,0},{4,60},{8,8},{12,52},{16,16},{20,44},{24,24},{28,36},{32,32}... | collective-permute-start | bytes 196616 | tf_op jit(solution)/shard_map/ppermute | solution.py:233
  21.0 0.5 collective-permute-start.5
  21.5 1.1 %collective-permute-done.4.refs_1_ = f32[64,256]{1,0:T(8,128)S(1)} collective-permute-done((f32[64,256]{1,0:T(8,128)S(1)}, f32[64,256]{1,0:T(8,128)S(1)}, u32[]{:S(2)}, u32[]{:S(2)}) %collective-permute-start.4) | collective-permute-done | bytes 65568 | tf_op jit(solution)/shard_map/ppermute | solution.py:233
  22.7 1.2 %collective-permute-done.6.refs_3_ = f32[64,256]{1,0:T(8,128)S(1)} collective-permute-done((f32[64,256]{1,0:T(8,128)S(1)}, f32[64,256]{1,0:T(8,128)S(1)}, u32[]{:S(2)}, u32[]{:S(2)}) %collective-permute-start.6) | collective-permute-done | bytes 65568 | tf_op jit(solution)/shard_map/ppermute | solution.py:233
  23.9 0.4 lift_nodes.1
  24.4 4.6 %collective-permute-start.8 = (f32[64,256]{1,0:T(8,128)S(1)}, f32[64,256]{1,0:T(8,128)S(1)}, u32[]{:S(2)}, u32[]{:S(2)}) collective-permute-start(f32[64,256]{1,0:T(8,128)S(1)} %get-tuple-element.39), channel_id=1, source_target_pairs={{0,0},{4,196},{8,8},{12,204},{16,16},{20,212},{24,24},{28,220},{32... | collective-permute-start | bytes 196616 | tf_op jit(solution)/shard_map/ppermute | solution.py:233
  29.1 2.0 %collective-permute-done.8.refs_1_ = f32[64,256]{1,0:T(8,128)S(1)} collective-permute-done((f32[64,256]{1,0:T(8,128)S(1)}, f32[64,256]{1,0:T(8,128)S(1)}, u32[]{:S(2)}, u32[]{:S(2)}) %collective-permute-start.8) | collective-permute-done | bytes 65568 | tf_op jit(solution)/shard_map/ppermute | solution.py:233
  31.1 1.1 %collective-permute-done.7.refs_0_ = f32[64,256]{1,0:T(8,128)S(1)} collective-permute-done((f32[64,256]{1,0:T(8,128)S(1)}, f32[64,256]{1,0:T(8,128)S(1)}, u32[]{:S(2)}, u32[]{:S(2)}) %collective-permute-start.7) | collective-permute-done | bytes 65568 | tf_op jit(solution)/shard_map/ppermute | solution.py:233
  32.2 0.8 %couple_nodes.1 = (f32[64,256]{1,0:T(8,128)S(1)}, f32[64,256]{1,0:T(8,128)S(1)}) custom-call(f32[256,256]{1,0:T(8,128)S(1)} %get-tuple-element.40.refs_0_, f32[3,3,256,256]{3,2,1,0:T(8,128)S(1)} %copy-done.1), custom_call_target="tpu_custom_call" | custom-call | flops 150994944 | bytes 2621440 | tf_op jit(solution)/shard_map/couple_nodes/pallas_call | solution.py:45
  33.1 0.4 collective-permute-done.9.refs_2_
  33.5 1.1 %top.1 = (f32[64,256]{1,0:T(8,128)S(1)}, f32[64,256]{1,0:T(8,128)S(1)}) custom-call(f32[64,256]{1,0:T(8,128)S(1)} %collective-permute-done.7.refs_0_, f32[64,256]{1,0:T(8,128)S(1)} %collective-permute-done.8.refs_1_, f32[64,256]{1,0:T(8,128)S(1)} %collective-permute-done.9.refs_2_, f32[64,256]{1,0:T(8,128)S(1)} %collective-permute-done.10.refs_3_, ...), custom_call_target="tpu_custom_call" | custom-call | flops 125829120 | bytes 4849664 | tf_op jit(solution)/shard_map/top/pallas_call | solution.py:45
  34.6 3.0 %collective-permute-start.11 = (f32[64,256]{1,0:T(8,128)S(1)}, f32[64,256]{1,0:T(8,128)S(1)}, u32[]{:S(2)}, u32[]{:S(2)}) collective-permute-start(f32[64,256]{1,0:T(8,128)S(1)} %get-tuple-element.43), channel_id=1, source_target_pairs={{0,40},{4,20},{8,32},{12,28},{16,56},{20,4},{24,48},{28,12},{32,8}... | collective-permute-start | bytes 196616 | tf_op jit(solution)/shard_map/ppermute | solution.py:233
  37.6 4.8 %collective-permute-start.12 = (f32[64,256]{1,0:T(8,128)S(1)}, f32[64,256]{1,0:T(8,128)S(1)}, u32[]{:S(2)}, u32[]{:S(2)}) collective-permute-start(f32[64,256]{1,0:T(8,128)S(1)} %get-tuple-element.44), channel_id=1, source_target_pairs={{0,0},{4,60},{8,8},{12,52},{16,16},{20,44},{24,24},{28,36},{32,32}... | collective-permute-start | bytes 196616 | tf_op jit(solution)/shard_map/ppermute | solution.py:233
  42.4 1.7 %couple_leaves.1 = (f32[128,256]{1,0:T(8,128)S(1)}, f32[128,256]{1,0:T(8,128)S(1)}, f32[128,256]{1,0:T(8,128)S(1)}, f32[128,256]{1,0:T(8,128)S(1)}) custom-call(f32[128,256]{1,0:T(8,128)S(1)} %get-tuple-element.33.refs_0_, f32[128,256]{1,0:T(8,128)S(1)} %collective-permute-done.refs_1_, f32[128,256]{1,0:T(8,128)S(1)} %collective-permute-done.1.refs_2_, ...), custom_call_target="tpu_custom_call" | custom-call | flops 603979776 | bytes 2883584 | tf_op jit(solution)/shard_map/couple_leaves/pallas_call | solution.py:45
  44.1 0.2 collective-permute-done.12.refs_1_
  44.3 0.7 %descend.1 = (f32[128,256]{1,0:T(8,128)S(1)}, f32[128,256]{1,0:T(8,128)S(1)}, f32[128,256]{1,0:T(8,128)S(1)}, f32[128,256]{1,0:T(8,128)S(1)}) custom-call(f32[64,256]{1,0:T(8,128)S(1)} %collective-permute-done.11.refs_0_, f32[64,256]{1,0:T(8,128)S(1)} %collective-permute-done.12.refs_1_, f32[2,4,256,256]{3,2,1,0:T(8,128)S(1)} %copy-done, ...), custom_call_target="tpu_custom_call" | custom-call | flops 201326592 | bytes 2752512 | tf_op jit(solution)/shard_map/descend/pallas_call | solution.py:45
  45.0 1.0 %collective-permute-start.13 = (f32[128,256]{1,0:T(8,128)S(1)}, f32[128,256]{1,0:T(8,128)S(1)}, u32[]{:S(2)}, u32[]{:S(2)}) collective-permute-start(f32[128,256]{1,0:T(8,128)S(1)} %get-tuple-element.49), channel_id=1, source_target_pairs={{0,12},{4,8},{8,4},{12,0},{16,28},{20,24},{24,20},{28,16},{32,44},... | collective-permute-start | bytes 393224 | tf_op jit(solution)/shard_map/ppermute | solution.py:233
  46.0 0.9 %collective-permute-start.14 = (f32[128,256]{1,0:T(8,128)S(1)}, f32[128,256]{1,0:T(8,128)S(1)}, u32[]{:S(2)}, u32[]{:S(2)}) collective-permute-start(f32[128,256]{1,0:T(8,128)S(1)} %get-tuple-element.50), channel_id=1, source_target_pairs={{0,8},{4,12},{8,0},{12,4},{16,24},{20,28},{24,16},{28,20},{32,40},... | collective-permute-start | bytes 393224 | tf_op jit(solution)/shard_map/ppermute | solution.py:233
  46.9 0.4 collective-permute-start.15
  47.2 2.1 %near_field.1.near_below = f32[512,512]{1,0:T(8,128)S(1)} custom-call(f32[512,1024]{1,0:T(8,128)S(1)} %get-tuple-element.32.refs_0_, f32[1024,512]{1,0:T(8,128)S(1)} %get-tuple-element.29.held.refs_1_), custom_call_target="tpu_custom_call" | custom-call | flops 1610612736 | bytes 4194304 | tf_op jit(solution)/shard_map/near_field/pallas_call | solution.py:45
  49.3 1.5 %finish_0.1.rest_1_ = f32[1024,512]{1,0:T(8,128)} custom-call(f32[512,512]{1,0:T(8,128)S(1)} %get-tuple-element.31.near_above, f32[512,512]{1,0:T(8,128)S(1)} %near_field.1.near_below, f32[1024,256]{1,0:T(8,128)S(1)} %bitcast.3, f32[128,256]{1,0:T(8,128)S(1)} %get-tuple-element.51.rest_0_, f32[128,256]{1,0:T(8,128)S(1)} %collective-permute-done.15.rest_1_), custom_call_target="tpu_custom_call" | custom-call | flops 402653184 | bytes 1048576 | tf_op jit(solution)/shard_map/finish_0/pallas_call | solution.py:351
  50.8 2.5 %collective-permute-done.14.rest_0_ = f32[128,256]{1,0:T(8,128)S(1)} collective-permute-done((f32[128,256]{1,0:T(8,128)S(1)}, f32[128,256]{1,0:T(8,128)S(1)}, u32[]{:S(2)}, u32[]{:S(2)}) %collective-permute-start.14) | collective-permute-done | bytes 131104 | tf_op jit(solution)/shard_map/ppermute | solution.py:233
  53.3 1.3 %finish_2.1.rest_1_ = f32[1024,512]{1,0:T(8,128)} custom-call(f32[512,512]{1,0:T(8,128)S(1)} %get-tuple-element.31.near_above, f32[512,512]{1,0:T(8,128)S(1)} %near_field.1.near_below, f32[1024,256]{1,0:T(8,128)S(1)} %bitcast.4, f32[128,256]{1,0:T(8,128)S(1)} %collective-permute-done.14.rest_0_, ...), custom_call_target="tpu_custom_call", output_to_operand_aliasing={{}: (4, {})} | custom-call | flops 201326592 | bytes 524288 | tf_op jit(solution)/shard_map/finish_2/pallas_call | solution.py:351
  54.6 1.3 %finish_3.1 = f32[1024,512]{1,0:T(8,128)} custom-call(f32[512,512]{1,0:T(8,128)S(1)} %get-tuple-element.31.near_above, f32[512,512]{1,0:T(8,128)S(1)} %near_field.1.near_below, f32[1024,256]{1,0:T(8,128)S(1)} %bitcast.5, f32[128,256]{1,0:T(8,128)S(1)} %collective-permute-done.13.rest_0_, f32[1024,512]{1,0:T(8,128)} %finish_2.1.rest_1_), custom_call_target="tpu_custom_call", output_to_operand_aliasing={{}: (4, {})} | custom-call | flops 201326592 | bytes 524288 | tf_op jit(solution)/shard_map/finish_3/pallas_call | solution.py:351
  (18 shorter events, 0.2 us)
Async XLA Ops:
  2.5 9.7 %collective-permute-start.1 = (f32[128,256]{1,0:T(8,128)S(1)}, f32[128,256]{1,0:T(8,128)S(1)}, u32[]{:S(2)}, u32[]{:S(2)}) collective-permute-start(f32[128,256]{1,0:T(8,128)S(1)} %get-tuple-element.35), channel_id=1, source_target_pairs={{0,8},{4,12},{8,0},{12,4},{16,24},{20,28},{24,16},{28,20},{32,40},... | collective-permute-start | bytes 393224 | tf_op jit(solution)/shard_map/ppermute | solution.py:233
  5.0 7.5 %collective-permute-start.2 = (f32[128,256]{1,0:T(8,128)S(1)}, f32[128,256]{1,0:T(8,128)S(1)}, u32[]{:S(2)}, u32[]{:S(2)}) collective-permute-start(f32[128,256]{1,0:T(8,128)S(1)} %get-tuple-element.36), channel_id=1, source_target_pairs={{0,12},{4,8},{8,4},{12,0},{16,28},{20,24},{24,20},{28,16},{32,44},... | collective-permute-start | bytes 393224 | tf_op jit(solution)/shard_map/ppermute | solution.py:233
  7.5 6.1 %copy-start = (f32[2,4,256,256]{3,2,1,0:T(8,128)S(1)}, f32[2,4,256,256]{3,2,1,0:T(8,128)}, u32[]{:S(2)}) copy-start(f32[2,4,256,256]{3,2,1,0:T(8,128)} %refs_2_.1) | copy-start | bytes 6291460
  12.1 1.4 %collective-permute-start = (f32[128,256]{1,0:T(8,128)S(1)}, f32[128,256]{1,0:T(8,128)S(1)}, u32[]{:S(2)}, u32[]{:S(2)}) collective-permute-start(f32[128,256]{1,0:T(8,128)S(1)} %get-tuple-element.34), channel_id=1, source_target_pairs={{0,4},{4,0},{8,12},{12,8},{16,20},{20,16},{24,28},{28,24},{32,36},... | collective-permute-start | bytes 393224 | tf_op jit(solution)/shard_map/ppermute | solution.py:233
  13.6 18.6 %copy-start.1 = (f32[3,3,256,256]{3,2,1,0:T(8,128)S(1)}, f32[3,3,256,256]{3,2,1,0:T(8,128)}, u32[]{:S(2)}) copy-start(f32[3,3,256,256]{3,2,1,0:T(8,128)} %refs_4_.7) | copy-start | bytes 7077892
  14.0 7.0 %collective-permute-start.3 = (f32[64,256]{1,0:T(8,128)S(1)}, f32[64,256]{1,0:T(8,128)S(1)}, u32[]{:S(2)}, u32[]{:S(2)}) collective-permute-start(f32[64,256]{1,0:T(8,128)S(1)} %get-tuple-element.37), channel_id=1, source_target_pairs={{0,40},{4,20},{8,32},{12,28},{16,56},{20,4},{24,48},{28,12},{32,8}... | collective-permute-start | bytes 196616 | tf_op jit(solution)/shard_map/ppermute | solution.py:233
  15.4 7.3 %collective-permute-start.4 = (f32[64,256]{1,0:T(8,128)S(1)}, f32[64,256]{1,0:T(8,128)S(1)}, u32[]{:S(2)}, u32[]{:S(2)}) collective-permute-start(f32[64,256]{1,0:T(8,128)S(1)} %get-tuple-element.38), channel_id=1, source_target_pairs={{0,0},{4,60},{8,8},{12,52},{16,16},{20,44},{24,24},{28,36},{32,32}... | collective-permute-start | bytes 196616 | tf_op jit(solution)/shard_map/ppermute | solution.py:233
  21.0 1.6 %collective-permute-start.5 = (f32[64,256]{1,0:T(8,128)S(1)}, f32[64,256]{1,0:T(8,128)S(1)}, u32[]{:S(2)}, u32[]{:S(2)}) collective-permute-start(f32[64,256]{1,0:T(8,128)S(1)} %collective-permute-done.3.refs_0_), channel_id=1, source_target_pairs={{0,4},{4,0},{8,12},{12,8},{16,20},{20,16},{24,28},{28,24},{32,36},... | collective-permute-start | bytes 196616 | tf_op jit(solution)/shard_map/ppermute | solution.py:233
  22.7 1.3 %collective-permute-start.6 = (f32[64,256]{1,0:T(8,128)S(1)}, f32[64,256]{1,0:T(8,128)S(1)}, u32[]{:S(2)}, u32[]{:S(2)}) collective-permute-start(f32[64,256]{1,0:T(8,128)S(1)} %collective-permute-done.4.refs_1_), channel_id=1, source_target_pairs={{0,4},{4,0},{8,12},{12,8},{16,20},{20,16},{24,28},{28,24},{32,36},... | collective-permute-start | bytes 196616 | tf_op jit(solution)/shard_map/ppermute | solution.py:233
  24.4 6.7 %collective-permute-start.8 = (f32[64,256]{1,0:T(8,128)S(1)}, f32[64,256]{1,0:T(8,128)S(1)}, u32[]{:S(2)}, u32[]{:S(2)}) collective-permute-start(f32[64,256]{1,0:T(8,128)S(1)} %get-tuple-element.39), channel_id=1, source_target_pairs={{0,0},{4,196},{8,8},{12,204},{16,16},{20,212},{24,24},{28,220},{32... | collective-permute-start | bytes 196616 | tf_op jit(solution)/shard_map/ppermute | solution.py:233
  29.0 3.2 %collective-permute-start.7 = (f32[64,256]{1,0:T(8,128)S(1)}, f32[64,256]{1,0:T(8,128)S(1)}, u32[]{:S(2)}, u32[]{:S(2)}) collective-permute-start(f32[64,256]{1,0:T(8,128)S(1)} %get-tuple-element.39), channel_id=1, source_target_pairs={{0,128},{4,68},{8,136},{12,76},{16,144},{20,84},{24,152},{28,92},{... | collective-permute-start | bytes 196616 | tf_op jit(solution)/shard_map/ppermute | solution.py:233
  31.1 2.0 %collective-permute-start.10 = (f32[64,256]{1,0:T(8,128)S(1)}, f32[64,256]{1,0:T(8,128)S(1)}, u32[]{:S(2)}, u32[]{:S(2)}) collective-permute-start(f32[64,256]{1,0:T(8,128)S(1)} %collective-permute-done.8.refs_1_), channel_id=1, source_target_pairs={{0,4},{4,0},{8,12},{12,8},{16,20},{20,16},{24,28},{28,24},{32,36},... | collective-permute-start | bytes 196616 | tf_op jit(solution)/shard_map/ppermute | solution.py:233
  32.2 1.3 %collective-permute-start.9 = (f32[64,256]{1,0:T(8,128)S(1)}, f32[64,256]{1,0:T(8,128)S(1)}, u32[]{:S(2)}, u32[]{:S(2)}) collective-permute-start(f32[64,256]{1,0:T(8,128)S(1)} %collective-permute-done.7.refs_0_), channel_id=1, source_target_pairs={{0,4},{4,0},{8,12},{12,8},{16,20},{20,16},{24,28},{28,24},{32,36},... | collective-permute-start | bytes 196616 | tf_op jit(solution)/shard_map/ppermute | solution.py:233
  34.6 9.5 %collective-permute-start.11 = (f32[64,256]{1,0:T(8,128)S(1)}, f32[64,256]{1,0:T(8,128)S(1)}, u32[]{:S(2)}, u32[]{:S(2)}) collective-permute-start(f32[64,256]{1,0:T(8,128)S(1)} %get-tuple-element.43), channel_id=1, source_target_pairs={{0,40},{4,20},{8,32},{12,28},{16,56},{20,4},{24,48},{28,12},{32,8}... | collective-permute-start | bytes 196616 | tf_op jit(solution)/shard_map/ppermute | solution.py:233
  37.6 6.7 %collective-permute-start.12 = (f32[64,256]{1,0:T(8,128)S(1)}, f32[64,256]{1,0:T(8,128)S(1)}, u32[]{:S(2)}, u32[]{:S(2)}) collective-permute-start(f32[64,256]{1,0:T(8,128)S(1)} %get-tuple-element.44), channel_id=1, source_target_pairs={{0,0},{4,60},{8,8},{12,52},{16,16},{20,44},{24,24},{28,36},{32,32}... | collective-permute-start | bytes 196616 | tf_op jit(solution)/shard_map/ppermute | solution.py:233
  45.0 9.6 %collective-permute-start.13 = (f32[128,256]{1,0:T(8,128)S(1)}, f32[128,256]{1,0:T(8,128)S(1)}, u32[]{:S(2)}, u32[]{:S(2)}) collective-permute-start(f32[128,256]{1,0:T(8,128)S(1)} %get-tuple-element.49), channel_id=1, source_target_pairs={{0,12},{4,8},{8,4},{12,0},{16,28},{20,24},{24,20},{28,16},{32,44},... | collective-permute-start | bytes 393224 | tf_op jit(solution)/shard_map/ppermute | solution.py:233
  46.0 7.3 %collective-permute-start.14 = (f32[128,256]{1,0:T(8,128)S(1)}, f32[128,256]{1,0:T(8,128)S(1)}, u32[]{:S(2)}, u32[]{:S(2)}) collective-permute-start(f32[128,256]{1,0:T(8,128)S(1)} %get-tuple-element.50), channel_id=1, source_target_pairs={{0,8},{4,12},{8,0},{12,4},{16,24},{20,28},{24,16},{28,20},{32,40},... | collective-permute-start | bytes 393224 | tf_op jit(solution)/shard_map/ppermute | solution.py:233
  46.9 2.4 %collective-permute-start.15 = (f32[128,256]{1,0:T(8,128)S(1)}, f32[128,256]{1,0:T(8,128)S(1)}, u32[]{:S(2)}, u32[]{:S(2)}) collective-permute-start(f32[128,256]{1,0:T(8,128)S(1)} %get-tuple-element.52), channel_id=1, source_target_pairs={{0,4},{4,0},{8,12},{12,8},{16,20},{20,16},{24,28},{28,24},{32,36},... | collective-permute-start | bytes 393224 | tf_op jit(solution)/shard_map/ppermute | solution.py:233
  47.2 2.1 %copy-start.2 = (f32[1,1024,256]{2,1,0:T(8,128)S(1)}, f32[1,1024,256]{2,1,0:T(8,128)}, u32[]{:S(2)}) copy-start(f32[1,1024,256]{2,1,0:T(8,128)} %param.8) | copy-start | bytes 3145732

commit v5 on v4

--- a/solution.py
+++ b/solution.py
@@ -69,40 +69,39 @@
     return (source - target + 4) % 4 - 1
 
 
-def far_coefficients(x, basis, o2, o3, held, basis_held, whole, sems, rest_sem):
+def far_coefficients(x, basis, o2, o3, held, basis_held, whole, sems):
     _, m, k, _ = place()
     users, wide = x.shape[0], x.shape[1] // 2
     chunk = users // CHUNKS
-    far = 1 - (k ^ m) // 2
-    columns = span(far, wide)
+    columns = span(1 - (k ^ m) // 2, wide)
     copies = []
     for i in range(CHUNKS):
         at = pl.ds(i * chunk, chunk)
         pair = (
             pltpu.make_async_copy(basis.at[at], basis_held.at[at], sems.at[0, i]),
-            pltpu.make_async_copy(x.at[at, columns], held.at[at, columns], sems.at[1, i]),
+            pltpu.make_async_copy(x.at[at, columns], held.at[at], sems.at[1, i]),
         )
         for copy in pair:
             copy.start()
         copies.append(pair)
-    near_columns = span(1 - far, wide)
-    rest = pltpu.make_async_copy(x.at[:, near_columns], held.at[:, near_columns], rest_sem)
-    rest.start()
     for i, pair in enumerate(copies):
         at = pl.ds(i * chunk, chunk)
         for copy in pair:
             copy.wait()
-        term = dot(held[at, columns], basis_held[at, :], 0, 0)
+        term = dot(held[at, :], basis_held[at, :], 0, 0)
         whole[...] = term if i == 0 else whole[...] + term
     for j, out in ((2, o2), (3, o3)):
         out[...] = whole[span((k ^ m ^ j) % 2, wide // 2), :]
-    rest.wait()
-
-
-def own_and_near(held, basis_held, dense, o0, o1, out, dense_rest, whole, dense_held, sems):
+
+
+def own_and_near(
+    far, basis_held, x, dense, o0, o1, out, dense_rest, held, whole, dense_held, sems, x_sem
+):
     _, m, k, _ = place()
-    wide = held.shape[1] // 2
-    users = dense.shape[0]
+    users, wide = x.shape[0], x.shape[1] // 2
+    own = span((k ^ m) // 2, wide)
+    own_copy = pltpu.make_async_copy(x.at[:, own], held.at[:, own], x_sem)
+    own_copy.start()
     chunk = users // (2 * CHUNKS)
     copies = []
     for i in range(CHUNKS):
@@ -112,7 +111,9 @@
     copies.append(pltpu.make_async_copy(dense.at[below], dense_rest, sems.at[CHUNKS]))
     for copy in copies:
         copy.start()
-    whole[...] = dot(held[:, span((k ^ m) // 2, wide)], basis_held[...], 0, 0)
+    held[:, span(1 - (k ^ m) // 2, wide)] = far[...]
+    own_copy.wait()
+    whole[...] = dot(held[:, own], basis_held[...], 0, 0)
     for j, piece in ((0, o0), (1, o1)):
         piece[...] = whole[span((k ^ m ^ j) % 2, wide // 2), :]
     for i in range(CHUNKS):
@@ -156,17 +157,40 @@
         )
 
 
-def lift_nodes(a, b, swapped_a, swapped_b, transfers, out, parts):
+def order(core, a, b, out):
+    step = a.shape[0]
+    out[pl.ds(0, step), :] = pick(core, b, a)
+    out[pl.ds(step, step), :] = pick(core, a, b)
+
+
+def merge(a, b, out):
+    order(place()[3], a, b, out)
+
+
+def merge_slices(a, b, out):
+    _, m, _, core = place()
+    step = a.shape[0]
+    out[span(m // 2, step), :] = pick(core, b, a)
+    out[span(1 - m // 2, step), :] = pick(core, a, b)
+
+
+def relay(block, out):
+    out[...] = block[...]
+
+
+def all_blocks(core, ours, theirs):
+    step = ours.shape[0] // 2
+    for j in range(4):
+        at = pl.ds(j // 2 * step, step)
+        even, odd = (ours, theirs) if j % 2 == 0 else (theirs, ours)
+        yield pick(core, even.at[at], odd.at[at])
+
+
+def lift_nodes(ours, theirs, transfers, out, parts):
     _, m, _, core = place()
     step = out.shape[0]
-    blocks = (
-        pick(core, b, swapped_b),
-        pick(core, swapped_a, a),
-        pick(core, a, swapped_a),
-        pick(core, swapped_b, b),
-    )
     total = None
-    for j, block in enumerate(blocks):
+    for j, block in enumerate(all_blocks(core, ours, theirs)):
         parts[pl.ds(j * step, step), :] = block
         term = dot(block, transfers[1, m ^ j], 1, 0)
         total = term if total is None else total + term
@@ -184,37 +208,26 @@
         )
 
 
-def top(a, b, swapped_a, swapped_b, couplings, transfers, field_a, field_rest, out_a, out_rest):
+def top(ours, theirs, couplings, transfers, field_a, field_rest, out_a, out_rest):
     r, m, _, core = place()
-    blocks = (pick(core, swapped_a, a), pick(core, a, swapped_a), pick(core, swapped_b, b))
     g = sum(
-        dot(block, couplings[2, offset(r ^ d, r)], 1, 1) for d, block in zip((1, 2, 3), blocks)
+        dot(block, couplings[2, offset(r ^ d, r)], 1, 1)
+        for d, block in enumerate(all_blocks(core, ours, theirs))
+        if d
     )
     out_a[...] = field_a[...] + dot(g, transfers[1, m ^ (2 - core)], 1, 1)
     out_rest[...] = field_rest[...] + dot(g, transfers[1, m ^ (3 * core)], 1, 1)
 
 
-def descend(a, b, transfers, f0, f1, f2, f3, o0, o1, o2, o3, whole):
-    _, m, k, core = place()
-    step = a.shape[0]
-    whole[span(m // 2, step), :] = pick(core, b, a)
-    whole[span(1 - m // 2, step), :] = pick(core, a, b)
-    g = whole[...]
-    for j, (field, out) in enumerate(((f0, o0), (f1, o1), (f2, o2), (f3, o3))):
-        out[...] = field[...] + dot(g, transfers[0, k ^ j], 1, 1)
-
-
-def finish(first, near_above, near_below, row_basis, *rest):
-    out, block, whole, sems = rest[-4:]
+def finish(first, near_above, near_below, row_basis, transfers, *rest):
+    *pieces, out, block, whole, sems = rest
+    pieces = [pieces[i : i + 2] for i in range(0, len(pieces) - len(pieces) % 2, 2)]
     _, m, k, _ = place()
-    wide, step = whole.shape[0], rest[0].shape[0]
-    if wide == step:
-        whole[...] = rest[0][...]
-        columns = span(k ^ m ^ first, wide)
-    else:
-        for j in (0, 1):
-            whole[span((k ^ m ^ j) % 2, step), :] = rest[j][...]
-        columns = span((k ^ m ^ first) // 2, wide)
+    wide, quarter = whole.shape[0], pieces[0][0].shape[0]
+    for n, (field, parent) in enumerate(pieces):
+        g = field[...] + dot(parent[...], transfers[0, k], 1, 1)
+        whole[span((k ^ m ^ (first + n)) % (wide // quarter), quarter), :] = g
+    columns = span((k ^ m ^ first) // (wide // quarter), wide)
     chunk = out.shape[0] // CHUNKS
     copies = []
     for i in range(CHUNKS):
@@ -262,19 +275,18 @@
         far_coefficients,
         out_shape=[
             pltpu.VMEM(shape, F32)
-            for shape in ((quarter, rank), (quarter, rank), (users, columns), (users, rank))
+            for shape in ((quarter, rank), (quarter, rank), (users, columns // 2), (users, rank))
         ],
         in_specs=[ANY] * 2,
         out_specs=[VMEM] * 4,
         scratch_shapes=[
             pltpu.VMEM((columns // 2, rank), F32),
             pltpu.SemaphoreType.DMA((2, CHUNKS)),
-            pltpu.SemaphoreType.DMA,
         ],
         **settings(3 * users * columns * rank, users * columns, "far_coefficients"),
     )(*in_hbm([ratings, cbasis]))
     c2, c3 = swap(c2, 2), swap(c3, 3)
-    c0, c1, near_above, dense_rest = pl.pallas_call(
+    c0, c1, near_above, dense_rest, held = pl.pallas_call(
         own_and_near,
         out_shape=[
             pltpu.VMEM(shape, F32)
@@ -283,17 +295,19 @@
                 (quarter, rank),
                 (users // 2, columns),
                 (users // 2, users),
+                (users, columns),
             )
         ],
-        in_specs=[VMEM, VMEM, ANY],
-        out_specs=[VMEM] * 4,
+        in_specs=[VMEM, VMEM, ANY, ANY],
+        out_specs=[VMEM] * 5,
         scratch_shapes=[
             pltpu.VMEM((columns // 2, rank), F32),
             pltpu.VMEM((users // 2, users), F32),
             pltpu.SemaphoreType.DMA((CHUNKS + 1,)),
+            pltpu.SemaphoreType.DMA,
         ],
         **settings(3 * users * users * columns, users * users, "own_and_near"),
-    )(*in_vmem([held, basis_held]), *in_hbm([dense]))
+    )(*in_vmem([held, basis_held]), *in_hbm([ratings, dense]))
     c1 = swap(c1, 1)
     (near_below,) = run(
         near_field,
@@ -315,56 +329,62 @@
     leaf_fields = run(
         couple_leaves, [*coef, couplings], [(quarter, rank)] * 4, "couple_leaves", unit * 3 * columns
     )
-    swapped_a, swapped_b = swap(got_a, 1), swap(got_b, 1)
+    (ours,) = run(
+        merge, [got_a, got_b], [(quarter, rank)], "merge_nodes", quarter * rank, after=leaf_fields
+    )
+    theirs = swap(ours, 1)
+    leaf_fields = [leaf_fields[0]] + [swap(leaf_fields[j], j) for j in (1, 2, 3)]
     crown, parts = run(
         lift_nodes,
-        [got_a, got_b, swapped_a, swapped_b, transfers],
+        [ours, theirs, transfers],
         [(slim, rank), (4 * slim, rank)],
         "lift_nodes",
         unit * 4 * slim,
     )
-    got_a, got_b = to_tops(crown)
+    (ours,) = run(merge, to_tops(crown), [(quarter, rank)], "merge_tops", quarter * rank)
+    theirs = swap(ours, 1)
     node_fields = run(
         couple_nodes, [parts, couplings], [(slim, rank)] * 2, "couple_nodes", unit * 6 * slim
     )
     a, rest = run(
         top,
-        [got_a, got_b, swap(got_a, 1), swap(got_b, 1), couplings, transfers, *node_fields],
+        [ours, theirs, couplings, transfers, *node_fields],
         [(slim, rank)] * 2,
         "top",
         unit * 5 * slim,
-    )
-    got_a, got_b = to_nodes(a, rest)
-
-    g0, g1, g2, g3 = run(
-        descend,
-        [got_a, got_b, transfers, *leaf_fields],
-        [(quarter, rank)] * 4,
-        "descend",
-        unit * columns,
-        scratch=[(quarter, rank)],
-    )
-    g2, g3, g1 = swap(g2, 2), swap(g3, 3), swap(g1, 1)
-
-    def write(first, pieces, out):
-        wide = len(pieces) * quarter
+        after=leaf_fields[2:3],
+    )
+    (parent,) = run(
+        merge_slices, to_nodes(a, rest), [(quarter, rank)], "merge_slices", quarter * rank
+    )
+    far_parent = swap(parent, 2)
+    parents = [parent, swap(parent, 1)]
+
+    def write(first, count, out):
+        wide = count * quarter
+        pieces = [x for j in range(first, first + count) for x in (leaf_fields[j], parents[j])]
+        ins = in_vmem([near_above, near_below, rbasis, transfers, *pieces])
         return pl.pallas_call(
             functools.partial(finish, first),
             out_shape=pltpu.HBM((users, columns), F32),
-            in_specs=[VMEM] * (3 + len(pieces)) + [ANY] * len(out),
+            in_specs=[VMEM] * len(ins) + [ANY] * len(out),
             out_specs=ANY,
             scratch_shapes=[
                 pltpu.VMEM((users, wide), F32),
                 pltpu.VMEM((wide, rank), F32),
                 pltpu.SemaphoreType.DMA((CHUNKS,)),
             ],
-            input_output_aliases={3 + len(pieces): 0} if out else {},
+            input_output_aliases={len(ins): 0} if out else {},
             **settings(6 * users * rank * wide, users * wide, "finish_%d" % first),
-        )(*in_vmem([near_above, near_below, rbasis, *pieces]), *out)
-
-    out = write(0, [g0, g1], [])
-    out = write(2, [g2], [out])
-    return write(3, [g3], [out])
+        )(*ins, *out)
+
+    out = write(0, 2, [])
+    (relayed,) = run(
+        relay, [far_parent], [(quarter, rank)], "relay", quarter * rank, after=in_hbm([out])
+    )
+    parents += [relayed, swap(relayed, 1)]
+    out = write(2, 1, [out])
+    return write(3, 1, [out])
 
 
 def solution(mesh):

time: 56.2 us -> 59.2 us (1.053)
  Pallas kernels: 18.5 us -> 21.1 us
  starting transfers between devices: 27.3 us -> 29.4 us
  waiting for transfers between devices: 9.9 us -> 8.09 us
    ppermute x16 -> x17, starting transfers between devices: 27.3 us -> 29.4 us  [send(): lax.ppermute(block, 'leaf', [(i, target(i, i % 2)) for i in range(lax.axi...]
    pallas_call x1, Pallas kernels: 4.67 us -> 6.64 us  [local(): pl.pallas_call(own_and_near, out_shape=[pltpu.VMEM(shape, F32) for shape...]
    ppermute x16 -> x17, waiting for transfers between devices: 9.9 us -> 8.09 us  [send(): lax.ppermute(block, 'leaf', [(i, target(i, i % 2)) for i in range(lax.axi...]
    pallas_call x3, Pallas kernels: 4.06 us -> 5.33 us  [write(): pl.pallas_call(functools.partial(finish, first), out_shape=pltpu.HBM((use...]
    pallas_call x7 -> x10, Pallas kernels: 7.24 us -> 6.66 us  [run(): pl.pallas_call(kernel, out_shape=[pltpu.VMEM(shape, F32) for shape in out...]
  transfers between devices with their start and end apart: 16 -> 17, of which waited for: 9 -> 6; matrix products, arithmetic and copies ran while one was open for 0% -> 0% of each run, Pallas kernels for 21% -> 25%
where the time goes in v5:
time: 59.2 us; the launch traced here: 59 us
  starting transfers between devices  29.4 us (50%)
  Pallas kernels  21.1 us (36%)
  waiting for transfers between devices  8.09 us (14%)
    ppermute x17, starting transfers between devices, send(): lax.ppermute(block, 'leaf', [(i, target(i, i % 2)) for i in range(lax.axi...  29.4 us
    ppermute x17, waiting for transfers between devices, send(): lax.ppermute(block, 'leaf', [(i, target(i, i % 2)) for i in range(lax.axi...  8.09 us
    pallas_call x10, Pallas kernels, run(): pl.pallas_call(kernel, out_shape=[pltpu.VMEM(shape, F32) for shape in out...  6.66 us
    pallas_call x1, Pallas kernels, local(): pl.pallas_call(own_and_near, out_shape=[pltpu.VMEM(shape, F32) for shape...  6.64 us
    pallas_call x3, Pallas kernels, write(): pl.pallas_call(functools.partial(finish, first), out_shape=pltpu.HBM((use...  5.33 us
    pallas_call x1, Pallas kernels, local(): pl.pallas_call(far_coefficients, out_shape=[pltpu.VMEM(shape, F32) for sh...  2.46 us
  transfers between devices with their start and end apart: 17, of which 6 were waited for; matrix products, arithmetic and copies ran while one was open for 0% of the time, Pallas kernels for 25%

profile of v5, /device:TPU:1, one launch (start us, length us, event | category | flops | bytes accessed | tf_op | source)
XLA Modules:
  0.0 59.0 jit_solution(7163093385658327622)
XLA Ops:
  0.0 2.5 %far_coefficients.1 = (f32[128,256]{1,0:T(8,128)S(1)}, f32[128,256]{1,0:T(8,128)S(1)}, f32[1024,256]{1,0:T(8,128)S(1)}, f32[1024,256]{1,0:T(8,128)S(1)}) custom-call(f32[1024,512]{1,0:T(8,128)} %x.3, f32[1024,256]{1,0:T(8,128)} %bitcast.7), custom_call_target="tpu_custom_call" | custom-call | flops 402653184 | bytes 2097152 | tf_op jit(solution)/shard_map/far_coefficients/pallas_call | solution.py:274
  2.5 2.6 %collective-permute-start.1 = (f32[128,256]{1,0:T(8,128)S(1)}, f32[128,256]{1,0:T(8,128)S(1)}, u32[]{:S(2)}, u32[]{:S(2)}) collective-permute-start(f32[128,256]{1,0:T(8,128)S(1)} %get-tuple-element.33), channel_id=1, source_target_pairs={{0,8},{4,12},{8,0},{12,4},{16,24},{20,28},{24,16},{28,20},{32,40},... | collective-permute-start | bytes 393224 | tf_op jit(solution)/shard_map/ppermute | solution.py:246
  5.0 2.4 %collective-permute-start.2 = (f32[128,256]{1,0:T(8,128)S(1)}, f32[128,256]{1,0:T(8,128)S(1)}, u32[]{:S(2)}, u32[]{:S(2)}) collective-permute-start(f32[128,256]{1,0:T(8,128)S(1)} %get-tuple-element.34), channel_id=1, source_target_pairs={{0,12},{4,8},{8,4},{12,0},{16,28},{20,24},{24,20},{28,16},{32,44},... | collective-permute-start | bytes 393224 | tf_op jit(solution)/shard_map/ppermute | solution.py:246
  7.4 6.6 %own_and_near.1 = (f32[128,256]{1,0:T(8,128)S(1)}, f32[128,256]{1,0:T(8,128)S(1)}, f32[512,512]{1,0:T(8,128)S(1)}, f32[512,1024]{1,0:T(8,128)S(1)}, f32[1024,512]{1,0:T(8,128)S(1)}) custom-call(f32[1024,256]{1,0:T(8,128)S(1)} %get-tuple-element.26.far, f32[1024,256]{1,0:T(8,128)S(1)} %get-tuple-element.27.basis_held, f32[1024,512]{1,0:T(8,128)} %x.3, ...), custom_call_target="tpu_custom_call" | custom-call | flops 1610612736 | bytes 4194304 | tf_op jit(solution)/shard_map/own_and_near/pallas_call | solution.py:289
  14.1 0.1 collective-permute-start
  14.2 1.3 %collective-permute-done.refs_1_ = f32[128,256]{1,0:T(8,128)S(1)} collective-permute-done((f32[128,256]{1,0:T(8,128)S(1)}, f32[128,256]{1,0:T(8,128)S(1)}, u32[]{:S(2)}, u32[]{:S(2)}) %collective-permute-start) | collective-permute-done | bytes 131104 | tf_op jit(solution)/shard_map/ppermute | solution.py:246
  15.5 0.4 lift_leaves.1
  16.0 1.3 %collective-permute-start.4 = (f32[64,256]{1,0:T(8,128)S(1)}, f32[64,256]{1,0:T(8,128)S(1)}, u32[]{:S(2)}, u32[]{:S(2)}) collective-permute-start(f32[64,256]{1,0:T(8,128)S(1)} %get-tuple-element.36), channel_id=1, source_target_pairs={{0,40},{4,20},{8,32},{12,28},{16,56},{20,4},{24,48},{28,12},{32,8}... | collective-permute-start | bytes 196616 | tf_op jit(solution)/shard_map/ppermute | solution.py:246
  17.3 5.7 %collective-permute-start.5 = (f32[64,256]{1,0:T(8,128)S(1)}, f32[64,256]{1,0:T(8,128)S(1)}, u32[]{:S(2)}, u32[]{:S(2)}) collective-permute-start(f32[64,256]{1,0:T(8,128)S(1)} %get-tuple-element.37), channel_id=1, source_target_pairs={{0,0},{4,60},{8,8},{12,52},{16,16},{20,44},{24,24},{28,36},{32,32}... | collective-permute-start | bytes 196616 | tf_op jit(solution)/shard_map/ppermute | solution.py:246
  23.0 1.7 %couple_leaves.1 = (f32[128,256]{1,0:T(8,128)S(1)}, f32[128,256]{1,0:T(8,128)S(1)}, f32[128,256]{1,0:T(8,128)S(1)}, f32[128,256]{1,0:T(8,128)S(1)}) custom-call(f32[128,256]{1,0:T(8,128)S(1)} %get-tuple-element.31.refs_0_, f32[128,256]{1,0:T(8,128)S(1)} %collective-permute-done.refs_1_, f32[128,256]{1,0:T(8,128)S(1)} %collective-permute-done.1.refs_2_, ...), custom_call_target="tpu_custom_call" | custom-call | flops 603979776 | bytes 2883584 | tf_op jit(solution)/shard_map/couple_leaves/pallas_call | solution.py:45
  24.7 0.1 collective-permute-start.6
  24.8 1.3 %collective-permute-done.6.refs_1_ = f32[128,256]{1,0:T(8,128)S(1)} collective-permute-done((f32[128,256]{1,0:T(8,128)S(1)}, f32[128,256]{1,0:T(8,128)S(1)}, u32[]{:S(2)}, u32[]{:S(2)}) %collective-permute-start.6) | collective-permute-done | bytes 131104 | tf_op jit(solution)/shard_map/ppermute | solution.py:246
  26.2 0.4 lift_nodes.1
  26.6 4.6 %collective-permute-start.8 = (f32[64,256]{1,0:T(8,128)S(1)}, f32[64,256]{1,0:T(8,128)S(1)}, u32[]{:S(2)}, u32[]{:S(2)}) collective-permute-start(f32[64,256]{1,0:T(8,128)S(1)} %get-tuple-element.41), channel_id=1, source_target_pairs={{0,0},{4,196},{8,8},{12,204},{16,16},{20,212},{24,24},{28,220},{32... | collective-permute-start | bytes 196616 | tf_op jit(solution)/shard_map/ppermute | solution.py:246
  31.2 0.1 collective-permute-start.7
  31.3 2.3 %collective-permute-start.10 = (f32[128,256]{1,0:T(8,128)S(1)}, f32[128,256]{1,0:T(8,128)S(1)}, u32[]{:S(2)}, u32[]{:S(2)}) collective-permute-start(f32[128,256]{1,0:T(8,128)S(1)} %get-tuple-element.40.refs_4_), channel_id=1, source_target_pairs={{0,8},{4,12},{8,0},{12,4},{16,24},{20,28},{24,16},{28,20},{32,40},... | collective-permute-start | bytes 393224 | tf_op jit(solution)/shard_map/ppermute | solution.py:246
  33.7 1.0 %collective-permute-done.7.refs_0_ = f32[64,256]{1,0:T(8,128)S(1)} collective-permute-done((f32[64,256]{1,0:T(8,128)S(1)}, f32[64,256]{1,0:T(8,128)S(1)}, u32[]{:S(2)}, u32[]{:S(2)}) %collective-permute-start.7) | collective-permute-done | bytes 65568 | tf_op jit(solution)/shard_map/ppermute | solution.py:246
  34.7 0.3 collective-permute-start.9
  35.0 0.9 %couple_nodes.1 = (f32[64,256]{1,0:T(8,128)S(1)}, f32[64,256]{1,0:T(8,128)S(1)}) custom-call(f32[256,256]{1,0:T(8,128)S(1)} %get-tuple-element.42.refs_0_, f32[3,3,256,256]{3,2,1,0:T(8,128)S(1)} %copy-done.1), custom_call_target="tpu_custom_call" | custom-call | flops 150994944 | bytes 2621440 | tf_op jit(solution)/shard_map/couple_nodes/pallas_call | solution.py:45
  35.9 1.0 %collective-permute-done.10.refs_6_.rest_0_ = f32[128,256]{1,0:T(8,128)S(1)} collective-permute-done((f32[128,256]{1,0:T(8,128)S(1)}, f32[128,256]{1,0:T(8,128)S(1)}, u32[]{:S(2)}, u32[]{:S(2)}) %collective-permute-start.10) | collective-permute-done | bytes 131104 | tf_op jit(solution)/shard_map/ppermute | solution.py:246
  36.9 1.1 %top.1 = (f32[64,256]{1,0:T(8,128)S(1)}, f32[64,256]{1,0:T(8,128)S(1)}) custom-call(f32[128,256]{1,0:T(8,128)S(1)} %merge_tops.1.refs_0_, f32[128,256]{1,0:T(8,128)S(1)} %collective-permute-done.9.refs_1_, f32[3,3,256,256]{3,2,1,0:T(8,128)S(1)} %copy-done.1, f32[2,4,256,256]{3,2,1,0:T(8,128)S(1)} %copy-done, f32[64,256]{1,0:T(8,128)S(1)} %get-tuple-element.43.refs_4_, ...), custom_call_target="tpu_custom_call" | custom-call | flops 125829120 | bytes 4849664 | tf_op jit(solution)/shard_map/top/pallas_call | solution.py:45
  38.0 2.3 %collective-permute-start.11 = (f32[64,256]{1,0:T(8,128)S(1)}, f32[64,256]{1,0:T(8,128)S(1)}, u32[]{:S(2)}, u32[]{:S(2)}) collective-permute-start(f32[64,256]{1,0:T(8,128)S(1)} %get-tuple-element.45), channel_id=1, source_target_pairs={{0,40},{4,20},{8,32},{12,28},{16,56},{20,4},{24,48},{28,12},{32,8}... | collective-permute-start | bytes 196616 | tf_op jit(solution)/shard_map/ppermute | solution.py:246
  40.3 4.8 %collective-permute-start.12 = (f32[64,256]{1,0:T(8,128)S(1)}, f32[64,256]{1,0:T(8,128)S(1)}, u32[]{:S(2)}, u32[]{:S(2)}) collective-permute-start(f32[64,256]{1,0:T(8,128)S(1)} %get-tuple-element.46), channel_id=1, source_target_pairs={{0,0},{4,60},{8,8},{12,52},{16,16},{20,44},{24,24},{28,36},{32,32}... | collective-permute-start | bytes 196616 | tf_op jit(solution)/shard_map/ppermute | solution.py:246
  45.2 1.8 %collective-permute-done.12.refs_1_ = f32[64,256]{1,0:T(8,128)S(1)} collective-permute-done((f32[64,256]{1,0:T(8,128)S(1)}, f32[64,256]{1,0:T(8,128)S(1)}, u32[]{:S(2)}, u32[]{:S(2)}) %collective-permute-start.12) | collective-permute-done | bytes 65568 | tf_op jit(solution)/shard_map/ppermute | solution.py:246
  47.1 1.8 %collective-permute-start.13 = (f32[128,256]{1,0:T(8,128)S(1)}, f32[128,256]{1,0:T(8,128)S(1)}, u32[]{:S(2)}, u32[]{:S(2)}) collective-permute-start(f32[128,256]{1,0:T(8,128)S(1)} %merge_slices.1.rest_1_), channel_id=1, source_target_pairs={{0,8},{4,12},{8,0},{12,4},{16,24},{20,28},{24,16},{28,20},{32,40},... | collective-permute-start | bytes 393224 | tf_op jit(solution)/shard_map/ppermute | solution.py:246
  48.9 2.0 %near_field.1.near_below = f32[512,512]{1,0:T(8,128)S(1)} custom-call(f32[512,1024]{1,0:T(8,128)S(1)} %get-tuple-element.29.refs_0_, f32[1024,512]{1,0:T(8,128)S(1)} %get-tuple-element.30.refs_1_), custom_call_target="tpu_custom_call" | custom-call | flops 1610612736 | bytes 4194304 | tf_op jit(solution)/shard_map/near_field/pallas_call | solution.py:45
  50.9 0.4 collective-permute-start.3
  51.4 1.9 %finish_0.1.refs_1_.rest_2_ = f32[1024,512]{1,0:T(8,128)} custom-call(f32[512,512]{1,0:T(8,128)S(1)} %get-tuple-element.28.near_above, f32[512,512]{1,0:T(8,128)S(1)} %near_field.1.near_below, f32[1024,256]{1,0:T(8,128)S(1)} %bitcast.3, f32[2,4,256,256]{3,2,1,0:T(8,128)S(1)} %copy-done, f32[128,256]{1,0:T(8,128)S(1)} %get-tuple-element.38.refs_2_.rest_0_, ...), custom_call_target="tpu_custom_call" | custom-call | flops 402653184 | bytes 1048576 | tf_op jit(solution)/shard_map/finish_0/pallas_call | solution.py:367
  53.3 0.5 collective-permute-start.16
  53.8 1.7 %finish_2.1.rest_2_ = f32[1024,512]{1,0:T(8,128)} custom-call(f32[512,512]{1,0:T(8,128)S(1)} %get-tuple-element.28.near_above, f32[512,512]{1,0:T(8,128)S(1)} %near_field.1.near_below, f32[1024,256]{1,0:T(8,128)S(1)} %bitcast.4, f32[2,4,256,256]{3,2,1,0:T(8,128)S(1)} %copy-done, ...), custom_call_target="tpu_custom_call", output_to_operand_aliasing={{}: (6, {})} | custom-call | flops 201326592 | bytes 524288 | tf_op jit(solution)/shard_map/finish_2/pallas_call | solution.py:367
  55.5 1.6 %collective-permute-done.3.rest_0_ = f32[128,256]{1,0:T(8,128)S(1)} collective-permute-done((f32[128,256]{1,0:T(8,128)S(1)}, f32[128,256]{1,0:T(8,128)S(1)}, u32[]{:S(2)}, u32[]{:S(2)}) %collective-permute-start.3) | collective-permute-done | bytes 131104 | tf_op jit(solution)/shard_map/ppermute | solution.py:246
  57.1 1.7 %finish_3.1 = f32[1024,512]{1,0:T(8,128)} custom-call(f32[512,512]{1,0:T(8,128)S(1)} %get-tuple-element.28.near_above, f32[512,512]{1,0:T(8,128)S(1)} %near_field.1.near_below, f32[1024,256]{1,0:T(8,128)S(1)} %bitcast.5, f32[2,4,256,256]{3,2,1,0:T(8,128)S(1)} %copy-done, ...), custom_call_target="tpu_custom_call", output_to_operand_aliasing={{}: (6, {})} | custom-call | flops 201326592 | bytes 524288 | tf_op jit(solution)/shard_map/finish_3/pallas_call | solution.py:367
  (23 shorter events, 0.3 us)
Async XLA Ops:
  2.5 11.7 %collective-permute-start.1 = (f32[128,256]{1,0:T(8,128)S(1)}, f32[128,256]{1,0:T(8,128)S(1)}, u32[]{:S(2)}, u32[]{:S(2)}) collective-permute-start(f32[128,256]{1,0:T(8,128)S(1)} %get-tuple-element.33), channel_id=1, source_target_pairs={{0,8},{4,12},{8,0},{12,4},{16,24},{20,28},{24,16},{28,20},{32,40},... | collective-permute-start | bytes 393224 | tf_op jit(solution)/shard_map/ppermute | solution.py:246
  5.0 9.2 %collective-permute-start.2 = (f32[128,256]{1,0:T(8,128)S(1)}, f32[128,256]{1,0:T(8,128)S(1)}, u32[]{:S(2)}, u32[]{:S(2)}) collective-permute-start(f32[128,256]{1,0:T(8,128)S(1)} %get-tuple-element.34), channel_id=1, source_target_pairs={{0,12},{4,8},{8,4},{12,0},{16,28},{20,24},{24,20},{28,16},{32,44},... | collective-permute-start | bytes 393224 | tf_op jit(solution)/shard_map/ppermute | solution.py:246
  7.4 8.1 %copy-start = (f32[2,4,256,256]{3,2,1,0:T(8,128)S(1)}, f32[2,4,256,256]{3,2,1,0:T(8,128)}, u32[]{:S(2)}) copy-start(f32[2,4,256,256]{3,2,1,0:T(8,128)} %transfers.5) | copy-start | bytes 6291460
  14.1 8.9 %copy-start.1 = (f32[3,3,256,256]{3,2,1,0:T(8,128)S(1)}, f32[3,3,256,256]{3,2,1,0:T(8,128)}, u32[]{:S(2)}) copy-start(f32[3,3,256,256]{3,2,1,0:T(8,128)} %refs_2_.3) | copy-start | bytes 7077892
  14.1 1.4 %collective-permute-start = (f32[128,256]{1,0:T(8,128)S(1)}, f32[128,256]{1,0:T(8,128)S(1)}, u32[]{:S(2)}, u32[]{:S(2)}) collective-permute-start(f32[128,256]{1,0:T(8,128)S(1)} %get-tuple-element.32), channel_id=1, source_target_pairs={{0,4},{4,0},{8,12},{12,8},{16,20},{20,16},{24,28},{28,24},{32,36},... | collective-permute-start | bytes 393224 | tf_op jit(solution)/shard_map/ppermute | solution.py:246
  16.0 8.7 %collective-permute-start.4 = (f32[64,256]{1,0:T(8,128)S(1)}, f32[64,256]{1,0:T(8,128)S(1)}, u32[]{:S(2)}, u32[]{:S(2)}) collective-permute-start(f32[64,256]{1,0:T(8,128)S(1)} %get-tuple-element.36), channel_id=1, source_target_pairs={{0,40},{4,20},{8,32},{12,28},{16,56},{20,4},{24,48},{28,12},{32,8}... | collective-permute-start | bytes 196616 | tf_op jit(solution)/shard_map/ppermute | solution.py:246
  17.3 7.4 %collective-permute-start.5 = (f32[64,256]{1,0:T(8,128)S(1)}, f32[64,256]{1,0:T(8,128)S(1)}, u32[]{:S(2)}, u32[]{:S(2)}) collective-permute-start(f32[64,256]{1,0:T(8,128)S(1)} %get-tuple-element.37), channel_id=1, source_target_pairs={{0,0},{4,60},{8,8},{12,52},{16,16},{20,44},{24,24},{28,36},{32,32}... | collective-permute-start | bytes 196616 | tf_op jit(solution)/shard_map/ppermute | solution.py:246
  24.7 1.4 %collective-permute-start.6 = (f32[128,256]{1,0:T(8,128)S(1)}, f32[128,256]{1,0:T(8,128)S(1)}, u32[]{:S(2)}, u32[]{:S(2)}) collective-permute-start(f32[128,256]{1,0:T(8,128)S(1)} %merge_nodes.1.refs_0_), channel_id=1, source_target_pairs={{0,4},{4,0},{8,12},{12,8},{16,20},{20,16},{24,28},{28,24},{32,36},... | collective-permute-start | bytes 393224 | tf_op jit(solution)/shard_map/ppermute | solution.py:246
  26.6 7.1 %collective-permute-start.8 = (f32[64,256]{1,0:T(8,128)S(1)}, f32[64,256]{1,0:T(8,128)S(1)}, u32[]{:S(2)}, u32[]{:S(2)}) collective-permute-start(f32[64,256]{1,0:T(8,128)S(1)} %get-tuple-element.41), channel_id=1, source_target_pairs={{0,0},{4,196},{8,8},{12,204},{16,16},{20,212},{24,24},{28,220},{32... | collective-permute-start | bytes 196616 | tf_op jit(solution)/shard_map/ppermute | solution.py:246
  31.2 3.5 %collective-permute-start.7 = (f32[64,256]{1,0:T(8,128)S(1)}, f32[64,256]{1,0:T(8,128)S(1)}, u32[]{:S(2)}, u32[]{:S(2)}) collective-permute-start(f32[64,256]{1,0:T(8,128)S(1)} %get-tuple-element.41), channel_id=1, source_target_pairs={{0,128},{4,68},{8,136},{12,76},{16,144},{20,84},{24,152},{28,92},{... | collective-permute-start | bytes 196616 | tf_op jit(solution)/shard_map/ppermute | solution.py:246
  31.3 5.6 %collective-permute-start.10 = (f32[128,256]{1,0:T(8,128)S(1)}, f32[128,256]{1,0:T(8,128)S(1)}, u32[]{:S(2)}, u32[]{:S(2)}) collective-permute-start(f32[128,256]{1,0:T(8,128)S(1)} %get-tuple-element.40.refs_4_), channel_id=1, source_target_pairs={{0,8},{4,12},{8,0},{12,4},{16,24},{20,28},{24,16},{28,20},{32,40},... | collective-permute-start | bytes 393224 | tf_op jit(solution)/shard_map/ppermute | solution.py:246
  34.7 2.1 %collective-permute-start.9 = (f32[128,256]{1,0:T(8,128)S(1)}, f32[128,256]{1,0:T(8,128)S(1)}, u32[]{:S(2)}, u32[]{:S(2)}) collective-permute-start(f32[128,256]{1,0:T(8,128)S(1)} %merge_tops.1.refs_0_), channel_id=1, source_target_pairs={{0,4},{4,0},{8,12},{12,8},{16,20},{20,16},{24,28},{28,24},{32,36},... | collective-permute-start | bytes 393224 | tf_op jit(solution)/shard_map/ppermute | solution.py:246
  38.0 7.2 %collective-permute-start.11 = (f32[64,256]{1,0:T(8,128)S(1)}, f32[64,256]{1,0:T(8,128)S(1)}, u32[]{:S(2)}, u32[]{:S(2)}) collective-permute-start(f32[64,256]{1,0:T(8,128)S(1)} %get-tuple-element.45), channel_id=1, source_target_pairs={{0,40},{4,20},{8,32},{12,28},{16,56},{20,4},{24,48},{28,12},{32,8}... | collective-permute-start | bytes 196616 | tf_op jit(solution)/shard_map/ppermute | solution.py:246
  40.3 6.6 %collective-permute-start.12 = (f32[64,256]{1,0:T(8,128)S(1)}, f32[64,256]{1,0:T(8,128)S(1)}, u32[]{:S(2)}, u32[]{:S(2)}) collective-permute-start(f32[64,256]{1,0:T(8,128)S(1)} %get-tuple-element.46), channel_id=1, source_target_pairs={{0,0},{4,60},{8,8},{12,52},{16,16},{20,44},{24,24},{28,36},{32,32}... | collective-permute-start | bytes 196616 | tf_op jit(solution)/shard_map/ppermute | solution.py:246
  45.1 6.3 %collective-permute-start.14 = (f32[128,256]{1,0:T(8,128)S(1)}, f32[128,256]{1,0:T(8,128)S(1)}, u32[]{:S(2)}, u32[]{:S(2)}) collective-permute-start(f32[128,256]{1,0:T(8,128)S(1)} %get-tuple-element.39.refs_3_), channel_id=1, source_target_pairs={{0,4},{4,0},{8,12},{12,8},{16,20},{20,16},{24,28},{28,24},{32,36},... | collective-permute-start | bytes 393224 | tf_op jit(solution)/shard_map/ppermute | solution.py:246
  47.0 4.4 %collective-permute-start.15 = (f32[128,256]{1,0:T(8,128)S(1)}, f32[128,256]{1,0:T(8,128)S(1)}, u32[]{:S(2)}, u32[]{:S(2)}) collective-permute-start(f32[128,256]{1,0:T(8,128)S(1)} %merge_slices.1.rest_1_), channel_id=1, source_target_pairs={{0,4},{4,0},{8,12},{12,8},{16,20},{20,16},{24,28},{28,24},{32,36},... | collective-permute-start | bytes 393224 | tf_op jit(solution)/shard_map/ppermute | solution.py:246
  47.1 6.2 %collective-permute-start.13 = (f32[128,256]{1,0:T(8,128)S(1)}, f32[128,256]{1,0:T(8,128)S(1)}, u32[]{:S(2)}, u32[]{:S(2)}) collective-permute-start(f32[128,256]{1,0:T(8,128)S(1)} %merge_slices.1.rest_1_), channel_id=1, source_target_pairs={{0,8},{4,12},{8,0},{12,4},{16,24},{20,28},{24,16},{28,20},{32,40},... | collective-permute-start | bytes 393224 | tf_op jit(solution)/shard_map/ppermute | solution.py:246
  48.9 2.5 %copy-start.2 = (f32[1,1024,256]{2,1,0:T(8,128)S(1)}, f32[1,1024,256]{2,1,0:T(8,128)}, u32[]{:S(2)}) copy-start(f32[1,1024,256]{2,1,0:T(8,128)} %param.8) | copy-start | bytes 3145732
  50.9 6.2 %collective-permute-start.3 = (f32[128,256]{1,0:T(8,128)S(1)}, f32[128,256]{1,0:T(8,128)S(1)}, u32[]{:S(2)}, u32[]{:S(2)}) collective-permute-start(f32[128,256]{1,0:T(8,128)S(1)} %get-tuple-element.35.refs_5_), channel_id=1, source_target_pairs={{0,12},{4,8},{8,4},{12,0},{16,28},{20,24},{24,20},{28,16},{32,44},... | collective-permute-start | bytes 393224 | tf_op jit(solution)/shard_map/ppermute | solution.py:246
  53.3 3.8 %collective-permute-start.16 = (f32[128,256]{1,0:T(8,128)S(1)}, f32[128,256]{1,0:T(8,128)S(1)}, u32[]{:S(2)}, u32[]{:S(2)}) collective-permute-start(f32[128,256]{1,0:T(8,128)S(1)} %relay.1.rest_1_), channel_id=1, source_target_pairs={{0,4},{4,0},{8,12},{12,8},{16,20},{20,16},{24,28},{28,24},{32,36},... | collective-permute-start | bytes 393224 | tf_op jit(solution)/shard_map/ppermute | solution.py:246

commit v6 on v3

v6 whole, which is shorter than its diff:
```python
import functools

import jax
import jax.numpy as jnp
from jax import lax
from jax.experimental import pallas as pl
from jax.experimental.pallas import tpu as pltpu
from jax.sharding import PartitionSpec as P


F32 = jnp.float32
HIGH = lax.Precision.HIGH
MIB = 1 << 20
VMEM = pl.BlockSpec(memory_space=pltpu.VMEM)
ANY = pl.BlockSpec(memory_space=pl.ANY)
CHUNKS = 4


def dot(a, b, ca, cb):
    return lax.dot_general(
        a, b, (((ca,), (cb,)), ((), ())), precision=HIGH, preferred_element_type=F32
    )


def in_vmem(arrays):
    return [pltpu.with_memory_space_constraint(x, pltpu.VMEM) for x in arrays]


def in_hbm(arrays):
    return [pltpu.with_memory_space_constraint(x, pltpu.HBM) for x in arrays]


def settings(flops, size, name):
    return dict(
        compiler_params=pltpu.CompilerParams(vmem_limit_bytes=24 * MIB),
        cost_estimate=pl.CostEstimate(flops=flops, bytes_accessed=4 * size, transcendentals=0),
        name=name,
    )


def run(body, ins, outs, name, flops, after=(), scratch=()):
    def kernel(*refs):
        body(*refs[: len(ins)], *refs[len(ins) + len(after) :])

    return pl.pallas_call(
        kernel,
        out_shape=[pltpu.VMEM(shape, F32) for shape in outs],
        in_specs=[VMEM] * len(ins) + [ANY] * len(after),
        out_specs=[VMEM] * len(outs),
        scratch_shapes=[pltpu.VMEM(shape, F32) for shape in scratch],
        **settings(flops, sum(x.size for x in ins), name),
    )(*in_vmem(ins), *after)


def place():
    leaf = lax.axis_index("leaf")
    return leaf // 16, leaf // 4 % 4, leaf % 4, leaf % 2


def mine(m, k):
    return k ^ (m & 2)


def span(index, count):
    return pl.ds(pl.multiple_of(index * count, count), count)


def offset(source, target):
    return (source - target + 4) % 4 - 1


def far_coefficients(x, basis, o2, o3, held, basis_held, whole, sems, rest_sem):
    _, m, k, _ = place()
    users, wide = x.shape[0], x.shape[1] // 2
    chunk = users // CHUNKS
    far = 1 - mine(m, k) // 2
    columns = span(far, wide)
    copies = []
    for i in range(CHUNKS):
        at = pl.ds(i * chunk, chunk)
        pair = (
            pltpu.make_async_copy(basis.at[at], basis_held.at[at], sems.at[0, i]),
            pltpu.make_async_copy(x.at[at, columns], held.at[at, columns], sems.at[1, i]),
        )
        for copy in pair:
            copy.start()
        copies.append(pair)
    near_columns = span(1 - far, wide)
    rest = pltpu.make_async_copy(x.at[:, near_columns], held.at[:, near_columns], rest_sem)
    rest.start()
    for i, pair in enumerate(copies):
        at = pl.ds(i * chunk, chunk)
        for copy in pair:
            copy.wait()
        term = dot(held[at, columns], basis_held[at, :], 0, 0)
        whole[...] = term if i == 0 else whole[...] + term
    for j, out in ((2, o2), (3, o3)):
        out[...] = whole[span((mine(m, k) ^ j) % 2, wide // 2), :]
    rest.wait()


def near_rows(dense, first, held, sems, x, out, meanwhile=None):
    count, chunk = len(sems), out.shape[0] // len(sems)
    copies = [
        pltpu.make_async_copy(
            dense.at[pl.ds(first + i * chunk, chunk)], held.at[pl.ds(i * chunk, chunk)], sems[i]
        )
        for i in range(count)
    ]
    for copy in copies:
        copy.start()
    if meanwhile is not None:
        meanwhile()
    for i, copy in enumerate(copies):
        at = pl.ds(i * chunk, chunk)
        copy.wait()
        out[at, :] = dot(held[at, :], x[...], 1, 0)


def own_and_near(held, basis_held, dense, o0, o1, out, whole, dense_held, sems):
    _, m, k, _ = place()
    wide = held.shape[1] // 2

    def own():
        whole[...] = dot(held[:, span(mine(m, k) // 2, wide)], basis_held[...], 0, 0)
        for j, piece in ((0, o0), (1, o1)):
            piece[...] = whole[span((mine(m, k) ^ j) % 2, wide // 2), :]

    near_rows(dense, 0, dense_held, [sems.at[i] for i in (0, 1)], held, out, own)


def near_field(dense, x, _, out, dense_held, sems):
    half = out.shape[0]
    near_rows(dense, half, dense_held, [sems.at[i] for i in (0, 1)], x, out)


def lift(level, digit, c0, c1, c2, c3, transfers, out):
    own = place()[digit]
    parts = (c0, c1, c2, c3)
    out[...] = sum(dot(c[...], transfers[level, own ^ j], 1, 0) for j, c in enumerate(parts))


def couple(level, digit, c0, c1, c2, c3, couplings, *fields):
    own = place()[digit]
    parts = (c0, c1, c2, c3)
    for target, out in enumerate(fields):
        at = own ^ target
        out[...] = sum(
            dot(parts[target ^ d][...], couplings[level, offset(at ^ d, at)], 1, 1) for d in (1, 2, 3)
        )


def turn(couplings, transfers, top_turned, node_turned, leaf_turned):
    _, m, _, _ = place()
    for i in range(3):
        top_turned[i] = couplings[2, i].T
    node_turned[...] = transfers[1, m].T
    for i in range(4):
        leaf_turned[i] = transfers[0, i].T


def descend(c1, c2, c3, top_turned, node_turned, leaf_turned, field, f0, f1, f2, f3, *outs):
    r, _, k, _ = place()
    parts = (c1, c2, c3)
    g = sum(dot(c[...], top_turned[offset(r ^ d, r)], 1, 0) for d, c in zip((1, 2, 3), parts))
    g = field[...] + dot(g, node_turned[...], 1, 0)
    for j, (f, out) in enumerate(zip((f0, f1, f2, f3), outs)):
        out[...] = f[...] + dot(g, leaf_turned[k ^ j], 1, 0)


def finish(first, near_above, near_below, row_basis, *rest):
    out, block, whole, sems = rest[-4:]
    _, m, k, _ = place()
    wide, step = whole.shape[0], rest[0].shape[0]
    if wide == step:
        whole[...] = rest[0][...]
        columns = span(mine(m, k) ^ first, wide)
    else:
        for j in (0, 1):
            whole[span((mine(m, k) ^ j) % 2, step), :] = rest[j][...]
        columns = span((mine(m, k) ^ first) // 2, wide)
    chunk = out.shape[0] // CHUNKS
    copies = []
    for i in range(CHUNKS):
        at = pl.ds(i * chunk, chunk)
        near = near_above if 2 * i < CHUNKS else near_below
        part = near[pl.ds(i * chunk % near.shape[0], chunk), columns]
        block[at, :] = part + dot(row_basis[at, :], whole[...], 1, 1)
        copy = pltpu.make_async_copy(block.at[at], out.at[at, columns], sems.at[i])
        copy.start()
        copies.append(copy)
    for copy in copies:
        copy.wait()


def swap(block, bits):
    return lax.ppermute(block, "leaf", [(i, i ^ bits) for i in range(lax.axis_size("leaf"))])


def local(ratings, dense_blocks, row_basis, col_basis, transfers, couplings):
    users, columns = ratings.shape
    rank = col_basis.shape[2]
    quarter = columns // 4
    unit = 2 * 3 * rank * rank
    dense, rbasis, cbasis = dense_blocks[0], row_basis[0], col_basis[0]

    c2, c3, held, basis_held = pl.pallas_call(
        far_coefficients,
        out_shape=[
            pltpu.VMEM(shape, F32)
            for shape in ((quarter, rank), (quarter, rank), (users, columns), (users, rank))
        ],
        in_specs=[ANY] * 2,
        out_specs=[VMEM] * 4,
        scratch_shapes=[
            pltpu.VMEM((columns // 2, rank), F32),
            pltpu.SemaphoreType.DMA((2, CHUNKS)),
            pltpu.SemaphoreType.DMA,
        ],
        **settings(3 * users * columns * rank, users * columns, "far_coefficients"),
    )(*in_hbm([ratings, cbasis]))
    c2, c3 = swap(c2, 2), swap(c3, 3)
    half_rows = (users // 2, columns)
    dense_half = [pltpu.VMEM((users // 2, users), F32), pltpu.SemaphoreType.DMA((2,))]
    c0, c1, near_above = pl.pallas_call(
        own_and_near,
        out_shape=[pltpu.VMEM(shape, F32) for shape in ((quarter, rank), (quarter, rank), half_rows)],
        in_specs=[VMEM, VMEM, ANY],
        out_specs=[VMEM] * 3,
        scratch_shapes=[pltpu.VMEM((columns // 2, rank), F32), *dense_half],
        **settings(3 * users * users * columns, users * users, "own_and_near"),
    )(*in_vmem([held, basis_held]), *in_hbm([dense]))
    c1 = swap(c1, 1)
    coef = [c0, c1, c2, c3]
    (lifted,) = run(
        functools.partial(lift, 0, 2),
        [*coef, transfers],
        [(quarter, rank)],
        "lift_leaves",
        unit * columns,
    )
    node_coef = [lifted] + [swap(lifted, bits) for bits in (4, 10, 14)]
    near_below = pl.pallas_call(
        near_field,
        out_shape=pltpu.VMEM(half_rows, F32),
        in_specs=[ANY, VMEM, ANY],
        out_specs=VMEM,
        scratch_shapes=dense_half,
        **settings(3 * users * users * columns, users * users, "near_field"),
    )(*in_hbm([dense]), *in_vmem([held]), lifted)
    leaf_fields = run(
        functools.partial(couple, 0, 2),
        [*coef, couplings],
        [(quarter, rank)] * 4,
        "couple_leaves",
        unit * 3 * columns,
    )
    turned = run(
        turn,
        [couplings, transfers],
        [(3, rank, rank), (rank, rank), (4, rank, rank)],
        "turn",
        unit * 8 * rank,
        after=[lifted],
    )
    (crown,) = run(
        functools.partial(lift, 1, 1),
        [*node_coef, transfers],
        [(quarter, rank)],
        "lift_nodes",
        unit * columns,
        after=[*leaf_fields, near_below, turned[1]],
    )
    top_coef = [swap(crown, bits) for bits in (16, 32, 48)]
    (node_field,) = run(
        functools.partial(couple, 1, 1),
        [*node_coef, couplings],
        [(quarter, rank)],
        "couple_nodes",
        unit * 3 * quarter,
    )
    g0, g1, g2, g3 = run(
        descend,
        [*top_coef, *turned, node_field, *leaf_fields],
        [(quarter, rank)] * 4,
        "descend",
        unit * 8 * quarter,
    )
    g2, g3, g1 = swap(g2, 2), swap(g3, 3), swap(g1, 1)

    def write(first, pieces, out):
        wide = len(pieces) * quarter
        return pl.pallas_call(
            functools.partial(finish, first),
            out_shape=pltpu.HBM((users, columns), F32),
            in_specs=[VMEM] * (3 + len(pieces)) + [ANY] * len(out),
            out_specs=ANY,
            scratch_shapes=[
                pltpu.VMEM((users, wide), F32),
                pltpu.VMEM((wide, rank), F32),
                pltpu.SemaphoreType.DMA((CHUNKS,)),
            ],
            input_output_aliases={3 + len(pieces): 0} if out else {},
            **settings(6 * users * rank * wide, users * wide, "finish_%d" % first),
        )(*in_vmem([near_above, near_below, rbasis, *pieces]), *out)

    out = write(0, [g0, g1], [])
    out = write(2, [g2], [out])
    return write(3, [g3], [out])


def solution(mesh):
    placed = (
        P("leaf", "col"),
        P("leaf", None, None),
        P("leaf", None, None),
        P("leaf", None, None),
        P(),
        P(),
    )
    return jax.shard_map(
        local, mesh=mesh, in_specs=placed, out_specs=P("leaf", "col"), check_vma=False
    )
```

time: 58.2 us -> 54.8 us (0.942)
  starting transfers between devices: 31.3 us -> 19.1 us
  waiting for transfers between devices: 7.87 us -> 16.5 us
    ppermute x17 -> x12, starting transfers between devices: 31.3 us -> 19.1 us  [swap(): lax.ppermute(block, 'leaf', [(i, i ^ bits) for i in range(lax.axis_size('...]
    ppermute x17 -> x12, waiting for transfers between devices: 7.87 us -> 16.5 us  [swap(): lax.ppermute(block, 'leaf', [(i, i ^ bits) for i in range(lax.axis_size('...]
    pallas_call x1 -> x2, Pallas kernels: 5.8 us -> 7.53 us  [the longest x1 4.08 us: local(): pl.pallas_call(own_and_near, out_shape=[pltpu.VMEM(shape, F32) for shape...]
    pallas_call x7 -> x6, Pallas kernels: 6.04 us -> 4.73 us  [run(): pl.pallas_call(kernel, out_shape=[pltpu.VMEM(shape, F32) for shape in out...]
  transfers between devices with their start and end apart: 17 -> 12, of which waited for: 7 -> 10; matrix products, arithmetic and copies ran while one was open for 0% -> 0% of each run, Pallas kernels for 19% -> 24%
where the time goes in v6:
time: 54.8 us; the launch traced here: 54.7 us
  starting transfers between devices  19.1 us (35%)
  Pallas kernels  18.8 us (34%)
  waiting for transfers between devices  16.5 us (30%)
    ppermute x12, starting transfers between devices, swap(): lax.ppermute(block, 'leaf', [(i, i ^ bits) for i in range(lax.axis_size('...  19.1 us
    ppermute x12, waiting for transfers between devices, swap(): lax.ppermute(block, 'leaf', [(i, i ^ bits) for i in range(lax.axis_size('...  16.5 us
    pallas_call x6, Pallas kernels, run(): pl.pallas_call(kernel, out_shape=[pltpu.VMEM(shape, F32) for shape in out...  4.73 us
    pallas_call x1, Pallas kernels, local(): pl.pallas_call(own_and_near, out_shape=[pltpu.VMEM(shape, F32) for shape...  4.08 us
    pallas_call x3, Pallas kernels, write(): pl.pallas_call(functools.partial(finish, first), out_shape=pltpu.HBM((use...  4.05 us
    pallas_call x1, Pallas kernels, local(): pl.pallas_call(near_field, out_shape=pltpu.VMEM(half_rows, F32), in_specs...  3.45 us
    pallas_call x1, Pallas kernels, local(): pl.pallas_call(far_coefficients, out_shape=[pltpu.VMEM(shape, F32) for sh...  2.49 us
  transfers between devices with their start and end apart: 12, of which 10 were waited for; matrix products, arithmetic and copies ran while one was open for 0% of the time, Pallas kernels for 24%

profile of v6, /device:TPU:1, one launch (start us, length us, event | category | flops | bytes accessed | tf_op | source)
XLA Modules:
  0.0 54.7 jit_solution(12305721208413670604)
XLA Ops:
  0.0 2.5 %far_coefficients.1 = (f32[128,256]{1,0:T(8,128)S(1)}, f32[128,256]{1,0:T(8,128)S(1)}, f32[1024,512]{1,0:T(8,128)S(1)}, f32[1024,256]{1,0:T(8,128)S(1)}) custom-call(f32[1024,512]{1,0:T(8,128)} %x.1, f32[1024,256]{1,0:T(8,128)} %bitcast.8), custom_call_target="tpu_custom_call" | custom-call | flops 402653184 | bytes 2097152 | tf_op jit(solution)/shard_map/far_coefficients/pallas_call | solution.py:207
  2.5 2.5 %collective-permute-start.1 = (f32[128,256]{1,0:T(8,128)S(1)}, f32[128,256]{1,0:T(8,128)S(1)}, u32[]{:S(2)}, u32[]{:S(2)}) collective-permute-start(f32[128,256]{1,0:T(8,128)S(1)} %get-tuple-element.28), channel_id=1, source_target_pairs={{0,8},{4,12},{8,0},{12,4},{16,24},{20,28},{24,16},{28,20},{32,40},... | collective-permute-start | bytes 393224 | tf_op jit(solution)/shard_map/ppermute | solution.py:197
  5.0 2.4 %collective-permute-start.2 = (f32[128,256]{1,0:T(8,128)S(1)}, f32[128,256]{1,0:T(8,128)S(1)}, u32[]{:S(2)}, u32[]{:S(2)}) collective-permute-start(f32[128,256]{1,0:T(8,128)S(1)} %get-tuple-element.29), channel_id=1, source_target_pairs={{0,12},{4,8},{8,4},{12,0},{16,28},{20,24},{24,20},{28,16},{32,44},... | collective-permute-start | bytes 393224 | tf_op jit(solution)/shard_map/ppermute | solution.py:197
  7.5 4.1 %own_and_near.1 = (f32[128,256]{1,0:T(8,128)S(1)}, f32[128,256]{1,0:T(8,128)S(1)}, f32[512,512]{1,0:T(8,128)S(1)}) custom-call(f32[1024,512]{1,0:T(8,128)S(1)} %get-tuple-element.23.held.x, f32[1024,256]{1,0:T(8,128)S(1)} %get-tuple-element.24.basis_held, f32[1024,1024]{1,0:T(8,128)} %bitcast.6), custom_call_target="tpu_custom_call" | custom-call | flops 1610612736 | bytes 4194304 | tf_op jit(solution)/shard_map/own_and_near/pallas_call | solution.py:225
  11.6 0.1 collective-permute-start
  11.7 0.8 %collective-permute-done.2.refs_3_ = f32[128,256]{1,0:T(8,128)S(1)} collective-permute-done((f32[128,256]{1,0:T(8,128)S(1)}, f32[128,256]{1,0:T(8,128)S(1)}, u32[]{:S(2)}, u32[]{:S(2)}) %collective-permute-start.2) | collective-permute-done | bytes 131104 | tf_op jit(solution)/shard_map/ppermute | solution.py:197
  12.5 0.5 collective-permute-done.refs_1_
  13.0 0.4 lift_leaves.1._.refs_2_.refs_0_
  13.4 4.1 %collective-permute-start.5 = (f32[128,256]{1,0:T(8,128)S(1)}, f32[128,256]{1,0:T(8,128)S(1)}, u32[]{:S(2)}, u32[]{:S(2)}) collective-permute-start(f32[128,256]{1,0:T(8,128)S(1)} %lift_leaves.1._.refs_2_.refs_0_), channel_id=1, source_target_pairs={{0,56},{4,60},{8,48},{12,52},{16,40},{20,44},{24,32},{28,36},{32,2... | collective-permute-start | bytes 393224 | tf_op jit(solution)/shard_map/ppermute | solution.py:197
  17.6 1.0 %collective-permute-start.4 = (f32[128,256]{1,0:T(8,128)S(1)}, f32[128,256]{1,0:T(8,128)S(1)}, u32[]{:S(2)}, u32[]{:S(2)}) collective-permute-start(f32[128,256]{1,0:T(8,128)S(1)} %lift_leaves.1._.refs_2_.refs_0_), channel_id=1, source_target_pairs={{0,40},{4,44},{8,32},{12,36},{16,56},{20,60},{24,48},{28,52},{32,8... | collective-permute-start | bytes 393224 | tf_op jit(solution)/shard_map/ppermute | solution.py:197
  18.5 1.2 %collective-permute-start.3 = (f32[128,256]{1,0:T(8,128)S(1)}, f32[128,256]{1,0:T(8,128)S(1)}, u32[]{:S(2)}, u32[]{:S(2)}) collective-permute-start(f32[128,256]{1,0:T(8,128)S(1)} %lift_leaves.1._.refs_2_.refs_0_), channel_id=1, source_target_pairs={{0,16},{4,20},{8,24},{12,28},{16,0},{20,4},{24,8},{28,12},{32,48},... | collective-permute-start | bytes 393224 | tf_op jit(solution)/shard_map/ppermute | solution.py:197
  19.7 0.6 %turn.1 = (f32[3,256,256]{2,1,0:T(8,128)S(1)}, f32[256,256]{1,0:T(8,128)S(1)}, f32[4,256,256]{2,1,0:T(8,128)S(1)}) custom-call(f32[3,3,256,256]{3,2,1,0:T(8,128)S(1)} %copy-done, f32[2,4,256,256]{3,2,1,0:T(8,128)S(1)} %copy-done.1, f32[128,256]{1,0:T(8,128)S(1)} %lift_leaves.1._.refs_2_.refs_0_), custom_call_target="tpu_custom_call" | custom-call | flops 805306368 | bytes 4456448 | tf_op jit(solution)/shard_map/turn/pallas_call | solution.py:45
  20.3 1.7 %couple_leaves.1 = (f32[128,256]{1,0:T(8,128)S(1)}, f32[128,256]{1,0:T(8,128)S(1)}, f32[128,256]{1,0:T(8,128)S(1)}, f32[128,256]{1,0:T(8,128)S(1)}) custom-call(f32[128,256]{1,0:T(8,128)S(1)} %get-tuple-element.26.refs_0_, f32[128,256]{1,0:T(8,128)S(1)} %collective-permute-done.refs_1_, f32[128,256]{1,0:T(8,128)S(1)} %collective-permute-done.1.refs_2_, ...), custom_call_target="tpu_custom_call" | custom-call | flops 603979776 | bytes 2883584 | tf_op jit(solution)/shard_map/couple_leaves/pallas_call | solution.py:45
  22.0 3.5 %near_field.1.refs_9_.near_below = f32[512,512]{1,0:T(8,128)S(1)} custom-call(f32[1024,1024]{1,0:T(8,128)} %bitcast.7, f32[1024,512]{1,0:T(8,128)S(1)} %get-tuple-element.23.held.x, f32[128,256]{1,0:T(8,128)S(1)} %lift_leaves.1._.refs_2_.refs_0_), custom_call_target="tpu_custom_call" | custom-call | flops 1610612736 | bytes 4194304 | tf_op jit(solution)/shard_map/near_field/pallas_call | solution.py:243
  25.5 0.5 collective-permute-done.5.refs_3_
  26.0 3.0 %collective-permute-done.4.refs_2_ = f32[128,256]{1,0:T(8,128)S(1)} collective-permute-done((f32[128,256]{1,0:T(8,128)S(1)}, f32[128,256]{1,0:T(8,128)S(1)}, u32[]{:S(2)}, u32[]{:S(2)}) %collective-permute-start.4) | collective-permute-done | bytes 131104 | tf_op jit(solution)/shard_map/ppermute | solution.py:197
  28.9 3.0 %collective-permute-done.3.refs_1_ = f32[128,256]{1,0:T(8,128)S(1)} collective-permute-done((f32[128,256]{1,0:T(8,128)S(1)}, f32[128,256]{1,0:T(8,128)S(1)}, u32[]{:S(2)}, u32[]{:S(2)}) %collective-permute-start.3) | collective-permute-done | bytes 131104 | tf_op jit(solution)/shard_map/ppermute | solution.py:197
  32.0 0.4 lift_nodes.1
  32.4 2.8 %collective-permute-start.8 = (f32[128,256]{1,0:T(8,128)S(1)}, f32[128,256]{1,0:T(8,128)S(1)}, u32[]{:S(2)}, u32[]{:S(2)}) collective-permute-start(f32[128,256]{1,0:T(8,128)S(1)} %lift_nodes.1), channel_id=1, source_target_pairs={{0,192},{4,196},{8,200},{12,204},{16,208},{20,212},{24,216},{28,22... | collective-permute-start | bytes 393224 | tf_op jit(solution)/shard_map/ppermute | solution.py:197
  35.2 0.5 collective-permute-start.7
  35.7 0.4 collective-permute-start.6
  36.1 0.6 %couple_nodes.1.refs_6_ = f32[128,256]{1,0:T(8,128)S(1)} custom-call(f32[128,256]{1,0:T(8,128)S(1)} %lift_leaves.1._.refs_2_.refs_0_, f32[128,256]{1,0:T(8,128)S(1)} %collective-permute-done.3.refs_1_, f32[128,256]{1,0:T(8,128)S(1)} %collective-permute-done.4.refs_2_, f32[128,256]{1,0:T(8,128)S(1)} %collective-permute-done.5.refs_3_, ...), custom_call_target="tpu_custom_call" | custom-call | flops 150994944 | bytes 2883584 | tf_op jit(solution)/shard_map/couple_nodes/pallas_call | solution.py:45
  36.6 3.8 %collective-permute-done.8.refs_2_ = f32[128,256]{1,0:T(8,128)S(1)} collective-permute-done((f32[128,256]{1,0:T(8,128)S(1)}, f32[128,256]{1,0:T(8,128)S(1)}, u32[]{:S(2)}, u32[]{:S(2)}) %collective-permute-start.8) | collective-permute-done | bytes 131104 | tf_op jit(solution)/shard_map/ppermute | solution.py:197
  40.5 1.3 %collective-permute-done.6.refs_0_ = f32[128,256]{1,0:T(8,128)S(1)} collective-permute-done((f32[128,256]{1,0:T(8,128)S(1)}, f32[128,256]{1,0:T(8,128)S(1)}, u32[]{:S(2)}, u32[]{:S(2)}) %collective-permute-start.6) | collective-permute-done | bytes 131104 | tf_op jit(solution)/shard_map/ppermute | solution.py:197
  41.8 1.1 %descend.1 = (f32[128,256]{1,0:T(8,128)S(1)}, f32[128,256]{1,0:T(8,128)S(1)}, f32[128,256]{1,0:T(8,128)S(1)}, f32[128,256]{1,0:T(8,128)S(1)}) custom-call(f32[128,256]{1,0:T(8,128)S(1)} %collective-permute-done.6.refs_0_, f32[128,256]{1,0:T(8,128)S(1)} %collective-permute-done.7.refs_1_, f32[128,256]{1,0:T(8,128)S(1)} %collective-permute-done.8.refs_2_, ...), custom_call_target="tpu_custom_call" | custom-call | flops 402653184 | bytes 3145728 | tf_op jit(solution)/shard_map/descend/pallas_call | solution.py:45
  42.9 2.3 %collective-permute-start.11 = (f32[128,256]{1,0:T(8,128)S(1)}, f32[128,256]{1,0:T(8,128)S(1)}, u32[]{:S(2)}, u32[]{:S(2)}) collective-permute-start(f32[128,256]{1,0:T(8,128)S(1)} %get-tuple-element.40), channel_id=1, source_target_pairs={{0,4},{4,0},{8,12},{12,8},{16,20},{20,16},{24,28},{28,24},{32,36},... | collective-permute-start | bytes 393224 | tf_op jit(solution)/shard_map/ppermute | solution.py:197
  45.2 1.7 %collective-permute-start.9 = (f32[128,256]{1,0:T(8,128)S(1)}, f32[128,256]{1,0:T(8,128)S(1)}, u32[]{:S(2)}, u32[]{:S(2)}) collective-permute-start(f32[128,256]{1,0:T(8,128)S(1)} %get-tuple-element.37), channel_id=1, source_target_pairs={{0,12},{4,8},{8,4},{12,0},{16,28},{20,24},{24,20},{28,16},{32,44},... | collective-permute-start | bytes 393224 | tf_op jit(solution)/shard_map/ppermute | solution.py:197
  46.9 1.5 %finish_0.1.rest_1_ = f32[1024,512]{1,0:T(8,128)} custom-call(f32[512,512]{1,0:T(8,128)S(1)} %get-tuple-element.25.near_above, f32[512,512]{1,0:T(8,128)S(1)} %near_field.1.refs_9_.near_below, f32[1024,256]{1,0:T(8,128)S(1)} %bitcast.3, f32[128,256]{1,0:T(8,128)S(1)} %get-tuple-element.39.rest_0_, f32[128,256]{1,0:T(8,128)S(1)} %collective-permute-done.11.rest_1_), custom_call_target="tpu_custom_call" | custom-call | flops 402653184 | bytes 1048576 | tf_op jit(solution)/shard_map/finish_0/pallas_call | solution.py:293
  48.5 1.8 %collective-permute-done.10.rest_0_ = f32[128,256]{1,0:T(8,128)S(1)} collective-permute-done((f32[128,256]{1,0:T(8,128)S(1)}, f32[128,256]{1,0:T(8,128)S(1)}, u32[]{:S(2)}, u32[]{:S(2)}) %collective-permute-start.10) | collective-permute-done | bytes 131104 | tf_op jit(solution)/shard_map/ppermute | solution.py:197
  50.3 1.3 %finish_2.1.rest_1_ = f32[1024,512]{1,0:T(8,128)} custom-call(f32[512,512]{1,0:T(8,128)S(1)} %get-tuple-element.25.near_above, f32[512,512]{1,0:T(8,128)S(1)} %near_field.1.refs_9_.near_below, f32[1024,256]{1,0:T(8,128)S(1)} %bitcast.4, f32[128,256]{1,0:T(8,128)S(1)} %collective-permute-done.10.rest_0_, ...), custom_call_target="tpu_custom_call", output_to_operand_aliasing={{}: (4, {})} | custom-call | flops 201326592 | bytes 524288 | tf_op jit(solution)/shard_map/finish_2/pallas_call | solution.py:293
  51.5 1.7 %collective-permute-done.9.rest_0_ = f32[128,256]{1,0:T(8,128)S(1)} collective-permute-done((f32[128,256]{1,0:T(8,128)S(1)}, f32[128,256]{1,0:T(8,128)S(1)}, u32[]{:S(2)}, u32[]{:S(2)}) %collective-permute-start.9) | collective-permute-done | bytes 131104 | tf_op jit(solution)/shard_map/ppermute | solution.py:197
  53.3 1.3 %finish_3.1 = f32[1024,512]{1,0:T(8,128)} custom-call(f32[512,512]{1,0:T(8,128)S(1)} %get-tuple-element.25.near_above, f32[512,512]{1,0:T(8,128)S(1)} %near_field.1.refs_9_.near_below, f32[1024,256]{1,0:T(8,128)S(1)} %bitcast.5, f32[128,256]{1,0:T(8,128)S(1)} %collective-permute-done.9.rest_0_, ...), custom_call_target="tpu_custom_call", output_to_operand_aliasing={{}: (4, {})} | custom-call | flops 201326592 | bytes 524288 | tf_op jit(solution)/shard_map/finish_3/pallas_call | solution.py:293
  (10 shorter events, 0.1 us)
Async XLA Ops:
  2.5 9.2 %collective-permute-start.1 = (f32[128,256]{1,0:T(8,128)S(1)}, f32[128,256]{1,0:T(8,128)S(1)}, u32[]{:S(2)}, u32[]{:S(2)}) collective-permute-start(f32[128,256]{1,0:T(8,128)S(1)} %get-tuple-element.28), channel_id=1, source_target_pairs={{0,8},{4,12},{8,0},{12,4},{16,24},{20,28},{24,16},{28,20},{32,40},... | collective-permute-start | bytes 393224 | tf_op jit(solution)/shard_map/ppermute | solution.py:197
  5.0 7.5 %collective-permute-start.2 = (f32[128,256]{1,0:T(8,128)S(1)}, f32[128,256]{1,0:T(8,128)S(1)}, u32[]{:S(2)}, u32[]{:S(2)}) collective-permute-start(f32[128,256]{1,0:T(8,128)S(1)} %get-tuple-element.29), channel_id=1, source_target_pairs={{0,12},{4,8},{8,4},{12,0},{16,28},{20,24},{24,20},{28,16},{32,44},... | collective-permute-start | bytes 393224 | tf_op jit(solution)/shard_map/ppermute | solution.py:197
  7.5 5.5 %copy-start.1 = (f32[2,4,256,256]{3,2,1,0:T(8,128)S(1)}, f32[2,4,256,256]{3,2,1,0:T(8,128)}, u32[]{:S(2)}) copy-start(f32[2,4,256,256]{3,2,1,0:T(8,128)} %refs_4_.6) | copy-start | bytes 6291460
  11.5 8.2 %copy-start = (f32[3,3,256,256]{3,2,1,0:T(8,128)S(1)}, f32[3,3,256,256]{3,2,1,0:T(8,128)}, u32[]{:S(2)}) copy-start(f32[3,3,256,256]{3,2,1,0:T(8,128)} %refs_4_.7) | copy-start | bytes 7077892
  11.6 1.4 %collective-permute-start = (f32[128,256]{1,0:T(8,128)S(1)}, f32[128,256]{1,0:T(8,128)S(1)}, u32[]{:S(2)}, u32[]{:S(2)}) collective-permute-start(f32[128,256]{1,0:T(8,128)S(1)} %get-tuple-element.27), channel_id=1, source_target_pairs={{0,4},{4,0},{8,12},{12,8},{16,20},{20,16},{24,28},{28,24},{32,36},... | collective-permute-start | bytes 393224 | tf_op jit(solution)/shard_map/ppermute | solution.py:197
  13.4 12.5 %collective-permute-start.5 = (f32[128,256]{1,0:T(8,128)S(1)}, f32[128,256]{1,0:T(8,128)S(1)}, u32[]{:S(2)}, u32[]{:S(2)}) collective-permute-start(f32[128,256]{1,0:T(8,128)S(1)} %lift_leaves.1._.refs_2_.refs_0_), channel_id=1, source_target_pairs={{0,56},{4,60},{8,48},{12,52},{16,40},{20,44},{24,32},{28,36},{32,2... | collective-permute-start | bytes 393224 | tf_op jit(solution)/shard_map/ppermute | solution.py:197
  17.6 11.4 %collective-permute-start.4 = (f32[128,256]{1,0:T(8,128)S(1)}, f32[128,256]{1,0:T(8,128)S(1)}, u32[]{:S(2)}, u32[]{:S(2)}) collective-permute-start(f32[128,256]{1,0:T(8,128)S(1)} %lift_leaves.1._.refs_2_.refs_0_), channel_id=1, source_target_pairs={{0,40},{4,44},{8,32},{12,36},{16,56},{20,60},{24,48},{28,52},{32,8... | collective-permute-start | bytes 393224 | tf_op jit(solution)/shard_map/ppermute | solution.py:197
  18.5 13.4 %collective-permute-start.3 = (f32[128,256]{1,0:T(8,128)S(1)}, f32[128,256]{1,0:T(8,128)S(1)}, u32[]{:S(2)}, u32[]{:S(2)}) collective-permute-start(f32[128,256]{1,0:T(8,128)S(1)} %lift_leaves.1._.refs_2_.refs_0_), channel_id=1, source_target_pairs={{0,16},{4,20},{8,24},{12,28},{16,0},{20,4},{24,8},{28,12},{32,48},... | collective-permute-start | bytes 393224 | tf_op jit(solution)/shard_map/ppermute | solution.py:197
  32.4 8.1 %collective-permute-start.8 = (f32[128,256]{1,0:T(8,128)S(1)}, f32[128,256]{1,0:T(8,128)S(1)}, u32[]{:S(2)}, u32[]{:S(2)}) collective-permute-start(f32[128,256]{1,0:T(8,128)S(1)} %lift_nodes.1), channel_id=1, source_target_pairs={{0,192},{4,196},{8,200},{12,204},{16,208},{20,212},{24,216},{28,22... | collective-permute-start | bytes 393224 | tf_op jit(solution)/shard_map/ppermute | solution.py:197
  35.2 5.3 %collective-permute-start.7 = (f32[128,256]{1,0:T(8,128)S(1)}, f32[128,256]{1,0:T(8,128)S(1)}, u32[]{:S(2)}, u32[]{:S(2)}) collective-permute-start(f32[128,256]{1,0:T(8,128)S(1)} %lift_nodes.1), channel_id=1, source_target_pairs={{0,128},{4,132},{8,136},{12,140},{16,144},{20,148},{24,152},{28,15... | collective-permute-start | bytes 393224 | tf_op jit(solution)/shard_map/ppermute | solution.py:197
  35.7 6.1 %collective-permute-start.6 = (f32[128,256]{1,0:T(8,128)S(1)}, f32[128,256]{1,0:T(8,128)S(1)}, u32[]{:S(2)}, u32[]{:S(2)}) collective-permute-start(f32[128,256]{1,0:T(8,128)S(1)} %lift_nodes.1), channel_id=1, source_target_pairs={{0,64},{4,68},{8,72},{12,76},{16,80},{20,84},{24,88},{28,92},{32,9... | collective-permute-start | bytes 393224 | tf_op jit(solution)/shard_map/ppermute | solution.py:197
  36.6 10.3 %copy-start.2 = (f32[1,1024,256]{2,1,0:T(8,128)S(1)}, f32[1,1024,256]{2,1,0:T(8,128)}, u32[]{:S(2)}) copy-start(f32[1,1024,256]{2,1,0:T(8,128)} %param.8) | copy-start | bytes 3145732
  42.9 4.1 %collective-permute-start.11 = (f32[128,256]{1,0:T(8,128)S(1)}, f32[128,256]{1,0:T(8,128)S(1)}, u32[]{:S(2)}, u32[]{:S(2)}) collective-permute-start(f32[128,256]{1,0:T(8,128)S(1)} %get-tuple-element.40), channel_id=1, source_target_pairs={{0,4},{4,0},{8,12},{12,8},{16,20},{20,16},{24,28},{28,24},{32,36},... | collective-permute-start | bytes 393224 | tf_op jit(solution)/shard_map/ppermute | solution.py:197
  45.2 5.1 %collective-permute-start.10 = (f32[128,256]{1,0:T(8,128)S(1)}, f32[128,256]{1,0:T(8,128)S(1)}, u32[]{:S(2)}, u32[]{:S(2)}) collective-permute-start(f32[128,256]{1,0:T(8,128)S(1)} %get-tuple-element.38), channel_id=1, source_target_pairs={{0,8},{4,12},{8,0},{12,4},{16,24},{20,28},{24,16},{28,20},{32,40},... | collective-permute-start | bytes 393224 | tf_op jit(solution)/shard_map/ppermute | solution.py:197
  45.2 8.0 %collective-permute-start.9 = (f32[128,256]{1,0:T(8,128)S(1)}, f32[128,256]{1,0:T(8,128)S(1)}, u32[]{:S(2)}, u32[]{:S(2)}) collective-permute-start(f32[128,256]{1,0:T(8,128)S(1)} %get-tuple-element.37), channel_id=1, source_target_pairs={{0,12},{4,8},{8,4},{12,0},{16,28},{20,24},{24,20},{28,16},{32,44},... | collective-permute-start | bytes 393224 | tf_op jit(solution)/shard_map/ppermute | solution.py:197

commit v7 on v6

--- a/solution.py
+++ b/solution.py
@@ -129,20 +129,29 @@
     near_rows(dense, 0, dense_held, [sems.at[i] for i in (0, 1)], held, out, own)
 
 
-def near_field(dense, x, _, out, dense_held, sems):
-    half = out.shape[0]
-    near_rows(dense, half, dense_held, [sems.at[i] for i in (0, 1)], x, out)
-
-
-def lift(level, digit, c0, c1, c2, c3, transfers, out):
+def near_below(dense, x, _, out, dense_rest, dense_held, sems):
+    count = out.shape[0]
+    rest = pltpu.make_async_copy(
+        dense.at[pl.ds(dense.shape[0] - count, count)], dense_rest, sems.at[2]
+    )
+    near_rows(dense, 2 * count, dense_held, [sems.at[i] for i in (0, 1)], x, out, rest.start)
+    rest.wait()
+
+
+def near_last(dense, x, out):
+    out[...] = dot(dense[...], x[...], 1, 0)
+
+
+def lift(level, digit, siblings, *refs):
+    *parts, transfers, out = refs
     own = place()[digit]
-    parts = (c0, c1, c2, c3)
-    out[...] = sum(dot(c[...], transfers[level, own ^ j], 1, 0) for j, c in enumerate(parts))
-
-
-def couple(level, digit, c0, c1, c2, c3, couplings, *fields):
+    out[...] = sum(dot(c[...], transfers[level, own ^ j], 1, 0) for j, c in zip(siblings, parts))
+
+
+def couple(level, digit, siblings, *refs):
     own = place()[digit]
-    parts = (c0, c1, c2, c3)
+    parts = dict(zip(siblings, refs))
+    couplings, *fields = refs[len(siblings) :]
     for target, out in enumerate(fields):
         at = own ^ target
         out[...] = sum(
@@ -168,7 +177,7 @@
         out[...] = f[...] + dot(g, leaf_turned[k ^ j], 1, 0)
 
 
-def finish(first, near_above, near_below, row_basis, *rest):
+def finish(first, near_above, near_third, near_fourth, row_basis, *rest):
     out, block, whole, sems = rest[-4:]
     _, m, k, _ = place()
     wide, step = whole.shape[0], rest[0].shape[0]
@@ -183,7 +192,7 @@
     copies = []
     for i in range(CHUNKS):
         at = pl.ds(i * chunk, chunk)
-        near = near_above if 2 * i < CHUNKS else near_below
+        near = (near_above, near_above, near_third, near_fourth)[i]
         part = near[pl.ds(i * chunk % near.shape[0], chunk), columns]
         block[at, :] = part + dot(row_basis[at, :], whole[...], 1, 1)
         copy = pltpu.make_async_copy(block.at[at], out.at[at, columns], sems.at[i])
@@ -233,23 +242,25 @@
     c1 = swap(c1, 1)
     coef = [c0, c1, c2, c3]
     (lifted,) = run(
-        functools.partial(lift, 0, 2),
+        functools.partial(lift, 0, 2, range(4)),
         [*coef, transfers],
         [(quarter, rank)],
         "lift_leaves",
         unit * columns,
     )
-    node_coef = [lifted] + [swap(lifted, bits) for bits in (4, 10, 14)]
-    near_below = pl.pallas_call(
-        near_field,
-        out_shape=pltpu.VMEM(half_rows, F32),
+    nodes = (0, 2, 3, 1)
+    node_coef = [swap(lifted, (j << 2) | (j & 2)) if j else lifted for j in nodes]
+    part_rows = (users // 4, columns)
+    near_third, dense_rest = pl.pallas_call(
+        near_below,
+        out_shape=[pltpu.VMEM(part_rows, F32), pltpu.VMEM((users // 4, users), F32)],
         in_specs=[ANY, VMEM, ANY],
-        out_specs=VMEM,
-        scratch_shapes=dense_half,
-        **settings(3 * users * users * columns, users * users, "near_field"),
+        out_specs=[VMEM] * 2,
+        scratch_shapes=[pltpu.VMEM((users // 4, users), F32), pltpu.SemaphoreType.DMA((3,))],
+        **settings(users * users * columns, users * users, "near_below"),
     )(*in_hbm([dense]), *in_vmem([held]), lifted)
     leaf_fields = run(
-        functools.partial(couple, 0, 2),
+        functools.partial(couple, 0, 2, range(4)),
         [*coef, couplings],
         [(quarter, rank)] * 4,
         "couple_leaves",
@@ -264,16 +275,16 @@
         after=[lifted],
     )
     (crown,) = run(
-        functools.partial(lift, 1, 1),
+        functools.partial(lift, 1, 1, nodes),
         [*node_coef, transfers],
         [(quarter, rank)],
         "lift_nodes",
         unit * columns,
-        after=[*leaf_fields, near_below, turned[1]],
+        after=[*leaf_fields, near_third, turned[1]],
     )
     top_coef = [swap(crown, bits) for bits in (16, 32, 48)]
     (node_field,) = run(
-        functools.partial(couple, 1, 1),
+        functools.partial(couple, 1, 1, nodes),
         [*node_coef, couplings],
         [(quarter, rank)],
         "couple_nodes",
@@ -286,6 +297,15 @@
         "descend",
         unit * 8 * quarter,
     )
+    (near_fourth,) = run(
+        near_last,
+        [dense_rest, held],
+        [part_rows],
+        "near_last",
+        3 * users * users * columns,
+        after=[g0],
+    )
+    nears = [near_above, near_third, near_fourth]
     g2, g3, g1 = swap(g2, 2), swap(g3, 3), swap(g1, 1)
 
     def write(first, pieces, out):
@@ -293,16 +313,16 @@
         return pl.pallas_call(
             functools.partial(finish, first),
             out_shape=pltpu.HBM((users, columns), F32),
-            in_specs=[VMEM] * (3 + len(pieces)) + [ANY] * len(out),
+            in_specs=[VMEM] * (4 + len(pieces)) + [ANY] * len(out),
             out_specs=ANY,
             scratch_shapes=[
                 pltpu.VMEM((users, wide), F32),
                 pltpu.VMEM((wide, rank), F32),
                 pltpu.SemaphoreType.DMA((CHUNKS,)),
             ],
-            input_output_aliases={3 + len(pieces): 0} if out else {},
+            input_output_aliases={4 + len(pieces): 0} if out else {},
             **settings(6 * users * rank * wide, users * wide, "finish_%d" % first),
-        )(*in_vmem([near_above, near_below, rbasis, *pieces]), *out)
+        )(*in_vmem([*nears, rbasis, *pieces]), *out)
 
     out = write(0, [g0, g1], [])
     out = write(2, [g2], [out])

time: 54.8 us -> 54 us (0.985)
  waiting for transfers between devices: 16.5 us -> 13.5 us
  starting transfers between devices: 19.1 us -> 21.1 us
    ppermute x12, waiting for transfers between devices: 16.5 us -> 13.5 us  [swap(): lax.ppermute(block, 'leaf', [(i, i ^ bits) for i in range(lax.axis_size('...]
    ppermute x12, starting transfers between devices: 19.1 us -> 21.1 us  [swap(): lax.ppermute(block, 'leaf', [(i, i ^ bits) for i in range(lax.axis_size('...]
    pallas_call x6 -> x7, Pallas kernels: 4.73 us -> 5.84 us  [run(): pl.pallas_call(kernel, out_shape=[pltpu.VMEM(shape, F32) for shape in out...]
    pallas_call x1, Pallas kernels: 3.45 us -> 2.37 us  [local(): pl.pallas_call(near_below, out_shape=[pltpu.VMEM(part_rows, F32), pltpu.V...]
  transfers between devices with their start and end apart: 12 -> 12, of which waited for: 10 -> 7; matrix products, arithmetic and copies ran while one was open for 0% -> 0% of each run, Pallas kernels for 24% -> 24%
where the time goes in v7:
time: 54 us; the launch traced here: 53.9 us
  starting transfers between devices  21.1 us (39%)
  Pallas kernels  18.8 us (35%)
  waiting for transfers between devices  13.5 us (25%)
    ppermute x12, starting transfers between devices, swap(): lax.ppermute(block, 'leaf', [(i, i ^ bits) for i in range(lax.axis_size('...  21.1 us
    ppermute x12, waiting for transfers between devices, swap(): lax.ppermute(block, 'leaf', [(i, i ^ bits) for i in range(lax.axis_size('...  13.5 us
    pallas_call x7, Pallas kernels, run(): pl.pallas_call(kernel, out_shape=[pltpu.VMEM(shape, F32) for shape in out...  5.84 us
    pallas_call x1, Pallas kernels, local(): pl.pallas_call(own_and_near, out_shape=[pltpu.VMEM(shape, F32) for shape...  4.08 us
    pallas_call x3, Pallas kernels, write(): pl.pallas_call(functools.partial(finish, first), out_shape=pltpu.HBM((use...  4.05 us
    pallas_call x1, Pallas kernels, local(): pl.pallas_call(far_coefficients, out_shape=[pltpu.VMEM(shape, F32) for sh...  2.49 us
    pallas_call x1, Pallas kernels, local(): pl.pallas_call(near_below, out_shape=[pltpu.VMEM(part_rows, F32), pltpu.V...  2.37 us
  transfers between devices with their start and end apart: 12, of which 7 were waited for; matrix products, arithmetic and copies ran while one was open for 0% of the time, Pallas kernels for 24%

profile of v7, /device:TPU:1, one launch (start us, length us, event | category | flops | bytes accessed | tf_op | source)
XLA Modules:
  0.0 53.9 jit_solution(10311029048288031135)
XLA Ops:
  0.0 2.5 %far_coefficients.1 = (f32[128,256]{1,0:T(8,128)S(1)}, f32[128,256]{1,0:T(8,128)S(1)}, f32[1024,512]{1,0:T(8,128)S(1)}, f32[1024,256]{1,0:T(8,128)S(1)}) custom-call(f32[1024,512]{1,0:T(8,128)} %x.1, f32[1024,256]{1,0:T(8,128)} %bitcast.8), custom_call_target="tpu_custom_call" | custom-call | flops 402653184 | bytes 2097152 | tf_op jit(solution)/shard_map/far_coefficients/pallas_call | solution.py:216
  2.5 2.5 %collective-permute-start.1 = (f32[128,256]{1,0:T(8,128)S(1)}, f32[128,256]{1,0:T(8,128)S(1)}, u32[]{:S(2)}, u32[]{:S(2)}) collective-permute-start(f32[128,256]{1,0:T(8,128)S(1)} %get-tuple-element.30), channel_id=1, source_target_pairs={{0,8},{4,12},{8,0},{12,4},{16,24},{20,28},{24,16},{28,20},{32,40},... | collective-permute-start | bytes 393224 | tf_op jit(solution)/shard_map/ppermute | solution.py:206
  5.0 2.4 %collective-permute-start.2 = (f32[128,256]{1,0:T(8,128)S(1)}, f32[128,256]{1,0:T(8,128)S(1)}, u32[]{:S(2)}, u32[]{:S(2)}) collective-permute-start(f32[128,256]{1,0:T(8,128)S(1)} %get-tuple-element.31), channel_id=1, source_target_pairs={{0,12},{4,8},{8,4},{12,0},{16,28},{20,24},{24,20},{28,16},{32,44},... | collective-permute-start | bytes 393224 | tf_op jit(solution)/shard_map/ppermute | solution.py:206
  7.5 4.1 %own_and_near.1 = (f32[128,256]{1,0:T(8,128)S(1)}, f32[128,256]{1,0:T(8,128)S(1)}, f32[512,512]{1,0:T(8,128)S(1)}) custom-call(f32[1024,512]{1,0:T(8,128)S(1)} %get-tuple-element.25.held.x.refs_1_, f32[1024,256]{1,0:T(8,128)S(1)} %get-tuple-element.26.basis_held, f32[1024,1024]{1,0:T(8,128)} %bitcast.6), custom_call_target="tpu_custom_call" | custom-call | flops 1610612736 | bytes 4194304 | tf_op jit(solution)/shard_map/own_and_near/pallas_call | solution.py:234
  11.5 0.1 collective-permute-start
  11.7 0.8 %collective-permute-done.2.refs_3_ = f32[128,256]{1,0:T(8,128)S(1)} collective-permute-done((f32[128,256]{1,0:T(8,128)S(1)}, f32[128,256]{1,0:T(8,128)S(1)}, u32[]{:S(2)}, u32[]{:S(2)}) %collective-permute-start.2) | collective-permute-done | bytes 131104 | tf_op jit(solution)/shard_map/ppermute | solution.py:206
  12.5 0.5 collective-permute-done.refs_1_
  13.0 0.4 lift_leaves.1._.refs_2_.refs_0_
  13.4 1.7 %collective-permute-start.5 = (f32[128,256]{1,0:T(8,128)S(1)}, f32[128,256]{1,0:T(8,128)S(1)}, u32[]{:S(2)}, u32[]{:S(2)}) collective-permute-start(f32[128,256]{1,0:T(8,128)S(1)} %lift_leaves.1._.refs_2_.refs_0_), channel_id=1, source_target_pairs={{0,16},{4,20},{8,24},{12,28},{16,0},{20,4},{24,8},{28,12},{32,48},... | collective-permute-start | bytes 393224 | tf_op jit(solution)/shard_map/ppermute | solution.py:206
  15.1 3.6 %collective-permute-start.4 = (f32[128,256]{1,0:T(8,128)S(1)}, f32[128,256]{1,0:T(8,128)S(1)}, u32[]{:S(2)}, u32[]{:S(2)}) collective-permute-start(f32[128,256]{1,0:T(8,128)S(1)} %lift_leaves.1._.refs_2_.refs_0_), channel_id=1, source_target_pairs={{0,56},{4,60},{8,48},{12,52},{16,40},{20,44},{24,32},{28,36},{32,2... | collective-permute-start | bytes 393224 | tf_op jit(solution)/shard_map/ppermute | solution.py:206
  18.7 0.9 %collective-permute-start.3 = (f32[128,256]{1,0:T(8,128)S(1)}, f32[128,256]{1,0:T(8,128)S(1)}, u32[]{:S(2)}, u32[]{:S(2)}) collective-permute-start(f32[128,256]{1,0:T(8,128)S(1)} %lift_leaves.1._.refs_2_.refs_0_), channel_id=1, source_target_pairs={{0,40},{4,44},{8,32},{12,36},{16,56},{20,60},{24,48},{28,52},{32,8... | collective-permute-start | bytes 393224 | tf_op jit(solution)/shard_map/ppermute | solution.py:206
  19.6 2.4 %near_below.1 = (f32[256,512]{1,0:T(8,128)S(1)}, f32[256,1024]{1,0:T(8,128)S(1)}) custom-call(f32[1024,1024]{1,0:T(8,128)} %bitcast.7, f32[1024,512]{1,0:T(8,128)S(1)} %get-tuple-element.25.held.x.refs_1_, f32[128,256]{1,0:T(8,128)S(1)} %lift_leaves.1._.refs_2_.refs_0_), custom_call_target="tpu_custom_call" | custom-call | flops 536870912 | bytes 4194304 | tf_op jit(solution)/shard_map/near_below/pallas_call | solution.py:254
  22.0 1.7 %couple_leaves.1 = (f32[128,256]{1,0:T(8,128)S(1)}, f32[128,256]{1,0:T(8,128)S(1)}, f32[128,256]{1,0:T(8,128)S(1)}, f32[128,256]{1,0:T(8,128)S(1)}) custom-call(f32[128,256]{1,0:T(8,128)S(1)} %get-tuple-element.28.refs_0_, f32[128,256]{1,0:T(8,128)S(1)} %collective-permute-done.refs_1_, f32[128,256]{1,0:T(8,128)S(1)} %collective-permute-done.1.refs_2_, ...), custom_call_target="tpu_custom_call" | custom-call | flops 603979776 | bytes 2883584 | tf_op jit(solution)/shard_map/couple_leaves/pallas_call | solution.py:45
  23.7 0.6 %turn.1 = (f32[3,256,256]{2,1,0:T(8,128)S(1)}, f32[256,256]{1,0:T(8,128)S(1)}, f32[4,256,256]{2,1,0:T(8,128)S(1)}) custom-call(f32[3,3,256,256]{3,2,1,0:T(8,128)S(1)} %copy-done, f32[2,4,256,256]{3,2,1,0:T(8,128)S(1)} %copy-done.1, f32[128,256]{1,0:T(8,128)S(1)} %lift_leaves.1._.refs_2_.refs_0_), custom_call_target="tpu_custom_call" | custom-call | flops 805306368 | bytes 4456448 | tf_op jit(solution)/shard_map/turn/pallas_call | solution.py:45
  24.3 0.9 %collective-permute-done.4.refs_2_ = f32[128,256]{1,0:T(8,128)S(1)} collective-permute-done((f32[128,256]{1,0:T(8,128)S(1)}, f32[128,256]{1,0:T(8,128)S(1)}, u32[]{:S(2)}, u32[]{:S(2)}) %collective-permute-start.4) | collective-permute-done | bytes 131104 | tf_op jit(solution)/shard_map/ppermute | solution.py:206
  25.3 4.6 %collective-permute-done.3.refs_1_ = f32[128,256]{1,0:T(8,128)S(1)} collective-permute-done((f32[128,256]{1,0:T(8,128)S(1)}, f32[128,256]{1,0:T(8,128)S(1)}, u32[]{:S(2)}, u32[]{:S(2)}) %collective-permute-start.3) | collective-permute-done | bytes 131104 | tf_op jit(solution)/shard_map/ppermute | solution.py:206
  29.8 0.4 lift_nodes.1
  30.3 2.8 %collective-permute-start.8 = (f32[128,256]{1,0:T(8,128)S(1)}, f32[128,256]{1,0:T(8,128)S(1)}, u32[]{:S(2)}, u32[]{:S(2)}) collective-permute-start(f32[128,256]{1,0:T(8,128)S(1)} %lift_nodes.1), channel_id=1, source_target_pairs={{0,192},{4,196},{8,200},{12,204},{16,208},{20,212},{24,216},{28,22... | collective-permute-start | bytes 393224 | tf_op jit(solution)/shard_map/ppermute | solution.py:206
  33.1 0.4 collective-permute-start.7
  33.4 0.3 collective-permute-start.6
  33.8 0.6 %couple_nodes.1.refs_6_ = f32[128,256]{1,0:T(8,128)S(1)} custom-call(f32[128,256]{1,0:T(8,128)S(1)} %lift_leaves.1._.refs_2_.refs_0_, f32[128,256]{1,0:T(8,128)S(1)} %collective-permute-done.3.refs_1_, f32[128,256]{1,0:T(8,128)S(1)} %collective-permute-done.4.refs_2_, f32[128,256]{1,0:T(8,128)S(1)} %collective-permute-done.5.refs_3_, ...), custom_call_target="tpu_custom_call" | custom-call | flops 150994944 | bytes 2883584 | tf_op jit(solution)/shard_map/couple_nodes/pallas_call | solution.py:45
  34.3 4.2 %collective-permute-done.8.refs_2_ = f32[128,256]{1,0:T(8,128)S(1)} collective-permute-done((f32[128,256]{1,0:T(8,128)S(1)}, f32[128,256]{1,0:T(8,128)S(1)}, u32[]{:S(2)}, u32[]{:S(2)}) %collective-permute-start.8) | collective-permute-done | bytes 131104 | tf_op jit(solution)/shard_map/ppermute | solution.py:206
  38.5 0.2 collective-permute-done.6.refs_0_
  38.7 1.1 %descend.1 = (f32[128,256]{1,0:T(8,128)S(1)}, f32[128,256]{1,0:T(8,128)S(1)}, f32[128,256]{1,0:T(8,128)S(1)}, f32[128,256]{1,0:T(8,128)S(1)}) custom-call(f32[128,256]{1,0:T(8,128)S(1)} %collective-permute-done.6.refs_0_, f32[128,256]{1,0:T(8,128)S(1)} %collective-permute-done.7.refs_1_, f32[128,256]{1,0:T(8,128)S(1)} %collective-permute-done.8.refs_2_, ...), custom_call_target="tpu_custom_call" | custom-call | flops 402653184 | bytes 3145728 | tf_op jit(solution)/shard_map/descend/pallas_call | solution.py:45
  39.8 5.8 %collective-permute-start.9 = (f32[128,256]{1,0:T(8,128)S(1)}, f32[128,256]{1,0:T(8,128)S(1)}, u32[]{:S(2)}, u32[]{:S(2)}) collective-permute-start(f32[128,256]{1,0:T(8,128)S(1)} %get-tuple-element.42), channel_id=1, source_target_pairs={{0,12},{4,8},{8,4},{12,0},{16,28},{20,24},{24,20},{28,16},{32,44},... | collective-permute-start | bytes 393224 | tf_op jit(solution)/shard_map/ppermute | solution.py:206
  45.6 0.5 collective-permute-start.11
  46.1 1.1 %near_last.1.near_fourth = f32[256,512]{1,0:T(8,128)S(1)} custom-call(f32[256,1024]{1,0:T(8,128)S(1)} %get-tuple-element.33.refs_0_, f32[1024,512]{1,0:T(8,128)S(1)} %get-tuple-element.25.held.x.refs_1_, f32[128,256]{1,0:T(8,128)S(1)} %get-tuple-element.41.refs_2_.rest_0_), custom_call_target="tpu_custom_call" | custom-call | flops 1610612736 | bytes 3145728 | tf_op jit(solution)/shard_map/near_last/pallas_call | solution.py:45
  47.2 0.1 copy-done.2
  47.3 1.5 %finish_0.1.rest_1_ = f32[1024,512]{1,0:T(8,128)} custom-call(f32[512,512]{1,0:T(8,128)S(1)} %get-tuple-element.27.near_above, f32[256,512]{1,0:T(8,128)S(1)} %get-tuple-element.32.refs_9_.near_third, f32[256,512]{1,0:T(8,128)S(1)} %near_last.1.near_fourth, f32[1024,256]{1,0:T(8,128)S(1)} %bitcast.3, f32[128,256]{1,0:T(8,128)S(1)} %get-tuple-element.41.refs_2_.rest_0_, ...), custom_call_target="tpu_custom_call" | custom-call | flops 402653184 | bytes 1048576 | tf_op jit(solution)/shard_map/finish_0/pallas_call | solution.py:313
  48.9 2.3 %collective-permute-done.10.rest_0_ = f32[128,256]{1,0:T(8,128)S(1)} collective-permute-done((f32[128,256]{1,0:T(8,128)S(1)}, f32[128,256]{1,0:T(8,128)S(1)}, u32[]{:S(2)}, u32[]{:S(2)}) %collective-permute-start.10) | collective-permute-done | bytes 131104 | tf_op jit(solution)/shard_map/ppermute | solution.py:206
  51.2 1.3 %finish_2.1.rest_1_ = f32[1024,512]{1,0:T(8,128)} custom-call(f32[512,512]{1,0:T(8,128)S(1)} %get-tuple-element.27.near_above, f32[256,512]{1,0:T(8,128)S(1)} %get-tuple-element.32.refs_9_.near_third, f32[256,512]{1,0:T(8,128)S(1)} %near_last.1.near_fourth, f32[1024,256]{1,0:T(8,128)S(1)} %bitcast.4, ...), custom_call_target="tpu_custom_call", output_to_operand_aliasing={{}: (5, {})} | custom-call | flops 201326592 | bytes 524288 | tf_op jit(solution)/shard_map/finish_2/pallas_call | solution.py:313
  52.5 1.3 %finish_3.1 = f32[1024,512]{1,0:T(8,128)} custom-call(f32[512,512]{1,0:T(8,128)S(1)} %get-tuple-element.27.near_above, f32[256,512]{1,0:T(8,128)S(1)} %get-tuple-element.32.refs_9_.near_third, f32[256,512]{1,0:T(8,128)S(1)} %near_last.1.near_fourth, f32[1024,256]{1,0:T(8,128)S(1)} %bitcast.5, ...), custom_call_target="tpu_custom_call", output_to_operand_aliasing={{}: (5, {})} | custom-call | flops 201326592 | bytes 524288 | tf_op jit(solution)/shard_map/finish_3/pallas_call | solution.py:313
  (11 shorter events, 0.0 us)
Async XLA Ops:
  2.5 9.2 %collective-permute-start.1 = (f32[128,256]{1,0:T(8,128)S(1)}, f32[128,256]{1,0:T(8,128)S(1)}, u32[]{:S(2)}, u32[]{:S(2)}) collective-permute-start(f32[128,256]{1,0:T(8,128)S(1)} %get-tuple-element.30), channel_id=1, source_target_pairs={{0,8},{4,12},{8,0},{12,4},{16,24},{20,28},{24,16},{28,20},{32,40},... | collective-permute-start | bytes 393224 | tf_op jit(solution)/shard_map/ppermute | solution.py:206
  5.0 7.5 %collective-permute-start.2 = (f32[128,256]{1,0:T(8,128)S(1)}, f32[128,256]{1,0:T(8,128)S(1)}, u32[]{:S(2)}, u32[]{:S(2)}) collective-permute-start(f32[128,256]{1,0:T(8,128)S(1)} %get-tuple-element.31), channel_id=1, source_target_pairs={{0,12},{4,8},{8,4},{12,0},{16,28},{20,24},{24,20},{28,16},{32,44},... | collective-permute-start | bytes 393224 | tf_op jit(solution)/shard_map/ppermute | solution.py:206
  7.5 5.5 %copy-start.1 = (f32[2,4,256,256]{3,2,1,0:T(8,128)S(1)}, f32[2,4,256,256]{3,2,1,0:T(8,128)}, u32[]{:S(2)}) copy-start(f32[2,4,256,256]{3,2,1,0:T(8,128)} %refs_4_.6) | copy-start | bytes 6291460
  11.5 1.4 %collective-permute-start = (f32[128,256]{1,0:T(8,128)S(1)}, f32[128,256]{1,0:T(8,128)S(1)}, u32[]{:S(2)}, u32[]{:S(2)}) collective-permute-start(f32[128,256]{1,0:T(8,128)S(1)} %get-tuple-element.29), channel_id=1, source_target_pairs={{0,4},{4,0},{8,12},{12,8},{16,20},{20,16},{24,28},{28,24},{32,36},... | collective-permute-start | bytes 393224 | tf_op jit(solution)/shard_map/ppermute | solution.py:206
  13.4 8.6 %copy-start = (f32[3,3,256,256]{3,2,1,0:T(8,128)S(1)}, f32[3,3,256,256]{3,2,1,0:T(8,128)}, u32[]{:S(2)}) copy-start(f32[3,3,256,256]{3,2,1,0:T(8,128)} %refs_4_.7) | copy-start | bytes 7077892
  13.4 10.9 %collective-permute-start.5 = (f32[128,256]{1,0:T(8,128)S(1)}, f32[128,256]{1,0:T(8,128)S(1)}, u32[]{:S(2)}, u32[]{:S(2)}) collective-permute-start(f32[128,256]{1,0:T(8,128)S(1)} %lift_leaves.1._.refs_2_.refs_0_), channel_id=1, source_target_pairs={{0,16},{4,20},{8,24},{12,28},{16,0},{20,4},{24,8},{28,12},{32,48},... | collective-permute-start | bytes 393224 | tf_op jit(solution)/shard_map/ppermute | solution.py:206
  15.1 10.1 %collective-permute-start.4 = (f32[128,256]{1,0:T(8,128)S(1)}, f32[128,256]{1,0:T(8,128)S(1)}, u32[]{:S(2)}, u32[]{:S(2)}) collective-permute-start(f32[128,256]{1,0:T(8,128)S(1)} %lift_leaves.1._.refs_2_.refs_0_), channel_id=1, source_target_pairs={{0,56},{4,60},{8,48},{12,52},{16,40},{20,44},{24,32},{28,36},{32,2... | collective-permute-start | bytes 393224 | tf_op jit(solution)/shard_map/ppermute | solution.py:206
  18.7 11.1 %collective-permute-start.3 = (f32[128,256]{1,0:T(8,128)S(1)}, f32[128,256]{1,0:T(8,128)S(1)}, u32[]{:S(2)}, u32[]{:S(2)}) collective-permute-start(f32[128,256]{1,0:T(8,128)S(1)} %lift_leaves.1._.refs_2_.refs_0_), channel_id=1, source_target_pairs={{0,40},{4,44},{8,32},{12,36},{16,56},{20,60},{24,48},{28,52},{32,8... | collective-permute-start | bytes 393224 | tf_op jit(solution)/shard_map/ppermute | solution.py:206
  30.3 8.3 %collective-permute-start.8 = (f32[128,256]{1,0:T(8,128)S(1)}, f32[128,256]{1,0:T(8,128)S(1)}, u32[]{:S(2)}, u32[]{:S(2)}) collective-permute-start(f32[128,256]{1,0:T(8,128)S(1)} %lift_nodes.1), channel_id=1, source_target_pairs={{0,192},{4,196},{8,200},{12,204},{16,208},{20,212},{24,216},{28,22... | collective-permute-start | bytes 393224 | tf_op jit(solution)/shard_map/ppermute | solution.py:206
  33.1 5.4 %collective-permute-start.7 = (f32[128,256]{1,0:T(8,128)S(1)}, f32[128,256]{1,0:T(8,128)S(1)}, u32[]{:S(2)}, u32[]{:S(2)}) collective-permute-start(f32[128,256]{1,0:T(8,128)S(1)} %lift_nodes.1), channel_id=1, source_target_pairs={{0,128},{4,132},{8,136},{12,140},{16,144},{20,148},{24,152},{28,15... | collective-permute-start | bytes 393224 | tf_op jit(solution)/shard_map/ppermute | solution.py:206
  33.4 5.3 %collective-permute-start.6 = (f32[128,256]{1,0:T(8,128)S(1)}, f32[128,256]{1,0:T(8,128)S(1)}, u32[]{:S(2)}, u32[]{:S(2)}) collective-permute-start(f32[128,256]{1,0:T(8,128)S(1)} %lift_nodes.1), channel_id=1, source_target_pairs={{0,64},{4,68},{8,72},{12,76},{16,80},{20,84},{24,88},{28,92},{32,9... | collective-permute-start | bytes 393224 | tf_op jit(solution)/shard_map/ppermute | solution.py:206
  39.8 12.7 %collective-permute-start.9 = (f32[128,256]{1,0:T(8,128)S(1)}, f32[128,256]{1,0:T(8,128)S(1)}, u32[]{:S(2)}, u32[]{:S(2)}) collective-permute-start(f32[128,256]{1,0:T(8,128)S(1)} %get-tuple-element.42), channel_id=1, source_target_pairs={{0,12},{4,8},{8,4},{12,0},{16,28},{20,24},{24,20},{28,16},{32,44},... | collective-permute-start | bytes 393224 | tf_op jit(solution)/shard_map/ppermute | solution.py:206
  45.6 5.5 %collective-permute-start.10 = (f32[128,256]{1,0:T(8,128)S(1)}, f32[128,256]{1,0:T(8,128)S(1)}, u32[]{:S(2)}, u32[]{:S(2)}) collective-permute-start(f32[128,256]{1,0:T(8,128)S(1)} %get-tuple-element.43), channel_id=1, source_target_pairs={{0,8},{4,12},{8,0},{12,4},{16,24},{20,28},{24,16},{28,20},{32,40},... | collective-permute-start | bytes 393224 | tf_op jit(solution)/shard_map/ppermute | solution.py:206
  45.6 1.6 %collective-permute-start.11 = (f32[128,256]{1,0:T(8,128)S(1)}, f32[128,256]{1,0:T(8,128)S(1)}, u32[]{:S(2)}, u32[]{:S(2)}) collective-permute-start(f32[128,256]{1,0:T(8,128)S(1)} %get-tuple-element.44), channel_id=1, source_target_pairs={{0,4},{4,0},{8,12},{12,8},{16,20},{20,16},{24,28},{28,24},{32,36},... | collective-permute-start | bytes 393224 | tf_op jit(solution)/shard_map/ppermute | solution.py:206
  46.1 1.2 %copy-start.2 = (f32[1,1024,256]{2,1,0:T(8,128)S(1)}, f32[1,1024,256]{2,1,0:T(8,128)}, u32[]{:S(2)}) copy-start(f32[1,1024,256]{2,1,0:T(8,128)} %param.8) | copy-start | bytes 3145732

commit v8 on v7

--- a/solution.py
+++ b/solution.py
@@ -168,7 +168,7 @@
         leaf_turned[i] = transfers[0, i].T
 
 
-def descend(c1, c2, c3, top_turned, node_turned, leaf_turned, field, f0, f1, f2, f3, *outs):
+def descend(c1, c3, c2, top_turned, node_turned, leaf_turned, field, f0, f1, f2, f3, *outs):
     r, _, k, _ = place()
     parts = (c1, c2, c3)
     g = sum(dot(c[...], top_turned[offset(r ^ d, r)], 1, 0) for d, c in zip((1, 2, 3), parts))
@@ -282,7 +282,7 @@
         unit * columns,
         after=[*leaf_fields, near_third, turned[1]],
     )
-    top_coef = [swap(crown, bits) for bits in (16, 32, 48)]
+    top_coef = [swap(crown, bits) for bits in (16, 48, 32)]
     (node_field,) = run(
         functools.partial(couple, 1, 1, nodes),
         [*node_coef, couplings],
@@ -325,8 +325,7 @@
         )(*in_vmem([*nears, rbasis, *pieces]), *out)
 
     out = write(0, [g0, g1], [])
-    out = write(2, [g2], [out])
-    return write(3, [g3], [out])
+    return write(2, [g2, g3], [out])
 
 
 def solution(mesh):

time: 54 us -> 52.1 us (0.965)
  starting transfers between devices: 21.1 us -> 19.5 us
  Pallas kernels: 18.8 us -> 17.8 us
  waiting for transfers between devices: 13.5 us -> 14.2 us
    ppermute x12, starting transfers between devices: 21.1 us -> 19.5 us  [swap(): lax.ppermute(block, 'leaf', [(i, i ^ bits) for i in range(lax.axis_size('...]
    pallas_call x3 -> x2, Pallas kernels: 4.05 us -> 3.01 us  [write(): pl.pallas_call(functools.partial(finish, first), out_shape=pltpu.HBM((use...]
    ppermute x12, waiting for transfers between devices: 13.5 us -> 14.2 us  [swap(): lax.ppermute(block, 'leaf', [(i, i ^ bits) for i in range(lax.axis_size('...]
  transfers between devices with their start and end apart: 12 -> 12, of which waited for: 7 -> 8; matrix products, arithmetic and copies ran while one was open for 0% -> 0% of each run, Pallas kernels for 24% -> 23%
where the time goes in v8:
time: 52.1 us; the launch traced here: 52 us
  starting transfers between devices  19.5 us (37%)
  Pallas kernels  17.8 us (34%)
  waiting for transfers between devices  14.2 us (27%)
    ppermute x12, starting transfers between devices, swap(): lax.ppermute(block, 'leaf', [(i, i ^ bits) for i in range(lax.axis_size('...  19.5 us
    ppermute x12, waiting for transfers between devices, swap(): lax.ppermute(block, 'leaf', [(i, i ^ bits) for i in range(lax.axis_size('...  14.2 us
    pallas_call x7, Pallas kernels, run(): pl.pallas_call(kernel, out_shape=[pltpu.VMEM(shape, F32) for shape in out...  5.84 us
    pallas_call x1, Pallas kernels, local(): pl.pallas_call(own_and_near, out_shape=[pltpu.VMEM(shape, F32) for shape...  4.08 us
    pallas_call x2, Pallas kernels, write(): pl.pallas_call(functools.partial(finish, first), out_shape=pltpu.HBM((use...  3.01 us
    pallas_call x1, Pallas kernels, local(): pl.pallas_call(far_coefficients, out_shape=[pltpu.VMEM(shape, F32) for sh...  2.49 us
    pallas_call x1, Pallas kernels, local(): pl.pallas_call(near_below, out_shape=[pltpu.VMEM(part_rows, F32), pltpu.V...  2.37 us
  transfers between devices with their start and end apart: 12, of which 8 were waited for; matrix products, arithmetic and copies ran while one was open for 0% of the time, Pallas kernels for 23%

profile of v8, /device:TPU:1, one launch (start us, length us, event | category | flops | bytes accessed | tf_op | source)
XLA Modules:
  0.0 52.0 jit_solution(449893383822647077)
XLA Ops:
  0.0 2.5 %far_coefficients.1 = (f32[128,256]{1,0:T(8,128)S(1)}, f32[128,256]{1,0:T(8,128)S(1)}, f32[1024,512]{1,0:T(8,128)S(1)}, f32[1024,256]{1,0:T(8,128)S(1)}) custom-call(f32[1024,512]{1,0:T(8,128)} %x.1, f32[1024,256]{1,0:T(8,128)} %bitcast.7), custom_call_target="tpu_custom_call" | custom-call | flops 402653184 | bytes 2097152 | tf_op jit(solution)/shard_map/far_coefficients/pallas_call | solution.py:216
  2.5 2.5 %collective-permute-start.1 = (f32[128,256]{1,0:T(8,128)S(1)}, f32[128,256]{1,0:T(8,128)S(1)}, u32[]{:S(2)}, u32[]{:S(2)}) collective-permute-start(f32[128,256]{1,0:T(8,128)S(1)} %get-tuple-element.30), channel_id=1, source_target_pairs={{0,8},{4,12},{8,0},{12,4},{16,24},{20,28},{24,16},{28,20},{32,40},... | collective-permute-start | bytes 393224 | tf_op jit(solution)/shard_map/ppermute | solution.py:206
  5.0 2.4 %collective-permute-start.2 = (f32[128,256]{1,0:T(8,128)S(1)}, f32[128,256]{1,0:T(8,128)S(1)}, u32[]{:S(2)}, u32[]{:S(2)}) collective-permute-start(f32[128,256]{1,0:T(8,128)S(1)} %get-tuple-element.31), channel_id=1, source_target_pairs={{0,12},{4,8},{8,4},{12,0},{16,28},{20,24},{24,20},{28,16},{32,44},... | collective-permute-start | bytes 393224 | tf_op jit(solution)/shard_map/ppermute | solution.py:206
  7.5 4.1 %own_and_near.1 = (f32[128,256]{1,0:T(8,128)S(1)}, f32[128,256]{1,0:T(8,128)S(1)}, f32[512,512]{1,0:T(8,128)S(1)}) custom-call(f32[1024,512]{1,0:T(8,128)S(1)} %get-tuple-element.25.held.x.refs_1_, f32[1024,256]{1,0:T(8,128)S(1)} %get-tuple-element.26.basis_held, f32[1024,1024]{1,0:T(8,128)} %bitcast.5), custom_call_target="tpu_custom_call" | custom-call | flops 1610612736 | bytes 4194304 | tf_op jit(solution)/shard_map/own_and_near/pallas_call | solution.py:234
  11.5 0.1 collective-permute-start
  11.7 0.8 %collective-permute-done.2.refs_3_ = f32[128,256]{1,0:T(8,128)S(1)} collective-permute-done((f32[128,256]{1,0:T(8,128)S(1)}, f32[128,256]{1,0:T(8,128)S(1)}, u32[]{:S(2)}, u32[]{:S(2)}) %collective-permute-start.2) | collective-permute-done | bytes 131104 | tf_op jit(solution)/shard_map/ppermute | solution.py:206
  12.5 0.5 collective-permute-done.refs_1_
  13.0 0.4 lift_leaves.1._.refs_2_.refs_0_
  13.4 1.7 %collective-permute-start.5 = (f32[128,256]{1,0:T(8,128)S(1)}, f32[128,256]{1,0:T(8,128)S(1)}, u32[]{:S(2)}, u32[]{:S(2)}) collective-permute-start(f32[128,256]{1,0:T(8,128)S(1)} %lift_leaves.1._.refs_2_.refs_0_), channel_id=1, source_target_pairs={{0,16},{4,20},{8,24},{12,28},{16,0},{20,4},{24,8},{28,12},{32,48},... | collective-permute-start | bytes 393224 | tf_op jit(solution)/shard_map/ppermute | solution.py:206
  15.1 3.6 %collective-permute-start.4 = (f32[128,256]{1,0:T(8,128)S(1)}, f32[128,256]{1,0:T(8,128)S(1)}, u32[]{:S(2)}, u32[]{:S(2)}) collective-permute-start(f32[128,256]{1,0:T(8,128)S(1)} %lift_leaves.1._.refs_2_.refs_0_), channel_id=1, source_target_pairs={{0,56},{4,60},{8,48},{12,52},{16,40},{20,44},{24,32},{28,36},{32,2... | collective-permute-start | bytes 393224 | tf_op jit(solution)/shard_map/ppermute | solution.py:206
  18.7 0.9 %collective-permute-start.3 = (f32[128,256]{1,0:T(8,128)S(1)}, f32[128,256]{1,0:T(8,128)S(1)}, u32[]{:S(2)}, u32[]{:S(2)}) collective-permute-start(f32[128,256]{1,0:T(8,128)S(1)} %lift_leaves.1._.refs_2_.refs_0_), channel_id=1, source_target_pairs={{0,40},{4,44},{8,32},{12,36},{16,56},{20,60},{24,48},{28,52},{32,8... | collective-permute-start | bytes 393224 | tf_op jit(solution)/shard_map/ppermute | solution.py:206
  19.6 2.4 %near_below.1 = (f32[256,512]{1,0:T(8,128)S(1)}, f32[256,1024]{1,0:T(8,128)S(1)}) custom-call(f32[1024,1024]{1,0:T(8,128)} %bitcast.6, f32[1024,512]{1,0:T(8,128)S(1)} %get-tuple-element.25.held.x.refs_1_, f32[128,256]{1,0:T(8,128)S(1)} %lift_leaves.1._.refs_2_.refs_0_), custom_call_target="tpu_custom_call" | custom-call | flops 536870912 | bytes 4194304 | tf_op jit(solution)/shard_map/near_below/pallas_call | solution.py:254
  22.0 1.7 %couple_leaves.1 = (f32[128,256]{1,0:T(8,128)S(1)}, f32[128,256]{1,0:T(8,128)S(1)}, f32[128,256]{1,0:T(8,128)S(1)}, f32[128,256]{1,0:T(8,128)S(1)}) custom-call(f32[128,256]{1,0:T(8,128)S(1)} %get-tuple-element.28.refs_0_, f32[128,256]{1,0:T(8,128)S(1)} %collective-permute-done.refs_1_, f32[128,256]{1,0:T(8,128)S(1)} %collective-permute-done.1.refs_2_, ...), custom_call_target="tpu_custom_call" | custom-call | flops 603979776 | bytes 2883584 | tf_op jit(solution)/shard_map/couple_leaves/pallas_call | solution.py:45
  23.7 0.6 %turn.1 = (f32[3,256,256]{2,1,0:T(8,128)S(1)}, f32[256,256]{1,0:T(8,128)S(1)}, f32[4,256,256]{2,1,0:T(8,128)S(1)}) custom-call(f32[3,3,256,256]{3,2,1,0:T(8,128)S(1)} %copy-done, f32[2,4,256,256]{3,2,1,0:T(8,128)S(1)} %copy-done.1, f32[128,256]{1,0:T(8,128)S(1)} %lift_leaves.1._.refs_2_.refs_0_), custom_call_target="tpu_custom_call" | custom-call | flops 805306368 | bytes 4456448 | tf_op jit(solution)/shard_map/turn/pallas_call | solution.py:45
  24.3 0.9 %collective-permute-done.4.refs_2_ = f32[128,256]{1,0:T(8,128)S(1)} collective-permute-done((f32[128,256]{1,0:T(8,128)S(1)}, f32[128,256]{1,0:T(8,128)S(1)}, u32[]{:S(2)}, u32[]{:S(2)}) %collective-permute-start.4) | collective-permute-done | bytes 131104 | tf_op jit(solution)/shard_map/ppermute | solution.py:206
  25.3 4.6 %collective-permute-done.3.refs_1_ = f32[128,256]{1,0:T(8,128)S(1)} collective-permute-done((f32[128,256]{1,0:T(8,128)S(1)}, f32[128,256]{1,0:T(8,128)S(1)}, u32[]{:S(2)}, u32[]{:S(2)}) %collective-permute-start.3) | collective-permute-done | bytes 131104 | tf_op jit(solution)/shard_map/ppermute | solution.py:206
  29.8 0.4 lift_nodes.1
  30.3 3.0 %collective-permute-start.8 = (f32[128,256]{1,0:T(8,128)S(1)}, f32[128,256]{1,0:T(8,128)S(1)}, u32[]{:S(2)}, u32[]{:S(2)}) collective-permute-start(f32[128,256]{1,0:T(8,128)S(1)} %lift_nodes.1), channel_id=1, source_target_pairs={{0,128},{4,132},{8,136},{12,140},{16,144},{20,148},{24,152},{28,15... | collective-permute-start | bytes 393224 | tf_op jit(solution)/shard_map/ppermute | solution.py:206
  33.3 0.8 %collective-permute-start.7 = (f32[128,256]{1,0:T(8,128)S(1)}, f32[128,256]{1,0:T(8,128)S(1)}, u32[]{:S(2)}, u32[]{:S(2)}) collective-permute-start(f32[128,256]{1,0:T(8,128)S(1)} %lift_nodes.1), channel_id=1, source_target_pairs={{0,192},{4,196},{8,200},{12,204},{16,208},{20,212},{24,216},{28,22... | collective-permute-start | bytes 393224 | tf_op jit(solution)/shard_map/ppermute | solution.py:206
  34.1 0.6 %couple_nodes.1.refs_6_ = f32[128,256]{1,0:T(8,128)S(1)} custom-call(f32[128,256]{1,0:T(8,128)S(1)} %lift_leaves.1._.refs_2_.refs_0_, f32[128,256]{1,0:T(8,128)S(1)} %collective-permute-done.3.refs_1_, f32[128,256]{1,0:T(8,128)S(1)} %collective-permute-done.4.refs_2_, f32[128,256]{1,0:T(8,128)S(1)} %collective-permute-done.5.refs_3_, ...), custom_call_target="tpu_custom_call" | custom-call | flops 150994944 | bytes 2883584 | tf_op jit(solution)/shard_map/couple_nodes/pallas_call | solution.py:45
  34.6 1.1 %collective-permute-done.8.refs_2_ = f32[128,256]{1,0:T(8,128)S(1)} collective-permute-done((f32[128,256]{1,0:T(8,128)S(1)}, f32[128,256]{1,0:T(8,128)S(1)}, u32[]{:S(2)}, u32[]{:S(2)}) %collective-permute-start.8) | collective-permute-done | bytes 131104 | tf_op jit(solution)/shard_map/ppermute | solution.py:206
  35.7 3.2 %collective-permute-done.7.refs_1_ = f32[128,256]{1,0:T(8,128)S(1)} collective-permute-done((f32[128,256]{1,0:T(8,128)S(1)}, f32[128,256]{1,0:T(8,128)S(1)}, u32[]{:S(2)}, u32[]{:S(2)}) %collective-permute-start.7) | collective-permute-done | bytes 131104 | tf_op jit(solution)/shard_map/ppermute | solution.py:206
  38.9 0.6 %collective-permute-done.6.refs_0_ = f32[128,256]{1,0:T(8,128)S(1)} collective-permute-done((f32[128,256]{1,0:T(8,128)S(1)}, f32[128,256]{1,0:T(8,128)S(1)}, u32[]{:S(2)}, u32[]{:S(2)}) %collective-permute-start.6) | collective-permute-done | bytes 131104 | tf_op jit(solution)/shard_map/ppermute | solution.py:206
  39.5 1.1 %descend.1 = (f32[128,256]{1,0:T(8,128)S(1)}, f32[128,256]{1,0:T(8,128)S(1)}, f32[128,256]{1,0:T(8,128)S(1)}, f32[128,256]{1,0:T(8,128)S(1)}) custom-call(f32[128,256]{1,0:T(8,128)S(1)} %collective-permute-done.6.refs_0_, f32[128,256]{1,0:T(8,128)S(1)} %collective-permute-done.7.refs_1_, f32[128,256]{1,0:T(8,128)S(1)} %collective-permute-done.8.refs_2_, ...), custom_call_target="tpu_custom_call" | custom-call | flops 402653184 | bytes 3145728 | tf_op jit(solution)/shard_map/descend/pallas_call | solution.py:45
  40.5 2.8 %collective-permute-start.9 = (f32[128,256]{1,0:T(8,128)S(1)}, f32[128,256]{1,0:T(8,128)S(1)}, u32[]{:S(2)}, u32[]{:S(2)}) collective-permute-start(f32[128,256]{1,0:T(8,128)S(1)} %get-tuple-element.42), channel_id=1, source_target_pairs={{0,8},{4,12},{8,0},{12,4},{16,24},{20,28},{24,16},{28,20},{32,40},... | collective-permute-start | bytes 393224 | tf_op jit(solution)/shard_map/ppermute | solution.py:206
  43.3 1.4 %collective-permute-start.10 = (f32[128,256]{1,0:T(8,128)S(1)}, f32[128,256]{1,0:T(8,128)S(1)}, u32[]{:S(2)}, u32[]{:S(2)}) collective-permute-start(f32[128,256]{1,0:T(8,128)S(1)} %get-tuple-element.43), channel_id=1, source_target_pairs={{0,12},{4,8},{8,4},{12,0},{16,28},{20,24},{24,20},{28,16},{32,44},... | collective-permute-start | bytes 393224 | tf_op jit(solution)/shard_map/ppermute | solution.py:206
  44.7 0.3 collective-permute-start.11
  45.0 1.1 %near_last.1.near_fourth = f32[256,512]{1,0:T(8,128)S(1)} custom-call(f32[256,1024]{1,0:T(8,128)S(1)} %get-tuple-element.33.refs_0_, f32[1024,512]{1,0:T(8,128)S(1)} %get-tuple-element.25.held.x.refs_1_, f32[128,256]{1,0:T(8,128)S(1)} %get-tuple-element.41.refs_2_.rest_0_), custom_call_target="tpu_custom_call" | custom-call | flops 1610612736 | bytes 3145728 | tf_op jit(solution)/shard_map/near_last/pallas_call | solution.py:45
  46.2 0.1 copy-done.2
  46.3 1.5 %finish_0.1.rest_2_ = f32[1024,512]{1,0:T(8,128)} custom-call(f32[512,512]{1,0:T(8,128)S(1)} %get-tuple-element.27.near_above, f32[256,512]{1,0:T(8,128)S(1)} %get-tuple-element.32.refs_9_.near_third, f32[256,512]{1,0:T(8,128)S(1)} %near_last.1.near_fourth, f32[1024,256]{1,0:T(8,128)S(1)} %bitcast.3, f32[128,256]{1,0:T(8,128)S(1)} %get-tuple-element.41.refs_2_.rest_0_, ...), custom_call_target="tpu_custom_call" | custom-call | flops 402653184 | bytes 1048576 | tf_op jit(solution)/shard_map/finish_0/pallas_call | solution.py:313
  47.8 2.5 %collective-permute-done.10.rest_1_ = f32[128,256]{1,0:T(8,128)S(1)} collective-permute-done((f32[128,256]{1,0:T(8,128)S(1)}, f32[128,256]{1,0:T(8,128)S(1)}, u32[]{:S(2)}, u32[]{:S(2)}) %collective-permute-start.10) | collective-permute-done | bytes 131104 | tf_op jit(solution)/shard_map/ppermute | solution.py:206
  50.3 1.5 %finish_2.1 = f32[1024,512]{1,0:T(8,128)} custom-call(f32[512,512]{1,0:T(8,128)S(1)} %get-tuple-element.27.near_above, f32[256,512]{1,0:T(8,128)S(1)} %get-tuple-element.32.refs_9_.near_third, f32[256,512]{1,0:T(8,128)S(1)} %near_last.1.near_fourth, f32[1024,256]{1,0:T(8,128)S(1)} %bitcast.4, ...), custom_call_target="tpu_custom_call", output_to_operand_aliasing={{}: (6, {})} | custom-call | flops 402653184 | bytes 1048576 | tf_op jit(solution)/shard_map/finish_2/pallas_call | solution.py:313
  (10 shorter events, 0.0 us)
Async XLA Ops:
  2.5 9.2 %collective-permute-start.1 = (f32[128,256]{1,0:T(8,128)S(1)}, f32[128,256]{1,0:T(8,128)S(1)}, u32[]{:S(2)}, u32[]{:S(2)}) collective-permute-start(f32[128,256]{1,0:T(8,128)S(1)} %get-tuple-element.30), channel_id=1, source_target_pairs={{0,8},{4,12},{8,0},{12,4},{16,24},{20,28},{24,16},{28,20},{32,40},... | collective-permute-start | bytes 393224 | tf_op jit(solution)/shard_map/ppermute | solution.py:206
  5.0 7.5 %collective-permute-start.2 = (f32[128,256]{1,0:T(8,128)S(1)}, f32[128,256]{1,0:T(8,128)S(1)}, u32[]{:S(2)}, u32[]{:S(2)}) collective-permute-start(f32[128,256]{1,0:T(8,128)S(1)} %get-tuple-element.31), channel_id=1, source_target_pairs={{0,12},{4,8},{8,4},{12,0},{16,28},{20,24},{24,20},{28,16},{32,44},... | collective-permute-start | bytes 393224 | tf_op jit(solution)/shard_map/ppermute | solution.py:206
  7.5 5.5 %copy-start.1 = (f32[2,4,256,256]{3,2,1,0:T(8,128)S(1)}, f32[2,4,256,256]{3,2,1,0:T(8,128)}, u32[]{:S(2)}) copy-start(f32[2,4,256,256]{3,2,1,0:T(8,128)} %refs_4_.6) | copy-start | bytes 6291460
  11.5 1.4 %collective-permute-start = (f32[128,256]{1,0:T(8,128)S(1)}, f32[128,256]{1,0:T(8,128)S(1)}, u32[]{:S(2)}, u32[]{:S(2)}) collective-permute-start(f32[128,256]{1,0:T(8,128)S(1)} %get-tuple-element.29), channel_id=1, source_target_pairs={{0,4},{4,0},{8,12},{12,8},{16,20},{20,16},{24,28},{28,24},{32,36},... | collective-permute-start | bytes 393224 | tf_op jit(solution)/shard_map/ppermute | solution.py:206
  13.4 8.6 %copy-start = (f32[3,3,256,256]{3,2,1,0:T(8,128)S(1)}, f32[3,3,256,256]{3,2,1,0:T(8,128)}, u32[]{:S(2)}) copy-start(f32[3,3,256,256]{3,2,1,0:T(8,128)} %refs_4_.7) | copy-start | bytes 7077892
  13.4 10.9 %collective-permute-start.5 = (f32[128,256]{1,0:T(8,128)S(1)}, f32[128,256]{1,0:T(8,128)S(1)}, u32[]{:S(2)}, u32[]{:S(2)}) collective-permute-start(f32[128,256]{1,0:T(8,128)S(1)} %lift_leaves.1._.refs_2_.refs_0_), channel_id=1, source_target_pairs={{0,16},{4,20},{8,24},{12,28},{16,0},{20,4},{24,8},{28,12},{32,48},... | collective-permute-start | bytes 393224 | tf_op jit(solution)/shard_map/ppermute | solution.py:206
  15.1 10.1 %collective-permute-start.4 = (f32[128,256]{1,0:T(8,128)S(1)}, f32[128,256]{1,0:T(8,128)S(1)}, u32[]{:S(2)}, u32[]{:S(2)}) collective-permute-start(f32[128,256]{1,0:T(8,128)S(1)} %lift_leaves.1._.refs_2_.refs_0_), channel_id=1, source_target_pairs={{0,56},{4,60},{8,48},{12,52},{16,40},{20,44},{24,32},{28,36},{32,2... | collective-permute-start | bytes 393224 | tf_op jit(solution)/shard_map/ppermute | solution.py:206
  18.7 11.1 %collective-permute-start.3 = (f32[128,256]{1,0:T(8,128)S(1)}, f32[128,256]{1,0:T(8,128)S(1)}, u32[]{:S(2)}, u32[]{:S(2)}) collective-permute-start(f32[128,256]{1,0:T(8,128)S(1)} %lift_leaves.1._.refs_2_.refs_0_), channel_id=1, source_target_pairs={{0,40},{4,44},{8,32},{12,36},{16,56},{20,60},{24,48},{28,52},{32,8... | collective-permute-start | bytes 393224 | tf_op jit(solution)/shard_map/ppermute | solution.py:206
  30.3 5.4 %collective-permute-start.8 = (f32[128,256]{1,0:T(8,128)S(1)}, f32[128,256]{1,0:T(8,128)S(1)}, u32[]{:S(2)}, u32[]{:S(2)}) collective-permute-start(f32[128,256]{1,0:T(8,128)S(1)} %lift_nodes.1), channel_id=1, source_target_pairs={{0,128},{4,132},{8,136},{12,140},{16,144},{20,148},{24,152},{28,15... | collective-permute-start | bytes 393224 | tf_op jit(solution)/shard_map/ppermute | solution.py:206
  33.3 5.6 %collective-permute-start.7 = (f32[128,256]{1,0:T(8,128)S(1)}, f32[128,256]{1,0:T(8,128)S(1)}, u32[]{:S(2)}, u32[]{:S(2)}) collective-permute-start(f32[128,256]{1,0:T(8,128)S(1)} %lift_nodes.1), channel_id=1, source_target_pairs={{0,192},{4,196},{8,200},{12,204},{16,208},{20,212},{24,216},{28,22... | collective-permute-start | bytes 393224 | tf_op jit(solution)/shard_map/ppermute | solution.py:206
  34.0 5.4 %collective-permute-start.6 = (f32[128,256]{1,0:T(8,128)S(1)}, f32[128,256]{1,0:T(8,128)S(1)}, u32[]{:S(2)}, u32[]{:S(2)}) collective-permute-start(f32[128,256]{1,0:T(8,128)S(1)} %lift_nodes.1), channel_id=1, source_target_pairs={{0,64},{4,68},{8,72},{12,76},{16,80},{20,84},{24,88},{28,92},{32,9... | collective-permute-start | bytes 393224 | tf_op jit(solution)/shard_map/ppermute | solution.py:206
  40.5 7.2 %collective-permute-start.9 = (f32[128,256]{1,0:T(8,128)S(1)}, f32[128,256]{1,0:T(8,128)S(1)}, u32[]{:S(2)}, u32[]{:S(2)}) collective-permute-start(f32[128,256]{1,0:T(8,128)S(1)} %get-tuple-element.42), channel_id=1, source_target_pairs={{0,8},{4,12},{8,0},{12,4},{16,24},{20,28},{24,16},{28,20},{32,40},... | collective-permute-start | bytes 393224 | tf_op jit(solution)/shard_map/ppermute | solution.py:206
  43.3 6.9 %collective-permute-start.10 = (f32[128,256]{1,0:T(8,128)S(1)}, f32[128,256]{1,0:T(8,128)S(1)}, u32[]{:S(2)}, u32[]{:S(2)}) collective-permute-start(f32[128,256]{1,0:T(8,128)S(1)} %get-tuple-element.43), channel_id=1, source_target_pairs={{0,12},{4,8},{8,4},{12,0},{16,28},{20,24},{24,20},{28,16},{32,44},... | collective-permute-start | bytes 393224 | tf_op jit(solution)/shard_map/ppermute | solution.py:206
  44.7 1.4 %collective-permute-start.11 = (f32[128,256]{1,0:T(8,128)S(1)}, f32[128,256]{1,0:T(8,128)S(1)}, u32[]{:S(2)}, u32[]{:S(2)}) collective-permute-start(f32[128,256]{1,0:T(8,128)S(1)} %get-tuple-element.44), channel_id=1, source_target_pairs={{0,4},{4,0},{8,12},{12,8},{16,20},{20,16},{24,28},{28,24},{32,36},... | collective-permute-start | bytes 393224 | tf_op jit(solution)/shard_map/ppermute | solution.py:206
  45.0 1.2 %copy-start.2 = (f32[1,1024,256]{2,1,0:T(8,128)S(1)}, f32[1,1024,256]{2,1,0:T(8,128)}, u32[]{:S(2)}) copy-start(f32[1,1024,256]{2,1,0:T(8,128)} %param.8) | copy-start | bytes 3145732

commit v9 on v8

--- a/solution.py
+++ b/solution.py
@@ -168,26 +168,28 @@
         leaf_turned[i] = transfers[0, i].T
 
 
-def descend(c1, c3, c2, top_turned, node_turned, leaf_turned, field, f0, f1, f2, f3, *outs):
-    r, _, k, _ = place()
-    parts = (c1, c2, c3)
-    g = sum(dot(c[...], top_turned[offset(r ^ d, r)], 1, 0) for d, c in zip((1, 2, 3), parts))
-    g = field[...] + dot(g, node_turned[...], 1, 0)
-    for j, (f, out) in enumerate(zip((f0, f1, f2, f3), outs)):
-        out[...] = f[...] + dot(g, leaf_turned[k ^ j], 1, 0)
-
-
-def finish(first, near_above, near_third, near_fourth, row_basis, *rest):
+def descend(c2, c3, c1, top_turned, node_turned, field, out):
+    r = place()[0]
+    g = sum(
+        dot(c[...], top_turned[offset(r ^ d, r)], 1, 0) for d, c in zip((2, 3, 1), (c2, c3, c1))
+    )
+    out[...] = field[...] + dot(g, node_turned[...], 1, 0)
+
+
+def relay(block, out):
+    out[...] = block[...]
+
+
+def finish(
+    first, near_above, near_third, near_fourth, row_basis, leaf_turned, f0, g0, f1, g1, *rest
+):
     out, block, whole, sems = rest[-4:]
     _, m, k, _ = place()
-    wide, step = whole.shape[0], rest[0].shape[0]
-    if wide == step:
-        whole[...] = rest[0][...]
-        columns = span(mine(m, k) ^ first, wide)
-    else:
-        for j in (0, 1):
-            whole[span((mine(m, k) ^ j) % 2, step), :] = rest[j][...]
-        columns = span((mine(m, k) ^ first) // 2, wide)
+    wide, step = whole.shape[0], g0.shape[0]
+    for j, (field, parent) in enumerate(((f0, g0), (f1, g1))):
+        at = span((mine(m, k) ^ j) % 2, step)
+        whole[at, :] = field[...] + dot(parent[...], leaf_turned[k], 1, 0)
+    columns = span((mine(m, k) ^ first) // 2, wide)
     chunk = out.shape[0] // CHUNKS
     copies = []
     for i in range(CHUNKS):
@@ -240,15 +242,15 @@
         **settings(3 * users * users * columns, users * users, "own_and_near"),
     )(*in_vmem([held, basis_held]), *in_hbm([dense]))
     c1 = swap(c1, 1)
-    coef = [c0, c1, c2, c3]
+    leaves, coef = (0, 2, 3, 1), [c0, c2, c3, c1]
     (lifted,) = run(
-        functools.partial(lift, 0, 2, range(4)),
+        functools.partial(lift, 0, 2, leaves),
         [*coef, transfers],
         [(quarter, rank)],
         "lift_leaves",
         unit * columns,
     )
-    nodes = (0, 2, 3, 1)
+    nodes = (0, 1, 3, 2)
     node_coef = [swap(lifted, (j << 2) | (j & 2)) if j else lifted for j in nodes]
     part_rows = (users // 4, columns)
     near_third, dense_rest = pl.pallas_call(
@@ -260,7 +262,7 @@
         **settings(users * users * columns, users * users, "near_below"),
     )(*in_hbm([dense]), *in_vmem([held]), lifted)
     leaf_fields = run(
-        functools.partial(couple, 0, 2, range(4)),
+        functools.partial(couple, 0, 2, leaves),
         [*coef, couplings],
         [(quarter, rank)] * 4,
         "couple_leaves",
@@ -282,7 +284,7 @@
         unit * columns,
         after=[*leaf_fields, near_third, turned[1]],
     )
-    top_coef = [swap(crown, bits) for bits in (16, 48, 32)]
+    top_coef = [swap(crown, bits) for bits in (32, 48, 16)]
     (node_field,) = run(
         functools.partial(couple, 1, 1, nodes),
         [*node_coef, couplings],
@@ -290,42 +292,47 @@
         "couple_nodes",
         unit * 3 * quarter,
     )
-    g0, g1, g2, g3 = run(
+    fields = [leaf_fields[0]] + [swap(leaf_fields[j], j) for j in (1, 2, 3)]
+    (parent,) = run(
         descend,
-        [*top_coef, *turned, node_field, *leaf_fields],
-        [(quarter, rank)] * 4,
+        [*top_coef, *turned[:2], node_field],
+        [(quarter, rank)],
         "descend",
-        unit * 8 * quarter,
-    )
+        unit * 4 * quarter,
+        after=fields[2:3],
+    )
+    far_parent, core_parent = swap(parent, 2), swap(parent, 1)
     (near_fourth,) = run(
         near_last,
         [dense_rest, held],
         [part_rows],
         "near_last",
         3 * users * users * columns,
-        after=[g0],
+        after=[parent],
     )
     nears = [near_above, near_third, near_fourth]
-    g2, g3, g1 = swap(g2, 2), swap(g3, 3), swap(g1, 1)
 
     def write(first, pieces, out):
-        wide = len(pieces) * quarter
+        ins = in_vmem([*nears, rbasis, turned[2], *pieces])
         return pl.pallas_call(
             functools.partial(finish, first),
             out_shape=pltpu.HBM((users, columns), F32),
-            in_specs=[VMEM] * (4 + len(pieces)) + [ANY] * len(out),
+            in_specs=[VMEM] * len(ins) + [ANY] * len(out),
             out_specs=ANY,
             scratch_shapes=[
-                pltpu.VMEM((users, wide), F32),
-                pltpu.VMEM((wide, rank), F32),
+                pltpu.VMEM((users, columns // 2), F32),
+                pltpu.VMEM((columns // 2, rank), F32),
                 pltpu.SemaphoreType.DMA((CHUNKS,)),
             ],
-            input_output_aliases={4 + len(pieces): 0} if out else {},
-            **settings(6 * users * rank * wide, users * wide, "finish_%d" % first),
-        )(*in_vmem([*nears, rbasis, *pieces]), *out)
-
-    out = write(0, [g0, g1], [])
-    return write(2, [g2, g3], [out])
+            input_output_aliases={len(ins): 0} if out else {},
+            **settings(3 * users * rank * columns, users * columns, "finish_%d" % first),
+        )(*ins, *out)
+
+    out = write(0, [fields[0], parent, fields[1], core_parent], [])
+    (far_parent,) = run(
+        relay, [far_parent], [(quarter, rank)], "relay", quarter * rank, after=in_hbm([out])
+    )
+    return write(2, [fields[2], far_parent, fields[3], swap(far_parent, 1)], [out])
 
 
 def solution(mesh):

time: 52.1 us -> 51.1 us (0.981)
  waiting for transfers between devices: 14.2 us -> 8.32 us
  starting transfers between devices: 19.5 us -> 24.3 us
    ppermute x12 -> x15, waiting for transfers between devices: 14.2 us -> 8.32 us  [swap(): lax.ppermute(block, 'leaf', [(i, i ^ bits) for i in range(lax.axis_size('...]
    ppermute x12 -> x15, starting transfers between devices: 19.5 us -> 24.3 us  [swap(): lax.ppermute(block, 'leaf', [(i, i ^ bits) for i in range(lax.axis_size('...]
    pallas_call x2, Pallas kernels: 3.01 us -> 3.54 us  [write(): pl.pallas_call(functools.partial(finish, first), out_shape=pltpu.HBM((use...]
    pallas_call x7 -> x8, Pallas kernels: 5.84 us -> 5.34 us  [run(): pl.pallas_call(kernel, out_shape=[pltpu.VMEM(shape, F32) for shape in out...]
  transfers between devices with their start and end apart: 12 -> 15, of which waited for: 8 -> 7; matrix products, arithmetic and copies ran while one was open for 0% -> 0% of each run, Pallas kernels for 23% -> 26%
where the time goes in v9:
time: 51.1 us; the launch traced here: 50.9 us
  starting transfers between devices  24.3 us (48%)
  Pallas kernels  17.8 us (35%)
  waiting for transfers between devices  8.32 us (16%)
    ppermute x15, starting transfers between devices, swap(): lax.ppermute(block, 'leaf', [(i, i ^ bits) for i in range(lax.axis_size('...  24.3 us
    ppermute x15, waiting for transfers between devices, swap(): lax.ppermute(block, 'leaf', [(i, i ^ bits) for i in range(lax.axis_size('...  8.32 us
    pallas_call x8, Pallas kernels, run(): pl.pallas_call(kernel, out_shape=[pltpu.VMEM(shape, F32) for shape in out...  5.34 us
    pallas_call x1, Pallas kernels, local(): pl.pallas_call(own_and_near, out_shape=[pltpu.VMEM(shape, F32) for shape...  4.08 us
    pallas_call x2, Pallas kernels, write(): pl.pallas_call(functools.partial(finish, first), out_shape=pltpu.HBM((use...  3.54 us
    pallas_call x1, Pallas kernels, local(): pl.pallas_call(far_coefficients, out_shape=[pltpu.VMEM(shape, F32) for sh...  2.49 us
    pallas_call x1, Pallas kernels, local(): pl.pallas_call(near_below, out_shape=[pltpu.VMEM(part_rows, F32), pltpu.V...  2.37 us
  transfers between devices with their start and end apart: 15, of which 7 were waited for; matrix products, arithmetic and copies ran while one was open for 0% of the time, Pallas kernels for 26%

profile of v9, /device:TPU:1, one launch (start us, length us, event | category | flops | bytes accessed | tf_op | source)
XLA Modules:
  0.0 50.9 jit_solution(18251439433396031125)
XLA Ops:
  0.0 2.5 %far_coefficients.1 = (f32[128,256]{1,0:T(8,128)S(1)}, f32[128,256]{1,0:T(8,128)S(1)}, f32[1024,512]{1,0:T(8,128)S(1)}, f32[1024,256]{1,0:T(8,128)S(1)}) custom-call(f32[1024,512]{1,0:T(8,128)} %x.1, f32[1024,256]{1,0:T(8,128)} %bitcast.7), custom_call_target="tpu_custom_call" | custom-call | flops 402653184 | bytes 2097152 | tf_op jit(solution)/shard_map/far_coefficients/pallas_call | solution.py:218
  2.5 2.5 %collective-permute-start = (f32[128,256]{1,0:T(8,128)S(1)}, f32[128,256]{1,0:T(8,128)S(1)}, u32[]{:S(2)}, u32[]{:S(2)}) collective-permute-start(f32[128,256]{1,0:T(8,128)S(1)} %get-tuple-element.25), channel_id=1, source_target_pairs={{0,8},{4,12},{8,0},{12,4},{16,24},{20,28},{24,16},{28,20},{32,40},... | collective-permute-start | bytes 393224 | tf_op jit(solution)/shard_map/ppermute | solution.py:208
  5.0 2.4 %collective-permute-start.1 = (f32[128,256]{1,0:T(8,128)S(1)}, f32[128,256]{1,0:T(8,128)S(1)}, u32[]{:S(2)}, u32[]{:S(2)}) collective-permute-start(f32[128,256]{1,0:T(8,128)S(1)} %get-tuple-element.26), channel_id=1, source_target_pairs={{0,12},{4,8},{8,4},{12,0},{16,28},{20,24},{24,20},{28,16},{32,44},... | collective-permute-start | bytes 393224 | tf_op jit(solution)/shard_map/ppermute | solution.py:208
  7.5 4.1 %own_and_near.1 = (f32[128,256]{1,0:T(8,128)S(1)}, f32[128,256]{1,0:T(8,128)S(1)}, f32[512,512]{1,0:T(8,128)S(1)}) custom-call(f32[1024,512]{1,0:T(8,128)S(1)} %get-tuple-element.21.held.x.refs_1_, f32[1024,256]{1,0:T(8,128)S(1)} %get-tuple-element.22.basis_held, f32[1024,1024]{1,0:T(8,128)} %bitcast.5), custom_call_target="tpu_custom_call" | custom-call | flops 1610612736 | bytes 4194304 | tf_op jit(solution)/shard_map/own_and_near/pallas_call | solution.py:236
  11.7 0.8 %collective-permute-done.1.refs_2_ = f32[128,256]{1,0:T(8,128)S(1)} collective-permute-done((f32[128,256]{1,0:T(8,128)S(1)}, f32[128,256]{1,0:T(8,128)S(1)}, u32[]{:S(2)}, u32[]{:S(2)}) %collective-permute-start.1) | collective-permute-done | bytes 131104 | tf_op jit(solution)/shard_map/ppermute | solution.py:208
  12.5 0.5 collective-permute-done.2.refs_3_
  13.0 0.4 lift_leaves.1._.refs_2_.refs_0_
  13.4 1.7 %collective-permute-start.3 = (f32[128,256]{1,0:T(8,128)S(1)}, f32[128,256]{1,0:T(8,128)S(1)}, u32[]{:S(2)}, u32[]{:S(2)}) collective-permute-start(f32[128,256]{1,0:T(8,128)S(1)} %lift_leaves.1._.refs_2_.refs_0_), channel_id=1, source_target_pairs={{0,16},{4,20},{8,24},{12,28},{16,0},{20,4},{24,8},{28,12},{32,48},... | collective-permute-start | bytes 393224 | tf_op jit(solution)/shard_map/ppermute | solution.py:208
  15.1 3.6 %collective-permute-start.4 = (f32[128,256]{1,0:T(8,128)S(1)}, f32[128,256]{1,0:T(8,128)S(1)}, u32[]{:S(2)}, u32[]{:S(2)}) collective-permute-start(f32[128,256]{1,0:T(8,128)S(1)} %lift_leaves.1._.refs_2_.refs_0_), channel_id=1, source_target_pairs={{0,56},{4,60},{8,48},{12,52},{16,40},{20,44},{24,32},{28,36},{32,2... | collective-permute-start | bytes 393224 | tf_op jit(solution)/shard_map/ppermute | solution.py:208
  18.7 0.9 %collective-permute-start.5 = (f32[128,256]{1,0:T(8,128)S(1)}, f32[128,256]{1,0:T(8,128)S(1)}, u32[]{:S(2)}, u32[]{:S(2)}) collective-permute-start(f32[128,256]{1,0:T(8,128)S(1)} %lift_leaves.1._.refs_2_.refs_0_), channel_id=1, source_target_pairs={{0,40},{4,44},{8,32},{12,36},{16,56},{20,60},{24,48},{28,52},{32,8... | collective-permute-start | bytes 393224 | tf_op jit(solution)/shard_map/ppermute | solution.py:208
  19.6 1.7 %couple_leaves.1 = (f32[128,256]{1,0:T(8,128)S(1)}, f32[128,256]{1,0:T(8,128)S(1)}, f32[128,256]{1,0:T(8,128)S(1)}, f32[128,256]{1,0:T(8,128)S(1)}) custom-call(f32[128,256]{1,0:T(8,128)S(1)} %get-tuple-element.24.refs_0_, f32[128,256]{1,0:T(8,128)S(1)} %collective-permute-done.refs_1_, f32[128,256]{1,0:T(8,128)S(1)} %collective-permute-done.1.refs_2_, ...), custom_call_target="tpu_custom_call" | custom-call | flops 603979776 | bytes 2883584 | tf_op jit(solution)/shard_map/couple_leaves/pallas_call | solution.py:45
  21.3 0.8 %collective-permute-start.9 = (f32[128,256]{1,0:T(8,128)S(1)}, f32[128,256]{1,0:T(8,128)S(1)}, u32[]{:S(2)}, u32[]{:S(2)}) collective-permute-start(f32[128,256]{1,0:T(8,128)S(1)} %get-tuple-element.32.refs_7_), channel_id=1, source_target_pairs={{0,8},{4,12},{8,0},{12,4},{16,24},{20,28},{24,16},{28,20},{32,40},... | collective-permute-start | bytes 393224 | tf_op jit(solution)/shard_map/ppermute | solution.py:208
  22.1 2.4 %near_below.1 = (f32[256,512]{1,0:T(8,128)S(1)}, f32[256,1024]{1,0:T(8,128)S(1)}) custom-call(f32[1024,1024]{1,0:T(8,128)} %bitcast.6, f32[1024,512]{1,0:T(8,128)S(1)} %get-tuple-element.21.held.x.refs_1_, f32[128,256]{1,0:T(8,128)S(1)} %lift_leaves.1._.refs_2_.refs_0_), custom_call_target="tpu_custom_call" | custom-call | flops 536870912 | bytes 4194304 | tf_op jit(solution)/shard_map/near_below/pallas_call | solution.py:256
  24.5 0.6 %turn.1 = (f32[3,256,256]{2,1,0:T(8,128)S(1)}, f32[256,256]{1,0:T(8,128)S(1)}, f32[4,256,256]{2,1,0:T(8,128)S(1)}) custom-call(f32[3,3,256,256]{3,2,1,0:T(8,128)S(1)} %copy-done, f32[2,4,256,256]{3,2,1,0:T(8,128)S(1)} %copy-done.1, f32[128,256]{1,0:T(8,128)S(1)} %lift_leaves.1._.refs_2_.refs_0_), custom_call_target="tpu_custom_call" | custom-call | flops 805306368 | bytes 4456448 | tf_op jit(solution)/shard_map/turn/pallas_call | solution.py:45
  25.1 0.2 collective-permute-done.4.refs_2_
  25.2 4.6 %collective-permute-done.5.refs_3_ = f32[128,256]{1,0:T(8,128)S(1)} collective-permute-done((f32[128,256]{1,0:T(8,128)S(1)}, f32[128,256]{1,0:T(8,128)S(1)}, u32[]{:S(2)}, u32[]{:S(2)}) %collective-permute-start.5) | collective-permute-done | bytes 131104 | tf_op jit(solution)/shard_map/ppermute | solution.py:208
  29.8 0.4 lift_nodes.1
  30.3 3.0 %collective-permute-start.6 = (f32[128,256]{1,0:T(8,128)S(1)}, f32[128,256]{1,0:T(8,128)S(1)}, u32[]{:S(2)}, u32[]{:S(2)}) collective-permute-start(f32[128,256]{1,0:T(8,128)S(1)} %lift_nodes.1), channel_id=1, source_target_pairs={{0,128},{4,132},{8,136},{12,140},{16,144},{20,148},{24,152},{28,15... | collective-permute-start | bytes 393224 | tf_op jit(solution)/shard_map/ppermute | solution.py:208
  33.2 0.8 %collective-permute-start.7 = (f32[128,256]{1,0:T(8,128)S(1)}, f32[128,256]{1,0:T(8,128)S(1)}, u32[]{:S(2)}, u32[]{:S(2)}) collective-permute-start(f32[128,256]{1,0:T(8,128)S(1)} %lift_nodes.1), channel_id=1, source_target_pairs={{0,192},{4,196},{8,200},{12,204},{16,208},{20,212},{24,216},{28,22... | collective-permute-start | bytes 393224 | tf_op jit(solution)/shard_map/ppermute | solution.py:208
  34.0 1.6 %collective-permute-start.11 = (f32[128,256]{1,0:T(8,128)S(1)}, f32[128,256]{1,0:T(8,128)S(1)}, u32[]{:S(2)}, u32[]{:S(2)}) collective-permute-start(f32[128,256]{1,0:T(8,128)S(1)} %get-tuple-element.31.refs_6_), channel_id=1, source_target_pairs={{0,4},{4,0},{8,12},{12,8},{16,20},{20,16},{24,28},{28,24},{32,36},... | collective-permute-start | bytes 393224 | tf_op jit(solution)/shard_map/ppermute | solution.py:208
  35.6 0.6 %couple_nodes.1.refs_5_ = f32[128,256]{1,0:T(8,128)S(1)} custom-call(f32[128,256]{1,0:T(8,128)S(1)} %lift_leaves.1._.refs_2_.refs_0_, f32[128,256]{1,0:T(8,128)S(1)} %collective-permute-done.3.refs_1_, f32[128,256]{1,0:T(8,128)S(1)} %collective-permute-done.4.refs_2_, f32[128,256]{1,0:T(8,128)S(1)} %collective-permute-done.5.refs_3_, ...), custom_call_target="tpu_custom_call" | custom-call | flops 150994944 | bytes 2883584 | tf_op jit(solution)/shard_map/couple_nodes/pallas_call | solution.py:45
  36.2 2.3 %collective-permute-start.13 = (f32[128,256]{1,0:T(8,128)S(1)}, f32[128,256]{1,0:T(8,128)S(1)}, u32[]{:S(2)}, u32[]{:S(2)}) collective-permute-start(f32[128,256]{1,0:T(8,128)S(1)} %get-tuple-element.33.refs_8_), channel_id=1, source_target_pairs={{0,12},{4,8},{8,4},{12,0},{16,28},{20,24},{24,20},{28,16},{32,44},... | collective-permute-start | bytes 393224 | tf_op jit(solution)/shard_map/ppermute | solution.py:208
  38.5 0.3 collective-permute-done.7.refs_1_
  38.9 0.7 %collective-permute-done.8.refs_2_ = f32[128,256]{1,0:T(8,128)S(1)} collective-permute-done((f32[128,256]{1,0:T(8,128)S(1)}, f32[128,256]{1,0:T(8,128)S(1)}, u32[]{:S(2)}, u32[]{:S(2)}) %collective-permute-start.8) | collective-permute-done | bytes 131104 | tf_op jit(solution)/shard_map/ppermute | solution.py:208
  39.5 0.6 %descend.1.refs_2_.g0 = f32[128,256]{1,0:T(8,128)S(1)} custom-call(f32[128,256]{1,0:T(8,128)S(1)} %collective-permute-done.6.refs_0_, f32[128,256]{1,0:T(8,128)S(1)} %collective-permute-done.7.refs_1_, f32[128,256]{1,0:T(8,128)S(1)} %collective-permute-done.8.refs_2_, f32[3,256,256]{2,1,0:T(8,128)S(1)} %get-tuple-element.35.refs_3_, ...), custom_call_target="tpu_custom_call" | custom-call | flops 201326592 | bytes 1572864 | tf_op jit(solution)/shard_map/descend/pallas_call | solution.py:45
  40.1 2.7 %collective-permute-start.10 = (f32[128,256]{1,0:T(8,128)S(1)}, f32[128,256]{1,0:T(8,128)S(1)}, u32[]{:S(2)}, u32[]{:S(2)}) collective-permute-start(f32[128,256]{1,0:T(8,128)S(1)} %descend.1.refs_2_.g0), channel_id=1, source_target_pairs={{0,8},{4,12},{8,0},{12,4},{16,24},{20,28},{24,16},{28,20},{32,40},... | collective-permute-start | bytes 393224 | tf_op jit(solution)/shard_map/ppermute | solution.py:208
  42.8 1.7 %collective-permute-start.12 = (f32[128,256]{1,0:T(8,128)S(1)}, f32[128,256]{1,0:T(8,128)S(1)}, u32[]{:S(2)}, u32[]{:S(2)}) collective-permute-start(f32[128,256]{1,0:T(8,128)S(1)} %descend.1.refs_2_.g0), channel_id=1, source_target_pairs={{0,4},{4,0},{8,12},{12,8},{16,20},{20,16},{24,28},{28,24},{32,36},... | collective-permute-start | bytes 393224 | tf_op jit(solution)/shard_map/ppermute | solution.py:208
  44.5 1.1 %near_last.1.near_fourth = f32[256,512]{1,0:T(8,128)S(1)} custom-call(f32[256,1024]{1,0:T(8,128)S(1)} %get-tuple-element.29.refs_0_, f32[1024,512]{1,0:T(8,128)S(1)} %get-tuple-element.21.held.x.refs_1_, f32[128,256]{1,0:T(8,128)S(1)} %descend.1.refs_2_.g0), custom_call_target="tpu_custom_call" | custom-call | flops 1610612736 | bytes 3145728 | tf_op jit(solution)/shard_map/near_last/pallas_call | solution.py:45
  45.7 1.8 %finish_0.1.refs_1_.rest_0_ = f32[1024,512]{1,0:T(8,128)} custom-call(f32[512,512]{1,0:T(8,128)S(1)} %get-tuple-element.23.near_above, f32[256,512]{1,0:T(8,128)S(1)} %get-tuple-element.28.refs_9_.near_third, f32[256,512]{1,0:T(8,128)S(1)} %near_last.1.near_fourth, f32[1024,256]{1,0:T(8,128)S(1)} %bitcast.3, ...), custom_call_target="tpu_custom_call" | custom-call | flops 402653184 | bytes 2097152 | tf_op jit(solution)/shard_map/finish_0/pallas_call | solution.py:317
  47.5 0.2 collective-permute-start.14
  47.8 1.2 %collective-permute-done.14.g1 = f32[128,256]{1,0:T(8,128)S(1)} collective-permute-done((f32[128,256]{1,0:T(8,128)S(1)}, f32[128,256]{1,0:T(8,128)S(1)}, u32[]{:S(2)}, u32[]{:S(2)}) %collective-permute-start.14) | collective-permute-done | bytes 131104 | tf_op jit(solution)/shard_map/ppermute | solution.py:208
  49.0 1.8 %finish_2.1 = f32[1024,512]{1,0:T(8,128)} custom-call(f32[512,512]{1,0:T(8,128)S(1)} %get-tuple-element.23.near_above, f32[256,512]{1,0:T(8,128)S(1)} %get-tuple-element.28.refs_9_.near_third, f32[256,512]{1,0:T(8,128)S(1)} %near_last.1.near_fourth, f32[1024,256]{1,0:T(8,128)S(1)} %bitcast.4, ...), custom_call_target="tpu_custom_call", output_to_operand_aliasing={{}: (9, {})} | custom-call | flops 402653184 | bytes 2097152 | tf_op jit(solution)/shard_map/finish_2/pallas_call | solution.py:317
  (17 shorter events, 0.2 us)
Async XLA Ops:
  2.5 9.2 %collective-permute-start = (f32[128,256]{1,0:T(8,128)S(1)}, f32[128,256]{1,0:T(8,128)S(1)}, u32[]{:S(2)}, u32[]{:S(2)}) collective-permute-start(f32[128,256]{1,0:T(8,128)S(1)} %get-tuple-element.25), channel_id=1, source_target_pairs={{0,8},{4,12},{8,0},{12,4},{16,24},{20,28},{24,16},{28,20},{32,40},... | collective-permute-start | bytes 393224 | tf_op jit(solution)/shard_map/ppermute | solution.py:208
  5.0 7.5 %collective-permute-start.1 = (f32[128,256]{1,0:T(8,128)S(1)}, f32[128,256]{1,0:T(8,128)S(1)}, u32[]{:S(2)}, u32[]{:S(2)}) collective-permute-start(f32[128,256]{1,0:T(8,128)S(1)} %get-tuple-element.26), channel_id=1, source_target_pairs={{0,12},{4,8},{8,4},{12,0},{16,28},{20,24},{24,20},{28,16},{32,44},... | collective-permute-start | bytes 393224 | tf_op jit(solution)/shard_map/ppermute | solution.py:208
  7.5 5.5 %copy-start.1 = (f32[2,4,256,256]{3,2,1,0:T(8,128)S(1)}, f32[2,4,256,256]{3,2,1,0:T(8,128)}, u32[]{:S(2)}) copy-start(f32[2,4,256,256]{3,2,1,0:T(8,128)} %refs_4_.6) | copy-start | bytes 6291460
  11.5 8.1 %copy-start = (f32[3,3,256,256]{3,2,1,0:T(8,128)S(1)}, f32[3,3,256,256]{3,2,1,0:T(8,128)}, u32[]{:S(2)}) copy-start(f32[3,3,256,256]{3,2,1,0:T(8,128)} %refs_4_.7) | copy-start | bytes 7077892
  11.6 1.4 %collective-permute-start.2 = (f32[128,256]{1,0:T(8,128)S(1)}, f32[128,256]{1,0:T(8,128)S(1)}, u32[]{:S(2)}, u32[]{:S(2)}) collective-permute-start(f32[128,256]{1,0:T(8,128)S(1)} %get-tuple-element.27), channel_id=1, source_target_pairs={{0,4},{4,0},{8,12},{12,8},{16,20},{20,16},{24,28},{28,24},{32,36},... | collective-permute-start | bytes 393224 | tf_op jit(solution)/shard_map/ppermute | solution.py:208
  13.4 11.6 %collective-permute-start.3 = (f32[128,256]{1,0:T(8,128)S(1)}, f32[128,256]{1,0:T(8,128)S(1)}, u32[]{:S(2)}, u32[]{:S(2)}) collective-permute-start(f32[128,256]{1,0:T(8,128)S(1)} %lift_leaves.1._.refs_2_.refs_0_), channel_id=1, source_target_pairs={{0,16},{4,20},{8,24},{12,28},{16,0},{20,4},{24,8},{28,12},{32,48},... | collective-permute-start | bytes 393224 | tf_op jit(solution)/shard_map/ppermute | solution.py:208
  15.1 10.1 %collective-permute-start.4 = (f32[128,256]{1,0:T(8,128)S(1)}, f32[128,256]{1,0:T(8,128)S(1)}, u32[]{:S(2)}, u32[]{:S(2)}) collective-permute-start(f32[128,256]{1,0:T(8,128)S(1)} %lift_leaves.1._.refs_2_.refs_0_), channel_id=1, source_target_pairs={{0,56},{4,60},{8,48},{12,52},{16,40},{20,44},{24,32},{28,36},{32,2... | collective-permute-start | bytes 393224 | tf_op jit(solution)/shard_map/ppermute | solution.py:208
  18.7 11.1 %collective-permute-start.5 = (f32[128,256]{1,0:T(8,128)S(1)}, f32[128,256]{1,0:T(8,128)S(1)}, u32[]{:S(2)}, u32[]{:S(2)}) collective-permute-start(f32[128,256]{1,0:T(8,128)S(1)} %lift_leaves.1._.refs_2_.refs_0_), channel_id=1, source_target_pairs={{0,40},{4,44},{8,32},{12,36},{16,56},{20,60},{24,48},{28,52},{32,8... | collective-permute-start | bytes 393224 | tf_op jit(solution)/shard_map/ppermute | solution.py:208
  21.3 14.9 %collective-permute-start.9 = (f32[128,256]{1,0:T(8,128)S(1)}, f32[128,256]{1,0:T(8,128)S(1)}, u32[]{:S(2)}, u32[]{:S(2)}) collective-permute-start(f32[128,256]{1,0:T(8,128)S(1)} %get-tuple-element.32.refs_7_), channel_id=1, source_target_pairs={{0,8},{4,12},{8,0},{12,4},{16,24},{20,28},{24,16},{28,20},{32,40},... | collective-permute-start | bytes 393224 | tf_op jit(solution)/shard_map/ppermute | solution.py:208
  30.3 8.3 %collective-permute-start.6 = (f32[128,256]{1,0:T(8,128)S(1)}, f32[128,256]{1,0:T(8,128)S(1)}, u32[]{:S(2)}, u32[]{:S(2)}) collective-permute-start(f32[128,256]{1,0:T(8,128)S(1)} %lift_nodes.1), channel_id=1, source_target_pairs={{0,128},{4,132},{8,136},{12,140},{16,144},{20,148},{24,152},{28,15... | collective-permute-start | bytes 393224 | tf_op jit(solution)/shard_map/ppermute | solution.py:208
  33.2 5.6 %collective-permute-start.7 = (f32[128,256]{1,0:T(8,128)S(1)}, f32[128,256]{1,0:T(8,128)S(1)}, u32[]{:S(2)}, u32[]{:S(2)}) collective-permute-start(f32[128,256]{1,0:T(8,128)S(1)} %lift_nodes.1), channel_id=1, source_target_pairs={{0,192},{4,196},{8,200},{12,204},{16,208},{20,212},{24,216},{28,22... | collective-permute-start | bytes 393224 | tf_op jit(solution)/shard_map/ppermute | solution.py:208
  34.0 5.5 %collective-permute-start.8 = (f32[128,256]{1,0:T(8,128)S(1)}, f32[128,256]{1,0:T(8,128)S(1)}, u32[]{:S(2)}, u32[]{:S(2)}) collective-permute-start(f32[128,256]{1,0:T(8,128)S(1)} %lift_nodes.1), channel_id=1, source_target_pairs={{0,64},{4,68},{8,72},{12,76},{16,80},{20,84},{24,88},{28,92},{32,9... | collective-permute-start | bytes 393224 | tf_op jit(solution)/shard_map/ppermute | solution.py:208
  34.0 11.6 %collective-permute-start.11 = (f32[128,256]{1,0:T(8,128)S(1)}, f32[128,256]{1,0:T(8,128)S(1)}, u32[]{:S(2)}, u32[]{:S(2)}) collective-permute-start(f32[128,256]{1,0:T(8,128)S(1)} %get-tuple-element.31.refs_6_), channel_id=1, source_target_pairs={{0,4},{4,0},{8,12},{12,8},{16,20},{20,16},{24,28},{28,24},{32,36},... | collective-permute-start | bytes 393224 | tf_op jit(solution)/shard_map/ppermute | solution.py:208
  36.2 11.6 %collective-permute-start.13 = (f32[128,256]{1,0:T(8,128)S(1)}, f32[128,256]{1,0:T(8,128)S(1)}, u32[]{:S(2)}, u32[]{:S(2)}) collective-permute-start(f32[128,256]{1,0:T(8,128)S(1)} %get-tuple-element.33.refs_8_), channel_id=1, source_target_pairs={{0,12},{4,8},{8,4},{12,0},{16,28},{20,24},{24,20},{28,16},{32,44},... | collective-permute-start | bytes 393224 | tf_op jit(solution)/shard_map/ppermute | solution.py:208
  40.1 7.4 %collective-permute-start.10 = (f32[128,256]{1,0:T(8,128)S(1)}, f32[128,256]{1,0:T(8,128)S(1)}, u32[]{:S(2)}, u32[]{:S(2)}) collective-permute-start(f32[128,256]{1,0:T(8,128)S(1)} %descend.1.refs_2_.g0), channel_id=1, source_target_pairs={{0,8},{4,12},{8,0},{12,4},{16,24},{20,28},{24,16},{28,20},{32,40},... | collective-permute-start | bytes 393224 | tf_op jit(solution)/shard_map/ppermute | solution.py:208
  42.8 2.8 %collective-permute-start.12 = (f32[128,256]{1,0:T(8,128)S(1)}, f32[128,256]{1,0:T(8,128)S(1)}, u32[]{:S(2)}, u32[]{:S(2)}) collective-permute-start(f32[128,256]{1,0:T(8,128)S(1)} %descend.1.refs_2_.g0), channel_id=1, source_target_pairs={{0,4},{4,0},{8,12},{12,8},{16,20},{20,16},{24,28},{28,24},{32,36},... | collective-permute-start | bytes 393224 | tf_op jit(solution)/shard_map/ppermute | solution.py:208
  44.5 1.2 %copy-start.2 = (f32[1,1024,256]{2,1,0:T(8,128)S(1)}, f32[1,1024,256]{2,1,0:T(8,128)}, u32[]{:S(2)}) copy-start(f32[1,1024,256]{2,1,0:T(8,128)} %param.8) | copy-start | bytes 3145732
  47.5 1.4 %collective-permute-start.14 = (f32[128,256]{1,0:T(8,128)S(1)}, f32[128,256]{1,0:T(8,128)S(1)}, u32[]{:S(2)}, u32[]{:S(2)}) collective-permute-start(f32[128,256]{1,0:T(8,128)S(1)} %relay.1.g0), channel_id=1, source_target_pairs={{0,4},{4,0},{8,12},{12,8},{16,20},{20,16},{24,28},{28,24},{32,36},... | collective-permute-start | bytes 393224 | tf_op jit(solution)/shard_map/ppermute | solution.py:208

commit v10 on v9

--- a/solution.py
+++ b/solution.py
@@ -197,6 +197,40 @@
         near = (near_above, near_above, near_third, near_fourth)[i]
         part = near[pl.ds(i * chunk % near.shape[0], chunk), columns]
         block[at, :] = part + dot(row_basis[at, :], whole[...], 1, 1)
+        copy = pltpu.make_async_copy(block.at[at], out.at[at, columns], sems.at[i])
+        copy.start()
+        copies.append(copy)
+    for copy in copies:
+        copy.wait()
+
+
+def far_block(near_above, near_third, near_fourth, row_basis, leaf_turned, field, parent, out):
+    _, m, k, _ = place()
+    columns = span(mine(m, k) ^ 2, out.shape[1])
+    g = field[...] + dot(parent[...], leaf_turned[k], 1, 0)
+    first_row = 0
+    for near in (near_above, near_third, near_fourth):
+        at = pl.ds(first_row, near.shape[0])
+        out[at, :] = near[:, columns] + dot(row_basis[at, :], g, 1, 1)
+        first_row += near.shape[0]
+
+
+def finish_last(
+    near_above, near_third, near_fourth, row_basis, leaf_turned, ready, field, parent, _, *rest
+):
+    out, block, sems = rest
+    _, m, k, _ = place()
+    wide = block.shape[1]
+    copies = [pltpu.make_async_copy(ready, out.at[:, span(mine(m, k) ^ 2, wide)], sems.at[CHUNKS])]
+    copies[0].start()
+    g = field[...] + dot(parent[...], leaf_turned[k], 1, 0)
+    columns = span(mine(m, k) ^ 3, wide)
+    chunk = out.shape[0] // CHUNKS
+    for i in range(CHUNKS):
+        at = pl.ds(i * chunk, chunk)
+        near = (near_above, near_above, near_third, near_fourth)[i]
+        part = near[pl.ds(i * chunk % near.shape[0], chunk), columns]
+        block[at, :] = part + dot(row_basis[at, :], g, 1, 1)
         copy = pltpu.make_async_copy(block.at[at], out.at[at, columns], sems.at[i])
         copy.start()
         copies.append(copy)
@@ -332,7 +366,26 @@
     (far_parent,) = run(
         relay, [far_parent], [(quarter, rank)], "relay", quarter * rank, after=in_hbm([out])
     )
-    return write(2, [fields[2], far_parent, fields[3], swap(far_parent, 1)], [out])
+    (ready,) = run(
+        far_block,
+        [*nears, rbasis, turned[2], fields[2], far_parent],
+        [(users, quarter)],
+        "far_block",
+        6 * users * rank * quarter,
+    )
+    ins = in_vmem([*nears, rbasis, turned[2], ready, fields[3], swap(far_parent, 1)])
+    return pl.pallas_call(
+        finish_last,
+        out_shape=pltpu.HBM((users, columns), F32),
+        in_specs=[VMEM] * len(ins) + [ANY],
+        out_specs=ANY,
+        scratch_shapes=[
+            pltpu.VMEM((users, quarter), F32),
+            pltpu.SemaphoreType.DMA((CHUNKS + 1,)),
+        ],
+        input_output_aliases={len(ins): 0},
+        **settings(6 * users * rank * quarter, users * columns, "finish_last"),
+    )(*ins, out)
 
 
 def solution(mesh):

time: 51.1 us -> 50.9 us (level)
  waiting for transfers between devices: 8.32 us -> 7.45 us
  Pallas kernels: 17.8 us -> 18.5 us
    pallas_call x2 -> x1, Pallas kernels: 3.54 us -> 1.76 us  [write(): pl.pallas_call(functools.partial(finish, first), out_shape=pltpu.HBM((use...]
    pallas_call x0 -> x1, Pallas kernels: none -> 1.58 us  [local(): pl.pallas_call(finish_last, out_shape=pltpu.HBM((users, columns), F32), i...]
    ppermute x15, waiting for transfers between devices: 8.32 us -> 7.45 us  [swap(): lax.ppermute(block, 'leaf', [(i, i ^ bits) for i in range(lax.axis_size('...]
    pallas_call x8 -> x9, Pallas kernels: 5.34 us -> 6.21 us  [run(): pl.pallas_call(kernel, out_shape=[pltpu.VMEM(shape, F32) for shape in out...]
  transfers between devices with their start and end apart: 15 -> 15, of which waited for: 7 -> 7; matrix products, arithmetic and copies ran while one was open for 0% -> 0% of each run, Pallas kernels for 26% -> 28%
where the time goes in v10:
time: 50.9 us; the launch traced here: 50.7 us
  starting transfers between devices  24.3 us (48%)
  Pallas kernels  18.5 us (36%)
  waiting for transfers between devices  7.45 us (15%)
    ppermute x15, starting transfers between devices, swap(): lax.ppermute(block, 'leaf', [(i, i ^ bits) for i in range(lax.axis_size('...  24.3 us
    ppermute x15, waiting for transfers between devices, swap(): lax.ppermute(block, 'leaf', [(i, i ^ bits) for i in range(lax.axis_size('...  7.45 us
    pallas_call x9, Pallas kernels, run(): pl.pallas_call(kernel, out_shape=[pltpu.VMEM(shape, F32) for shape in out...  6.21 us
    pallas_call x1, Pallas kernels, local(): pl.pallas_call(own_and_near, out_shape=[pltpu.VMEM(shape, F32) for shape...  4.08 us
    pallas_call x1, Pallas kernels, local(): pl.pallas_call(far_coefficients, out_shape=[pltpu.VMEM(shape, F32) for sh...  2.49 us
    pallas_call x1, Pallas kernels, local(): pl.pallas_call(near_below, out_shape=[pltpu.VMEM(part_rows, F32), pltpu.V...  2.37 us
    pallas_call x1, Pallas kernels, write(): pl.pallas_call(functools.partial(finish, first), out_shape=pltpu.HBM((use...  1.76 us
    pallas_call x1, Pallas kernels, local(): pl.pallas_call(finish_last, out_shape=pltpu.HBM((users, columns), F32), i...  1.58 us
  transfers between devices with their start and end apart: 15, of which 7 were waited for; matrix products, arithmetic and copies ran while one was open for 0% of the time, Pallas kernels for 28%

profile of v10, /device:TPU:1, one launch (start us, length us, event | category | flops | bytes accessed | tf_op | source)
XLA Modules:
  0.0 50.7 jit_solution(3524747160479442163)
XLA Ops:
  0.0 2.5 %far_coefficients.1 = (f32[128,256]{1,0:T(8,128)S(1)}, f32[128,256]{1,0:T(8,128)S(1)}, f32[1024,512]{1,0:T(8,128)S(1)}, f32[1024,256]{1,0:T(8,128)S(1)}) custom-call(f32[1024,512]{1,0:T(8,128)} %x.1, f32[1024,256]{1,0:T(8,128)} %bitcast.8), custom_call_target="tpu_custom_call" | custom-call | flops 402653184 | bytes 2097152 | tf_op jit(solution)/shard_map/far_coefficients/pallas_call | solution.py:252
  2.5 2.5 %collective-permute-start = (f32[128,256]{1,0:T(8,128)S(1)}, f32[128,256]{1,0:T(8,128)S(1)}, u32[]{:S(2)}, u32[]{:S(2)}) collective-permute-start(f32[128,256]{1,0:T(8,128)S(1)} %get-tuple-element.25), channel_id=1, source_target_pairs={{0,8},{4,12},{8,0},{12,4},{16,24},{20,28},{24,16},{28,20},{32,40},... | collective-permute-start | bytes 393224 | tf_op jit(solution)/shard_map/ppermute | solution.py:242
  5.0 2.4 %collective-permute-start.1 = (f32[128,256]{1,0:T(8,128)S(1)}, f32[128,256]{1,0:T(8,128)S(1)}, u32[]{:S(2)}, u32[]{:S(2)}) collective-permute-start(f32[128,256]{1,0:T(8,128)S(1)} %get-tuple-element.26), channel_id=1, source_target_pairs={{0,12},{4,8},{8,4},{12,0},{16,28},{20,24},{24,20},{28,16},{32,44},... | collective-permute-start | bytes 393224 | tf_op jit(solution)/shard_map/ppermute | solution.py:242
  7.5 4.1 %own_and_near.1 = (f32[128,256]{1,0:T(8,128)S(1)}, f32[128,256]{1,0:T(8,128)S(1)}, f32[512,512]{1,0:T(8,128)S(1)}) custom-call(f32[1024,512]{1,0:T(8,128)S(1)} %get-tuple-element.21.held.x.refs_1_, f32[1024,256]{1,0:T(8,128)S(1)} %get-tuple-element.22.basis_held, f32[1024,1024]{1,0:T(8,128)} %bitcast.6), custom_call_target="tpu_custom_call" | custom-call | flops 1610612736 | bytes 4194304 | tf_op jit(solution)/shard_map/own_and_near/pallas_call | solution.py:270
  11.7 0.8 %collective-permute-done.1.refs_2_ = f32[128,256]{1,0:T(8,128)S(1)} collective-permute-done((f32[128,256]{1,0:T(8,128)S(1)}, f32[128,256]{1,0:T(8,128)S(1)}, u32[]{:S(2)}, u32[]{:S(2)}) %collective-permute-start.1) | collective-permute-done | bytes 131104 | tf_op jit(solution)/shard_map/ppermute | solution.py:242
  12.5 0.5 collective-permute-done.2.refs_3_
  13.0 0.4 lift_leaves.1._.refs_2_.refs_0_
  13.4 1.7 %collective-permute-start.3 = (f32[128,256]{1,0:T(8,128)S(1)}, f32[128,256]{1,0:T(8,128)S(1)}, u32[]{:S(2)}, u32[]{:S(2)}) collective-permute-start(f32[128,256]{1,0:T(8,128)S(1)} %lift_leaves.1._.refs_2_.refs_0_), channel_id=1, source_target_pairs={{0,16},{4,20},{8,24},{12,28},{16,0},{20,4},{24,8},{28,12},{32,48},... | collective-permute-start | bytes 393224 | tf_op jit(solution)/shard_map/ppermute | solution.py:242
  15.1 3.6 %collective-permute-start.4 = (f32[128,256]{1,0:T(8,128)S(1)}, f32[128,256]{1,0:T(8,128)S(1)}, u32[]{:S(2)}, u32[]{:S(2)}) collective-permute-start(f32[128,256]{1,0:T(8,128)S(1)} %lift_leaves.1._.refs_2_.refs_0_), channel_id=1, source_target_pairs={{0,56},{4,60},{8,48},{12,52},{16,40},{20,44},{24,32},{28,36},{32,2... | collective-permute-start | bytes 393224 | tf_op jit(solution)/shard_map/ppermute | solution.py:242
  18.7 0.9 %collective-permute-start.5 = (f32[128,256]{1,0:T(8,128)S(1)}, f32[128,256]{1,0:T(8,128)S(1)}, u32[]{:S(2)}, u32[]{:S(2)}) collective-permute-start(f32[128,256]{1,0:T(8,128)S(1)} %lift_leaves.1._.refs_2_.refs_0_), channel_id=1, source_target_pairs={{0,40},{4,44},{8,32},{12,36},{16,56},{20,60},{24,48},{28,52},{32,8... | collective-permute-start | bytes 393224 | tf_op jit(solution)/shard_map/ppermute | solution.py:242
  19.6 1.7 %couple_leaves.1 = (f32[128,256]{1,0:T(8,128)S(1)}, f32[128,256]{1,0:T(8,128)S(1)}, f32[128,256]{1,0:T(8,128)S(1)}, f32[128,256]{1,0:T(8,128)S(1)}) custom-call(f32[128,256]{1,0:T(8,128)S(1)} %get-tuple-element.24.refs_0_, f32[128,256]{1,0:T(8,128)S(1)} %collective-permute-done.refs_1_, f32[128,256]{1,0:T(8,128)S(1)} %collective-permute-done.1.refs_2_, ...), custom_call_target="tpu_custom_call" | custom-call | flops 603979776 | bytes 2883584 | tf_op jit(solution)/shard_map/couple_leaves/pallas_call | solution.py:45
  21.3 0.8 %collective-permute-start.9 = (f32[128,256]{1,0:T(8,128)S(1)}, f32[128,256]{1,0:T(8,128)S(1)}, u32[]{:S(2)}, u32[]{:S(2)}) collective-permute-start(f32[128,256]{1,0:T(8,128)S(1)} %get-tuple-element.32.refs_7_), channel_id=1, source_target_pairs={{0,8},{4,12},{8,0},{12,4},{16,24},{20,28},{24,16},{28,20},{32,40},... | collective-permute-start | bytes 393224 | tf_op jit(solution)/shard_map/ppermute | solution.py:242
  22.1 2.4 %near_below.1 = (f32[256,512]{1,0:T(8,128)S(1)}, f32[256,1024]{1,0:T(8,128)S(1)}) custom-call(f32[1024,1024]{1,0:T(8,128)} %bitcast.7, f32[1024,512]{1,0:T(8,128)S(1)} %get-tuple-element.21.held.x.refs_1_, f32[128,256]{1,0:T(8,128)S(1)} %lift_leaves.1._.refs_2_.refs_0_), custom_call_target="tpu_custom_call" | custom-call | flops 536870912 | bytes 4194304 | tf_op jit(solution)/shard_map/near_below/pallas_call | solution.py:290
  24.5 0.6 %turn.1 = (f32[3,256,256]{2,1,0:T(8,128)S(1)}, f32[256,256]{1,0:T(8,128)S(1)}, f32[4,256,256]{2,1,0:T(8,128)S(1)}) custom-call(f32[3,3,256,256]{3,2,1,0:T(8,128)S(1)} %copy-done, f32[2,4,256,256]{3,2,1,0:T(8,128)S(1)} %copy-done.1, f32[128,256]{1,0:T(8,128)S(1)} %lift_leaves.1._.refs_2_.refs_0_), custom_call_target="tpu_custom_call" | custom-call | flops 805306368 | bytes 4456448 | tf_op jit(solution)/shard_map/turn/pallas_call | solution.py:45
  25.2 4.6 %collective-permute-done.5.refs_3_ = f32[128,256]{1,0:T(8,128)S(1)} collective-permute-done((f32[128,256]{1,0:T(8,128)S(1)}, f32[128,256]{1,0:T(8,128)S(1)}, u32[]{:S(2)}, u32[]{:S(2)}) %collective-permute-start.5) | collective-permute-done | bytes 131104 | tf_op jit(solution)/shard_map/ppermute | solution.py:242
  29.8 0.4 lift_nodes.1
  30.3 3.0 %collective-permute-start.6 = (f32[128,256]{1,0:T(8,128)S(1)}, f32[128,256]{1,0:T(8,128)S(1)}, u32[]{:S(2)}, u32[]{:S(2)}) collective-permute-start(f32[128,256]{1,0:T(8,128)S(1)} %lift_nodes.1), channel_id=1, source_target_pairs={{0,128},{4,132},{8,136},{12,140},{16,144},{20,148},{24,152},{28,15... | collective-permute-start | bytes 393224 | tf_op jit(solution)/shard_map/ppermute | solution.py:242
  33.2 0.8 %collective-permute-start.7 = (f32[128,256]{1,0:T(8,128)S(1)}, f32[128,256]{1,0:T(8,128)S(1)}, u32[]{:S(2)}, u32[]{:S(2)}) collective-permute-start(f32[128,256]{1,0:T(8,128)S(1)} %lift_nodes.1), channel_id=1, source_target_pairs={{0,192},{4,196},{8,200},{12,204},{16,208},{20,212},{24,216},{28,22... | collective-permute-start | bytes 393224 | tf_op jit(solution)/shard_map/ppermute | solution.py:242
  34.0 1.6 %collective-permute-start.11 = (f32[128,256]{1,0:T(8,128)S(1)}, f32[128,256]{1,0:T(8,128)S(1)}, u32[]{:S(2)}, u32[]{:S(2)}) collective-permute-start(f32[128,256]{1,0:T(8,128)S(1)} %get-tuple-element.31.refs_6_), channel_id=1, source_target_pairs={{0,4},{4,0},{8,12},{12,8},{16,20},{20,16},{24,28},{28,24},{32,36},... | collective-permute-start | bytes 393224 | tf_op jit(solution)/shard_map/ppermute | solution.py:242
  35.6 0.6 %couple_nodes.1.refs_5_ = f32[128,256]{1,0:T(8,128)S(1)} custom-call(f32[128,256]{1,0:T(8,128)S(1)} %lift_leaves.1._.refs_2_.refs_0_, f32[128,256]{1,0:T(8,128)S(1)} %collective-permute-done.3.refs_1_, f32[128,256]{1,0:T(8,128)S(1)} %collective-permute-done.4.refs_2_, f32[128,256]{1,0:T(8,128)S(1)} %collective-permute-done.5.refs_3_, ...), custom_call_target="tpu_custom_call" | custom-call | flops 150994944 | bytes 2883584 | tf_op jit(solution)/shard_map/couple_nodes/pallas_call | solution.py:45
  36.2 2.3 %collective-permute-start.13 = (f32[128,256]{1,0:T(8,128)S(1)}, f32[128,256]{1,0:T(8,128)S(1)}, u32[]{:S(2)}, u32[]{:S(2)}) collective-permute-start(f32[128,256]{1,0:T(8,128)S(1)} %get-tuple-element.33.refs_8_), channel_id=1, source_target_pairs={{0,12},{4,8},{8,4},{12,0},{16,28},{20,24},{24,20},{28,16},{32,44},... | collective-permute-start | bytes 393224 | tf_op jit(solution)/shard_map/ppermute | solution.py:242
  38.5 0.3 collective-permute-done.7.refs_1_
  38.9 0.7 %collective-permute-done.8.refs_2_ = f32[128,256]{1,0:T(8,128)S(1)} collective-permute-done((f32[128,256]{1,0:T(8,128)S(1)}, f32[128,256]{1,0:T(8,128)S(1)}, u32[]{:S(2)}, u32[]{:S(2)}) %collective-permute-start.8) | collective-permute-done | bytes 131104 | tf_op jit(solution)/shard_map/ppermute | solution.py:242
  39.5 0.6 %descend.1.refs_2_.g0 = f32[128,256]{1,0:T(8,128)S(1)} custom-call(f32[128,256]{1,0:T(8,128)S(1)} %collective-permute-done.6.refs_0_, f32[128,256]{1,0:T(8,128)S(1)} %collective-permute-done.7.refs_1_, f32[128,256]{1,0:T(8,128)S(1)} %collective-permute-done.8.refs_2_, f32[3,256,256]{2,1,0:T(8,128)S(1)} %get-tuple-element.35.refs_3_, ...), custom_call_target="tpu_custom_call" | custom-call | flops 201326592 | bytes 1572864 | tf_op jit(solution)/shard_map/descend/pallas_call | solution.py:45
  40.1 2.7 %collective-permute-start.10 = (f32[128,256]{1,0:T(8,128)S(1)}, f32[128,256]{1,0:T(8,128)S(1)}, u32[]{:S(2)}, u32[]{:S(2)}) collective-permute-start(f32[128,256]{1,0:T(8,128)S(1)} %descend.1.refs_2_.g0), channel_id=1, source_target_pairs={{0,8},{4,12},{8,0},{12,4},{16,24},{20,28},{24,16},{28,20},{32,40},... | collective-permute-start | bytes 393224 | tf_op jit(solution)/shard_map/ppermute | solution.py:242
  42.8 1.7 %collective-permute-start.12 = (f32[128,256]{1,0:T(8,128)S(1)}, f32[128,256]{1,0:T(8,128)S(1)}, u32[]{:S(2)}, u32[]{:S(2)}) collective-permute-start(f32[128,256]{1,0:T(8,128)S(1)} %descend.1.refs_2_.g0), channel_id=1, source_target_pairs={{0,4},{4,0},{8,12},{12,8},{16,20},{20,16},{24,28},{28,24},{32,36},... | collective-permute-start | bytes 393224 | tf_op jit(solution)/shard_map/ppermute | solution.py:242
  44.5 1.1 %near_last.1.near_fourth.refs_2_ = f32[256,512]{1,0:T(8,128)S(1)} custom-call(f32[256,1024]{1,0:T(8,128)S(1)} %get-tuple-element.29.refs_0_, f32[1024,512]{1,0:T(8,128)S(1)} %get-tuple-element.21.held.x.refs_1_, f32[128,256]{1,0:T(8,128)S(1)} %descend.1.refs_2_.g0), custom_call_target="tpu_custom_call" | custom-call | flops 1610612736 | bytes 3145728 | tf_op jit(solution)/shard_map/near_last/pallas_call | solution.py:45
  45.7 1.8 %finish_0.1.refs_1_._ = f32[1024,512]{1,0:T(8,128)} custom-call(f32[512,512]{1,0:T(8,128)S(1)} %get-tuple-element.23.near_above.refs_0_, f32[256,512]{1,0:T(8,128)S(1)} %get-tuple-element.28.refs_9_.near_third.refs_1_, f32[256,512]{1,0:T(8,128)S(1)} %near_last.1.near_fourth.refs_2_, f32[1024,256]{1,0:T(8,128)S(1)} %bitcast.3, ...), custom_call_target="tpu_custom_call" | custom-call | flops 402653184 | bytes 2097152 | tf_op jit(solution)/shard_map/finish_0/pallas_call | solution.py:351
  47.5 0.2 collective-permute-start.14
  47.8 0.9 %far_block.1.ready = f32[1024,128]{1,0:T(8,128)S(1)} custom-call(f32[512,512]{1,0:T(8,128)S(1)} %get-tuple-element.23.near_above.refs_0_, f32[256,512]{1,0:T(8,128)S(1)} %get-tuple-element.28.refs_9_.near_third.refs_1_, f32[256,512]{1,0:T(8,128)S(1)} %near_last.1.near_fourth.refs_2_, f32[1024,256]{1,0:T(8,128)S(1)} %bitcast.4, ...), custom_call_target="tpu_custom_call" | custom-call | flops 201326592 | bytes 4456448 | tf_op jit(solution)/shard_map/far_block/pallas_call | solution.py:45
  48.6 0.3 collective-permute-done.14.parent
  49.0 1.6 %finish_last.1 = f32[1024,512]{1,0:T(8,128)} custom-call(f32[512,512]{1,0:T(8,128)S(1)} %get-tuple-element.23.near_above.refs_0_, f32[256,512]{1,0:T(8,128)S(1)} %get-tuple-element.28.refs_9_.near_third.refs_1_, f32[256,512]{1,0:T(8,128)S(1)} %near_last.1.near_fourth.refs_2_, f32[1024,256]{1,0:T(8,128)S(1)} %bitcast.5, ...), custom_call_target="tpu_custom_call", output_to_operand_aliasing={{}: (8, {})} | custom-call | flops 201326592 | bytes 2097152 | tf_op jit(solution)/shard_map/finish_last/pallas_call | solution.py:377
  (18 shorter events, 0.4 us)
Async XLA Ops:
  2.5 9.2 %collective-permute-start = (f32[128,256]{1,0:T(8,128)S(1)}, f32[128,256]{1,0:T(8,128)S(1)}, u32[]{:S(2)}, u32[]{:S(2)}) collective-permute-start(f32[128,256]{1,0:T(8,128)S(1)} %get-tuple-element.25), channel_id=1, source_target_pairs={{0,8},{4,12},{8,0},{12,4},{16,24},{20,28},{24,16},{28,20},{32,40},... | collective-permute-start | bytes 393224 | tf_op jit(solution)/shard_map/ppermute | solution.py:242
  5.0 7.5 %collective-permute-start.1 = (f32[128,256]{1,0:T(8,128)S(1)}, f32[128,256]{1,0:T(8,128)S(1)}, u32[]{:S(2)}, u32[]{:S(2)}) collective-permute-start(f32[128,256]{1,0:T(8,128)S(1)} %get-tuple-element.26), channel_id=1, source_target_pairs={{0,12},{4,8},{8,4},{12,0},{16,28},{20,24},{24,20},{28,16},{32,44},... | collective-permute-start | bytes 393224 | tf_op jit(solution)/shard_map/ppermute | solution.py:242
  7.5 5.5 %copy-start.1 = (f32[2,4,256,256]{3,2,1,0:T(8,128)S(1)}, f32[2,4,256,256]{3,2,1,0:T(8,128)}, u32[]{:S(2)}) copy-start(f32[2,4,256,256]{3,2,1,0:T(8,128)} %refs_4_.6) | copy-start | bytes 6291460
  11.5 8.1 %copy-start = (f32[3,3,256,256]{3,2,1,0:T(8,128)S(1)}, f32[3,3,256,256]{3,2,1,0:T(8,128)}, u32[]{:S(2)}) copy-start(f32[3,3,256,256]{3,2,1,0:T(8,128)} %refs_4_.7) | copy-start | bytes 7077892
  11.6 1.4 %collective-permute-start.2 = (f32[128,256]{1,0:T(8,128)S(1)}, f32[128,256]{1,0:T(8,128)S(1)}, u32[]{:S(2)}, u32[]{:S(2)}) collective-permute-start(f32[128,256]{1,0:T(8,128)S(1)} %get-tuple-element.27), channel_id=1, source_target_pairs={{0,4},{4,0},{8,12},{12,8},{16,20},{20,16},{24,28},{28,24},{32,36},... | collective-permute-start | bytes 393224 | tf_op jit(solution)/shard_map/ppermute | solution.py:242
  13.4 11.6 %collective-permute-start.3 = (f32[128,256]{1,0:T(8,128)S(1)}, f32[128,256]{1,0:T(8,128)S(1)}, u32[]{:S(2)}, u32[]{:S(2)}) collective-permute-start(f32[128,256]{1,0:T(8,128)S(1)} %lift_leaves.1._.refs_2_.refs_0_), channel_id=1, source_target_pairs={{0,16},{4,20},{8,24},{12,28},{16,0},{20,4},{24,8},{28,12},{32,48},... | collective-permute-start | bytes 393224 | tf_op jit(solution)/shard_map/ppermute | solution.py:242
  15.1 10.1 %collective-permute-start.4 = (f32[128,256]{1,0:T(8,128)S(1)}, f32[128,256]{1,0:T(8,128)S(1)}, u32[]{:S(2)}, u32[]{:S(2)}) collective-permute-start(f32[128,256]{1,0:T(8,128)S(1)} %lift_leaves.1._.refs_2_.refs_0_), channel_id=1, source_target_pairs={{0,56},{4,60},{8,48},{12,52},{16,40},{20,44},{24,32},{28,36},{32,2... | collective-permute-start | bytes 393224 | tf_op jit(solution)/shard_map/ppermute | solution.py:242
  18.7 11.1 %collective-permute-start.5 = (f32[128,256]{1,0:T(8,128)S(1)}, f32[128,256]{1,0:T(8,128)S(1)}, u32[]{:S(2)}, u32[]{:S(2)}) collective-permute-start(f32[128,256]{1,0:T(8,128)S(1)} %lift_leaves.1._.refs_2_.refs_0_), channel_id=1, source_target_pairs={{0,40},{4,44},{8,32},{12,36},{16,56},{20,60},{24,48},{28,52},{32,8... | collective-permute-start | bytes 393224 | tf_op jit(solution)/shard_map/ppermute | solution.py:242
  21.3 14.9 %collective-permute-start.9 = (f32[128,256]{1,0:T(8,128)S(1)}, f32[128,256]{1,0:T(8,128)S(1)}, u32[]{:S(2)}, u32[]{:S(2)}) collective-permute-start(f32[128,256]{1,0:T(8,128)S(1)} %get-tuple-element.32.refs_7_), channel_id=1, source_target_pairs={{0,8},{4,12},{8,0},{12,4},{16,24},{20,28},{24,16},{28,20},{32,40},... | collective-permute-start | bytes 393224 | tf_op jit(solution)/shard_map/ppermute | solution.py:242
  30.3 8.3 %collective-permute-start.6 = (f32[128,256]{1,0:T(8,128)S(1)}, f32[128,256]{1,0:T(8,128)S(1)}, u32[]{:S(2)}, u32[]{:S(2)}) collective-permute-start(f32[128,256]{1,0:T(8,128)S(1)} %lift_nodes.1), channel_id=1, source_target_pairs={{0,128},{4,132},{8,136},{12,140},{16,144},{20,148},{24,152},{28,15... | collective-permute-start | bytes 393224 | tf_op jit(solution)/shard_map/ppermute | solution.py:242
  33.2 5.6 %collective-permute-start.7 = (f32[128,256]{1,0:T(8,128)S(1)}, f32[128,256]{1,0:T(8,128)S(1)}, u32[]{:S(2)}, u32[]{:S(2)}) collective-permute-start(f32[128,256]{1,0:T(8,128)S(1)} %lift_nodes.1), channel_id=1, source_target_pairs={{0,192},{4,196},{8,200},{12,204},{16,208},{20,212},{24,216},{28,22... | collective-permute-start | bytes 393224 | tf_op jit(solution)/shard_map/ppermute | solution.py:242
  34.0 5.5 %collective-permute-start.8 = (f32[128,256]{1,0:T(8,128)S(1)}, f32[128,256]{1,0:T(8,128)S(1)}, u32[]{:S(2)}, u32[]{:S(2)}) collective-permute-start(f32[128,256]{1,0:T(8,128)S(1)} %lift_nodes.1), channel_id=1, source_target_pairs={{0,64},{4,68},{8,72},{12,76},{16,80},{20,84},{24,88},{28,92},{32,9... | collective-permute-start | bytes 393224 | tf_op jit(solution)/shard_map/ppermute | solution.py:242
  34.0 11.6 %collective-permute-start.11 = (f32[128,256]{1,0:T(8,128)S(1)}, f32[128,256]{1,0:T(8,128)S(1)}, u32[]{:S(2)}, u32[]{:S(2)}) collective-permute-start(f32[128,256]{1,0:T(8,128)S(1)} %get-tuple-element.31.refs_6_), channel_id=1, source_target_pairs={{0,4},{4,0},{8,12},{12,8},{16,20},{20,16},{24,28},{28,24},{32,36},... | collective-permute-start | bytes 393224 | tf_op jit(solution)/shard_map/ppermute | solution.py:242
  36.2 12.4 %collective-permute-start.13 = (f32[128,256]{1,0:T(8,128)S(1)}, f32[128,256]{1,0:T(8,128)S(1)}, u32[]{:S(2)}, u32[]{:S(2)}) collective-permute-start(f32[128,256]{1,0:T(8,128)S(1)} %get-tuple-element.33.refs_8_), channel_id=1, source_target_pairs={{0,12},{4,8},{8,4},{12,0},{16,28},{20,24},{24,20},{28,16},{32,44},... | collective-permute-start | bytes 393224 | tf_op jit(solution)/shard_map/ppermute | solution.py:242
  40.1 7.4 %collective-permute-start.10 = (f32[128,256]{1,0:T(8,128)S(1)}, f32[128,256]{1,0:T(8,128)S(1)}, u32[]{:S(2)}, u32[]{:S(2)}) collective-permute-start(f32[128,256]{1,0:T(8,128)S(1)} %descend.1.refs_2_.g0), channel_id=1, source_target_pairs={{0,8},{4,12},{8,0},{12,4},{16,24},{20,28},{24,16},{28,20},{32,40},... | collective-permute-start | bytes 393224 | tf_op jit(solution)/shard_map/ppermute | solution.py:242
  42.8 2.8 %collective-permute-start.12 = (f32[128,256]{1,0:T(8,128)S(1)}, f32[128,256]{1,0:T(8,128)S(1)}, u32[]{:S(2)}, u32[]{:S(2)}) collective-permute-start(f32[128,256]{1,0:T(8,128)S(1)} %descend.1.refs_2_.g0), channel_id=1, source_target_pairs={{0,4},{4,0},{8,12},{12,8},{16,20},{20,16},{24,28},{28,24},{32,36},... | collective-permute-start | bytes 393224 | tf_op jit(solution)/shard_map/ppermute | solution.py:242
  44.5 1.2 %copy-start.2 = (f32[1,1024,256]{2,1,0:T(8,128)S(1)}, f32[1,1024,256]{2,1,0:T(8,128)}, u32[]{:S(2)}) copy-start(f32[1,1024,256]{2,1,0:T(8,128)} %param.8) | copy-start | bytes 3145732
  47.5 1.4 %collective-permute-start.14 = (f32[128,256]{1,0:T(8,128)S(1)}, f32[128,256]{1,0:T(8,128)S(1)}, u32[]{:S(2)}, u32[]{:S(2)}) collective-permute-start(f32[128,256]{1,0:T(8,128)S(1)} %relay.1.refs_6_), channel_id=1, source_target_pairs={{0,4},{4,0},{8,12},{12,8},{16,20},{20,16},{24,28},{28,24},{32,36},... | collective-permute-start | bytes 393224 | tf_op jit(solution)/shard_map/ppermute | solution.py:242
